TPU v7x, 32 devices: a whole 2x2x4 slice. The times are simulated.
32 devices in a mesh: seq: 2 (over y), sp: 16 (over z, x, core).
Axes of the slice: x: 2, y: 2, z: 4, core: 2. Of those that a mesh axis runs over, the one named last changes fastest.
Arguments:
- video: bfloat16 [4, 16, 128, 1152], P('seq', None, 'sp'), may hold values from -6 to 6
- segment_ids: int32 [4, 16], P('seq'), may hold values from 0 to 1, never falling along the last dimension, each value on 1 to 12 neighbouring positions
- timesteps: int32 [4, 2], P('seq'), may hold values from 0 to 999
- drop_mask: int32 [4, 2], P('seq'), may hold values 0 or 1
- captions: bfloat16 [4, 2, 120, 4096], P('seq', None, None, 'sp'), may hold values from -6 to 6
- null_caption: bfloat16 [120, 4096], P(None, 'sp'), may hold values from -6 to 6
- caption_weight: bfloat16 [4096, 1152], P('sp'), may hold values from -0.09375 to 0.09375
- spatial_qkv: bfloat16 [1152, 3456], P('sp'), may hold values from -0.1875 to 0.1875
- spatial_out: bfloat16 [1152, 1152], P('sp'), may hold values from -0.5 to 0.5
- spatial_expand: bfloat16 [1152, 4608], P('sp'), may hold values from -0.1875 to 0.1875
- spatial_shrink: bfloat16 [4608, 1152], P('sp'), may hold values from -0.09375 to 0.09375
- spatial_vectors: bfloat16 [14, 1152], P(None, 'sp'), may hold values from -2.5 to 2.5
- temporal_qkv: bfloat16 [1152, 3456], P('sp'), may hold values from -0.1875 to 0.1875
- temporal_out: bfloat16 [1152, 1152], P('sp'), may hold values from -0.25 to 0.25
- temporal_expand: bfloat16 [1152, 4608], P('sp'), may hold values from -0.1875 to 0.1875
- temporal_shrink: bfloat16 [4608, 1152], P('sp'), may hold values from -0.09375 to 0.09375
- cross_query: bfloat16 [1152, 1152], P('sp'), may hold values from -0.1875 to 0.1875
- cross_keyval: bfloat16 [1152, 2304], P('sp'), may hold values from -0.1875 to 0.1875
- cross_out: bfloat16 [1152, 1152], P('sp'), may hold values from -0.375 to 0.375
- temporal_vectors: bfloat16 [18, 1152], P(None, 'sp'), may hold values from -2.5 to 2.5
- cotangent: bfloat16 [4, 16, 128, 1152], P('seq', None, 'sp'), may hold values from -6 to 6
Outputs:
- layer_output: bfloat16 [4, 16, 128, 1152], P('seq', None, 'sp')
- video_grad: bfloat16 [4, 16, 128, 1152], P('seq', None, 'sp')
- null_caption_grad: float32 [120, 4096], P(None, 'sp')
- caption_weight_grad: float32 [4096, 1152], P('sp')
- spatial_qkv_grad: float32 [1152, 3456], P('sp')
- spatial_out_grad: float32 [1152, 1152], P('sp')
- spatial_expand_grad: float32 [1152, 4608], P('sp')
- spatial_shrink_grad: float32 [4608, 1152], P('sp')
- spatial_vectors_grad: float32 [14, 1152], P(None, 'sp')
- temporal_qkv_grad: float32 [1152, 3456], P('sp')
- temporal_out_grad: float32 [1152, 1152], P('sp')
- temporal_expand_grad: float32 [1152, 4608], P('sp')
- temporal_shrink_grad: float32 [4608, 1152], P('sp')
- cross_query_grad: float32 [1152, 1152], P('sp')
- cross_keyval_grad: float32 [1152, 2304], P('sp')
- cross_out_grad: float32 [1152, 1152], P('sp')
- temporal_vectors_grad: float32 [18, 1152], P(None, 'sp')
Inputs may be any that keep to these rules, and one draw needn't show every extreme that they name: `segment_ids`: within a sequence clip numbers never fall along the frames; each of the 2 clips has 1 to 12 frames.
All inputs are finite; a program needn't handle non-finite values. No bound on the sum of `drop_mask` on one device may be relied on, other than what follows from the above.
Results may differ from a plain program's by a relative error of at most 0.03.
Values may be sent and summed in bfloat16 or wider, within the bound.
A program may use at most 384 MiB of HBM per device.

v0:
```python
import math

import jax
import jax.numpy as jnp
from jax import lax
from jax.sharding import PartitionSpec as P

D = 1152
HEADS = 16
HEAD_DIM = 72
FF = 4608
CAP = 120
CLIPS = 2


norm_eps = 1e-06
masked_score = -1e30


def time_features(timestep):
    half_width = 3 * D
    frequency = jnp.exp(
        jnp.arange(half_width, dtype=jnp.float32) * (-math.log(10000.0) / half_width)
    )
    angles = timestep.astype(jnp.float32)[..., None] * frequency
    return 0.5 * jnp.concatenate([jnp.cos(angles), jnp.sin(angles)], axis=-1)


def layer_norm(residual):
    center = residual - jnp.mean(residual, axis=-1, keepdims=True)
    return center * lax.rsqrt(jnp.mean(center * center, axis=-1, keepdims=True) + norm_eps)


def modulate(residual, offset, scaling):
    return layer_norm(residual) * (1.0 + scaling) + offset


def gelu_tanh(inner_sum):
    return jax.nn.gelu(inner_sum, approximate=True)


def as_float(member):
    return member.astype(jnp.float32)


def project(inputs, weight):
    return jnp.dot(inputs, weight, preferred_element_type=jnp.float32)


def weight_grad(inputs, gradients):
    left_rows = inputs.reshape(-1, inputs.shape[-1])
    right_rows = gradients.reshape(-1, gradients.shape[-1])
    return lax.dot_general(
        left_rows, right_rows, (((0,), (0,)), ((), ())), preferred_element_type=jnp.float32
    )


def input_grad(gradients, weight):
    return lax.dot_general(
        gradients,
        weight,
        (((gradients.ndim - 1,), (1,)), ((), ())),
        preferred_element_type=jnp.float32,
    )


def column_sum(gradients):
    return jnp.sum(gradients.astype(jnp.float32).reshape(-1, gradients.shape[-1]), axis=0)


def triple_bias(query_bias, value_bias):
    head_query = query_bias.reshape(HEADS, 1, HEAD_DIM)
    head_value = value_bias.reshape(HEADS, 1, HEAD_DIM)
    return jnp.concatenate([head_query, jnp.zeros_like(head_query), head_value], axis=1).reshape(
        3 * D
    )


def pair_bias(value_bias):
    head_value = value_bias.reshape(HEADS, 1, HEAD_DIM)
    return jnp.concatenate([jnp.zeros_like(head_value), head_value], axis=1).reshape(2 * D)


def triple_bias_grad(totals):
    split_rows = totals.reshape(HEADS, 3, HEAD_DIM)
    return (split_rows[:, 0].reshape(D), split_rows[:, 2].reshape(D))


def frame_modulation(segment_ids, timesteps):
    onehot = (segment_ids[:, :, None] == jnp.arange(CLIPS)[None, None, :]).astype(jnp.float32)
    features = time_features(timesteps)
    return jnp.einsum("sfc,scz->sfz", onehot, features, precision=lax.Precision.HIGHEST)


def block_pieces(table_rows, frame_mod):
    modulation = table_rows[None, None] + frame_mod
    return [modulation[:, :, number][:, :, None, :] for number in range(6)]


def gated_back(grad_out, gating, branch):
    branch_grad = (gating * grad_out).astype(jnp.bfloat16)
    gate_grad = jnp.sum(grad_out * branch, axis=2, keepdims=True)
    return (branch_grad, gate_grad)


def to_pairs(values):
    groups, frames, patches, head_count, columns = values.shape
    reordered = jnp.transpose(values, (0, 1, 3, 2, 4))
    return reordered.reshape(lax.axis_size("sp"), -1, patches, columns)


def from_pairs(values, groups, frames):
    devices, pair_count, patches, columns = values.shape
    reordered = values.reshape(groups, frames, -1, patches, columns)
    return jnp.transpose(reordered, (0, 1, 3, 2, 4))


def pair_scores(triple):
    queries = triple[..., :HEAD_DIM]
    key_rows = triple[..., HEAD_DIM : 2 * HEAD_DIM]
    scores = jnp.einsum(
        "zkqe,zkre->zkqr", queries, key_rows, preferred_element_type=jnp.float32
    ) * HEAD_DIM ** (-0.5)
    return jax.nn.softmax(scores, axis=-1)


def attend_pairs(triple):
    attention = pair_scores(triple).astype(jnp.bfloat16)
    mixture = jnp.einsum(
        "zkqr,zkre->zkqe",
        attention,
        triple[..., 2 * HEAD_DIM :],
        preferred_element_type=jnp.float32,
    ).astype(jnp.bfloat16)
    return lax.all_to_all(mixture, "sp", split_axis=2, concat_axis=0, tiled=True)


def pair_backward(members):
    triple, out_grad = members
    queries = triple[..., :HEAD_DIM]
    key_rows = triple[..., HEAD_DIM : 2 * HEAD_DIM]
    value_rows = triple[..., 2 * HEAD_DIM :]
    attention = pair_scores(triple)
    rounded = attention.astype(jnp.bfloat16)
    prob_grad = jnp.einsum(
        "zkqe,zkre->zkqr", out_grad, value_rows, preferred_element_type=jnp.float32
    )
    centre = jnp.sum(prob_grad * attention, axis=-1, keepdims=True)
    score_grad = (attention * (prob_grad - centre)).astype(jnp.bfloat16)
    scaling = HEAD_DIM ** (-0.5)
    query_grad = (
        jnp.einsum("zkqr,zkre->zkqe", score_grad, key_rows, preferred_element_type=jnp.float32)
        * scaling
    )
    key_grad = (
        jnp.einsum("zkqr,zkqe->zkre", score_grad, queries, preferred_element_type=jnp.float32)
        * scaling
    )
    value_grad = jnp.einsum(
        "zkqr,zkqe->zkre", rounded, out_grad, preferred_element_type=jnp.float32
    )
    gradients = jnp.concatenate([query_grad, key_grad, value_grad], axis=-1).astype(jnp.bfloat16)
    return lax.all_to_all(gradients, "sp", split_axis=2, concat_axis=0, tiled=True)


def pair_attention(triple):
    groups, frames, patches = triple.shape[:3]
    shaped = triple.reshape(groups, frames, patches, HEADS, 3 * HEAD_DIM)
    exchanged = attend_pairs(
        lax.all_to_all(to_pairs(shaped), "sp", split_axis=0, concat_axis=2, tiled=True)
    )
    return from_pairs(exchanged, groups, frames).reshape(groups, frames, patches, D)


def pair_attention_back(triple, mixture_grad):
    groups, frames, patches = triple.shape[:3]
    shaped = triple.reshape(groups, frames, patches, HEADS, 3 * HEAD_DIM)
    grad_shaped = mixture_grad.reshape(groups, frames, patches, HEADS, HEAD_DIM)
    returned = pair_backward(
        (
            lax.all_to_all(to_pairs(shaped), "sp", split_axis=0, concat_axis=2, tiled=True),
            lax.all_to_all(to_pairs(grad_shaped), "sp", split_axis=0, concat_axis=2, tiled=True),
        )
    )
    return from_pairs(returned, groups, frames).reshape(groups, frames, patches, 3 * D)


def feed_forward(residual, offset, scaling, gating, expand, shrink, vectors, start_row):
    hidden = modulate(residual, offset, scaling).astype(jnp.bfloat16)
    inner_sum = project(hidden, expand) + vectors[start_row : start_row + 4].reshape(FF)
    active = gelu_tanh(inner_sum).astype(jnp.bfloat16)
    branch = project(active, shrink) + vectors[3]
    return ((hidden, inner_sum, active, branch), residual + gating * branch)


def feed_backward(grad_out, residual, offset, scaling, gating, stored, expand, shrink):
    hidden, inner_sum, active, branch = stored
    branch_grad, gate_grad = gated_back(grad_out, gating, branch)
    shrink_grad = weight_grad(active, branch_grad)
    active_grad = input_grad(branch_grad, shrink)
    gelu_value, gelu_back = jax.vjp(gelu_tanh, inner_sum)
    inner_grad = gelu_back(active_grad)[0].astype(jnp.bfloat16)
    expand_grad = weight_grad(hidden, inner_grad)
    hidden_grad = input_grad(inner_grad, expand)
    norm_value, norm_back = jax.vjp(modulate, residual, offset, scaling)
    residual_grad, offset_grad, scaling_grad = norm_back(hidden_grad)
    return (
        grad_out + residual_grad,
        [offset_grad, scaling_grad, gate_grad],
        (expand_grad, shrink_grad, column_sum(inner_grad), column_sum(branch_grad)),
    )


def table_sums(members):
    return jnp.stack([jnp.sum(member, axis=(0, 1, 2)) for member in members])


def spatial_forward(residual, weights, frame_mod):
    qkv_weight, out_weight, expand, shrink, vectors = weights
    vectors_f = as_float(vectors)
    pieces = block_pieces(vectors_f[4:10], frame_mod)
    hidden = modulate(residual, pieces[0], pieces[1]).astype(jnp.bfloat16)
    triple = (project(hidden, qkv_weight) + triple_bias(vectors_f[0], vectors_f[1])).astype(
        jnp.bfloat16
    )
    mixture = pair_attention(triple)
    branch = project(mixture, out_weight) + vectors_f[2]
    middle = residual + pieces[2] * branch
    stored_ffn, result = feed_forward(
        middle, pieces[3], pieces[4], pieces[5], expand, shrink, vectors_f, 10
    )
    return (result, (hidden, triple, mixture, branch, middle, stored_ffn))


def spatial_backward(grad_out, residual, weights, frame_mod, stored):
    qkv_weight, out_weight, expand, shrink, vectors = weights
    pieces = block_pieces(as_float(vectors)[4:10], frame_mod)
    hidden, triple, mixture, branch, middle, stored_ffn = stored
    middle_grad, ffn_table, ffn_grads = feed_backward(
        grad_out, middle, pieces[3], pieces[4], pieces[5], stored_ffn, expand, shrink
    )
    branch_grad, gate_grad = gated_back(middle_grad, pieces[2], branch)
    out_weight_grad = weight_grad(mixture, branch_grad)
    out_bias = column_sum(branch_grad)
    mixture_grad = input_grad(branch_grad, out_weight).astype(jnp.bfloat16)
    triple_grad = pair_attention_back(triple, mixture_grad)
    qkv_grad = weight_grad(hidden, triple_grad)
    query_bias, value_bias = triple_bias_grad(column_sum(triple_grad))
    hidden_grad = input_grad(triple_grad, qkv_weight)
    norm_value, norm_back = jax.vjp(modulate, residual, pieces[0], pieces[1])
    residual_grad, offset_grad, scaling_grad = norm_back(hidden_grad)
    table_grad = table_sums([offset_grad, scaling_grad, gate_grad] + ffn_table)
    vector_grad = jnp.concatenate(
        [
            jnp.stack([query_bias, value_bias, out_bias, ffn_grads[3]]),
            table_grad,
            ffn_grads[2].reshape(4, D),
        ],
        axis=0,
    )
    return (
        middle_grad + residual_grad,
        (qkv_grad, out_weight_grad, ffn_grads[0], ffn_grads[1], vector_grad),
    )


def temporal_scores(triple, same_clip):
    scores = jnp.einsum(
        "sfphe,sgphe->sphfg",
        triple[..., :HEAD_DIM],
        triple[..., HEAD_DIM : 2 * HEAD_DIM],
        preferred_element_type=jnp.float32,
    ) * HEAD_DIM ** (-0.5)
    return jax.nn.softmax(jnp.where(same_clip, scores, masked_score), axis=-1)


def caption_scores(queries, keyval, allowed):
    scores = jnp.einsum(
        "sfphe,srhe->sfphr", queries, keyval[..., :HEAD_DIM], preferred_element_type=jnp.float32
    ) * HEAD_DIM ** (-0.5)
    return jax.nn.softmax(jnp.where(allowed, scores, masked_score), axis=-1)


def temporal_forward(residual, weights, frame_mod, same_clip, allowed, context):
    qkv_weight, out_weight, expand, shrink, query_weight, keyval_weight, cross_weight, vectors = (
        weights
    )
    vectors_f = as_float(vectors)
    pieces = block_pieces(vectors_f[8:14], frame_mod)
    groups, frames, patches = residual.shape[:3]
    hidden = modulate(residual, pieces[0], pieces[1]).astype(jnp.bfloat16)
    triple = (project(hidden, qkv_weight) + triple_bias(vectors_f[0], vectors_f[1])).astype(
        jnp.bfloat16
    )
    triple = triple.reshape(groups, frames, patches, HEADS, 3 * HEAD_DIM)
    attention = temporal_scores(triple, same_clip).astype(jnp.bfloat16)
    mixture = (
        jnp.einsum(
            "sphfg,sgphe->sfphe",
            attention,
            triple[..., 2 * HEAD_DIM :],
            preferred_element_type=jnp.float32,
        )
        .astype(jnp.bfloat16)
        .reshape(groups, frames, patches, D)
    )
    branch = project(mixture, out_weight) + vectors_f[2]
    middle = residual + pieces[2] * branch
    lowered = middle.astype(jnp.bfloat16)
    queries = (project(lowered, query_weight) + vectors_f[4]).astype(jnp.bfloat16)
    queries = queries.reshape(groups, frames, patches, HEADS, HEAD_DIM)
    keyval = (project(context, keyval_weight) + pair_bias(vectors_f[5])).astype(jnp.bfloat16)
    keyval = keyval.reshape(groups, -1, HEADS, 2 * HEAD_DIM)
    cross_probs = caption_scores(queries, keyval, allowed).astype(jnp.bfloat16)
    cross_mix = (
        jnp.einsum(
            "sfphr,srhe->sfphe",
            cross_probs,
            keyval[..., HEAD_DIM:],
            preferred_element_type=jnp.float32,
        )
        .astype(jnp.bfloat16)
        .reshape(groups, frames, patches, D)
    )
    crossed = middle + project(cross_mix, cross_weight) + vectors_f[6]
    stored_ffn, result = feed_forward(
        crossed, pieces[3], pieces[4], pieces[5], expand, shrink, vectors_f, 14
    )
    return (
        result,
        (
            hidden,
            triple,
            mixture,
            branch,
            middle,
            lowered,
            queries,
            keyval,
            cross_mix,
            crossed,
            stored_ffn,
        ),
    )


def temporal_backward(grad_out, residual, weights, frame_mod, same_clip, allowed, stored):
    qkv_weight, out_weight, expand, shrink, query_weight, keyval_weight, cross_weight, vectors = (
        weights
    )
    pieces = block_pieces(as_float(vectors)[8:14], frame_mod)
    (
        hidden,
        triple,
        mixture,
        branch,
        middle,
        lowered,
        queries,
        keyval,
        cross_mix,
        crossed,
        stored_ffn,
    ) = stored
    groups, frames, patches = residual.shape[:3]
    scaling = HEAD_DIM ** (-0.5)
    crossed_grad, ffn_table, ffn_grads = feed_backward(
        grad_out, crossed, pieces[3], pieces[4], pieces[5], stored_ffn, expand, shrink
    )
    cross_branch_grad = crossed_grad.astype(jnp.bfloat16)
    cross_weight_grad = weight_grad(cross_mix, cross_branch_grad)
    cross_bias = column_sum(cross_branch_grad)
    mix_grad = input_grad(cross_branch_grad, cross_weight).astype(jnp.bfloat16)
    mix_grad = mix_grad.reshape(groups, frames, patches, HEADS, HEAD_DIM)
    cross_probs = caption_scores(queries, keyval, allowed)
    rounded = cross_probs.astype(jnp.bfloat16)
    prob_grad = jnp.einsum(
        "sfphe,srhe->sfphr", mix_grad, keyval[..., HEAD_DIM:], preferred_element_type=jnp.float32
    )
    centre = jnp.sum(prob_grad * cross_probs, axis=-1, keepdims=True)
    score_grad = (cross_probs * (prob_grad - centre)).astype(jnp.bfloat16)
    query_grad = (
        jnp.einsum(
            "sfphr,srhe->sfphe",
            score_grad,
            keyval[..., :HEAD_DIM],
            preferred_element_type=jnp.float32,
        )
        * scaling
    )
    query_grad = query_grad.astype(jnp.bfloat16).reshape(groups, frames, patches, D)
    key_grad = (
        jnp.einsum("sfphr,sfphe->srhe", score_grad, queries, preferred_element_type=jnp.float32)
        * scaling
    )
    value_grad = jnp.einsum(
        "sfphr,sfphe->srhe", rounded, mix_grad, preferred_element_type=jnp.float32
    )
    keyval_grad = jnp.concatenate([key_grad, value_grad], axis=-1).reshape(groups, -1, 2 * D)
    keyval_grad = lax.psum(keyval_grad, "sp").astype(jnp.bfloat16)
    query_weight_grad = weight_grad(lowered, query_grad)
    cross_query_bias = column_sum(query_grad)
    middle_grad = crossed_grad + input_grad(query_grad, query_weight)
    branch_grad, gate_grad = gated_back(middle_grad, pieces[2], branch)
    out_weight_grad = weight_grad(mixture, branch_grad)
    out_bias = column_sum(branch_grad)
    mixture_grad = input_grad(branch_grad, out_weight).astype(jnp.bfloat16)
    mixture_grad = mixture_grad.reshape(groups, frames, patches, HEADS, HEAD_DIM)
    attention = temporal_scores(triple, same_clip)
    rounded_t = attention.astype(jnp.bfloat16)
    prob_grad_t = jnp.einsum(
        "sfphe,sgphe->sphfg",
        mixture_grad,
        triple[..., 2 * HEAD_DIM :],
        preferred_element_type=jnp.float32,
    )
    centre_t = jnp.sum(prob_grad_t * attention, axis=-1, keepdims=True)
    score_grad_t = (attention * (prob_grad_t - centre_t)).astype(jnp.bfloat16)
    query_part = (
        jnp.einsum(
            "sphfg,sgphe->sfphe",
            score_grad_t,
            triple[..., HEAD_DIM : 2 * HEAD_DIM],
            preferred_element_type=jnp.float32,
        )
        * scaling
    )
    key_part = (
        jnp.einsum(
            "sphfg,sfphe->sgphe",
            score_grad_t,
            triple[..., :HEAD_DIM],
            preferred_element_type=jnp.float32,
        )
        * scaling
    )
    value_part = jnp.einsum(
        "sphfg,sfphe->sgphe", rounded_t, mixture_grad, preferred_element_type=jnp.float32
    )
    triple_grad = jnp.concatenate([query_part, key_part, value_part], axis=-1).astype(jnp.bfloat16)
    triple_grad = triple_grad.reshape(groups, frames, patches, 3 * D)
    qkv_grad = weight_grad(hidden, triple_grad)
    query_bias, value_bias = triple_bias_grad(column_sum(triple_grad))
    hidden_grad = input_grad(triple_grad, qkv_weight)
    norm_value, norm_back = jax.vjp(modulate, residual, pieces[0], pieces[1])
    residual_grad, offset_grad, scaling_grad = norm_back(hidden_grad)
    table_grad = table_sums([offset_grad, scaling_grad, gate_grad] + ffn_table)
    zero_row = jnp.zeros((D,), jnp.float32)
    vector_grad = jnp.concatenate(
        [
            jnp.stack(
                [
                    query_bias,
                    value_bias,
                    out_bias,
                    ffn_grads[3],
                    cross_query_bias,
                    zero_row,
                    cross_bias,
                    zero_row,
                ]
            ),
            table_grad,
            ffn_grads[2].reshape(4, D),
        ],
        axis=0,
    )
    terms = (
        qkv_grad,
        out_weight_grad,
        ffn_grads[0],
        ffn_grads[1],
        query_weight_grad,
        cross_weight_grad,
        vector_grad,
    )
    return (middle_grad + residual_grad, terms, keyval_grad)


def on_device(
    video,
    segment_ids,
    timesteps,
    drop_mask,
    captions,
    null_caption,
    caption_weight,
    spatial_qkv,
    spatial_out,
    spatial_expand,
    spatial_shrink,
    spatial_vectors,
    temporal_qkv,
    temporal_out,
    temporal_expand,
    temporal_shrink,
    cross_query,
    cross_keyval,
    cross_out,
    temporal_vectors,
    cotangent,
):
    groups, frames, patches = video.shape[:3]
    spatial = (
        lax.all_gather(spatial_qkv, "sp", axis=0, tiled=True),
        lax.all_gather(spatial_out, "sp", axis=0, tiled=True),
        lax.all_gather(spatial_expand, "sp", axis=0, tiled=True),
        lax.all_gather(spatial_shrink, "sp", axis=0, tiled=True),
        lax.all_gather(spatial_vectors, "sp", axis=1, tiled=True),
    )
    dropped = (drop_mask > 0).astype(jnp.float32)
    text_local = jnp.where(drop_mask[:, :, None, None] > 0, null_caption[None, None], captions)
    text_rows = text_local.reshape(groups, CLIPS * CAP, -1)
    caption_sum = lax.psum(project(text_rows, caption_weight), "sp")
    frame_mod = frame_modulation(segment_ids, timesteps).reshape(groups, frames, 6, D)
    same_clip = (segment_ids[:, :, None] == segment_ids[:, None, :])[:, None, None]
    row_clip = jnp.arange(CLIPS * CAP) // CAP
    allowed = (segment_ids[:, :, None] == row_clip[None, None, :])[:, :, None, None, :]
    residual = video.astype(jnp.float32)
    middle, spatial_kept = spatial_forward(residual, spatial, frame_mod)
    temporal = (
        lax.all_gather(temporal_qkv, "sp", axis=0, tiled=True),
        lax.all_gather(temporal_out, "sp", axis=0, tiled=True),
        lax.all_gather(temporal_expand, "sp", axis=0, tiled=True),
        lax.all_gather(temporal_shrink, "sp", axis=0, tiled=True),
        lax.all_gather(cross_query, "sp", axis=0, tiled=True),
        lax.all_gather(cross_keyval, "sp", axis=0, tiled=True),
        lax.all_gather(cross_out, "sp", axis=0, tiled=True),
        lax.all_gather(temporal_vectors, "sp", axis=1, tiled=True),
    )
    context = (caption_sum + as_float(temporal[7])[7]).astype(jnp.bfloat16)
    result, temporal_kept = temporal_forward(
        middle, temporal, frame_mod, same_clip, allowed, context
    )
    output = result.astype(jnp.bfloat16)
    temporal = (
        lax.all_gather(temporal_qkv, "sp", axis=0, tiled=True),
        lax.all_gather(temporal_out, "sp", axis=0, tiled=True),
        lax.all_gather(temporal_expand, "sp", axis=0, tiled=True),
        lax.all_gather(temporal_shrink, "sp", axis=0, tiled=True),
        lax.all_gather(cross_query, "sp", axis=0, tiled=True),
        lax.all_gather(cross_keyval, "sp", axis=0, tiled=True),
        lax.all_gather(cross_out, "sp", axis=0, tiled=True),
        lax.all_gather(temporal_vectors, "sp", axis=1, tiled=True),
    )
    middle_grad, temporal_terms, keyval_grad = temporal_backward(
        cotangent.astype(jnp.float32),
        middle,
        temporal,
        frame_mod,
        same_clip,
        allowed,
        temporal_kept,
    )
    shard_rows = D // lax.axis_size("sp")
    first_row = lax.axis_index("sp") * shard_rows
    context_grad = input_grad(keyval_grad, temporal[5]).astype(jnp.bfloat16)
    local_context = lax.dynamic_slice_in_dim(context, first_row, shard_rows, 2)
    keyval_weight_grad = weight_grad(local_context, keyval_grad)
    value_bias_full = column_sum(keyval_grad).reshape(HEADS, 2, HEAD_DIM)[:, 1].reshape(D)
    caption_bias_full = column_sum(context_grad)
    caption_weight_grad = weight_grad(text_rows, context_grad)
    text_grad = input_grad(context_grad, caption_weight).reshape(groups, CLIPS, CAP, -1)
    null_grad = jnp.sum(text_grad * dropped[:, :, None, None], axis=(0, 1))
    temporal_shards = (
        lax.psum_scatter(temporal_terms[0], "sp", scatter_dimension=0, tiled=True),
        lax.psum_scatter(temporal_terms[1], "sp", scatter_dimension=0, tiled=True),
        lax.psum_scatter(temporal_terms[2], "sp", scatter_dimension=0, tiled=True),
        lax.psum_scatter(temporal_terms[3], "sp", scatter_dimension=0, tiled=True),
        lax.psum_scatter(temporal_terms[4], "sp", scatter_dimension=0, tiled=True),
        lax.psum_scatter(temporal_terms[5], "sp", scatter_dimension=0, tiled=True),
        lax.psum_scatter(temporal_terms[6], "sp", scatter_dimension=1, tiled=True),
    )
    vector_fix = jnp.zeros((18, shard_rows), jnp.float32)
    vector_fix = vector_fix.at[5].set(
        lax.dynamic_slice_in_dim(value_bias_full, first_row, shard_rows, 0)
    )
    vector_fix = vector_fix.at[7].set(
        lax.dynamic_slice_in_dim(caption_bias_full, first_row, shard_rows, 0)
    )
    spatial = (
        lax.all_gather(spatial_qkv, "sp", axis=0, tiled=True),
        lax.all_gather(spatial_out, "sp", axis=0, tiled=True),
        lax.all_gather(spatial_expand, "sp", axis=0, tiled=True),
        lax.all_gather(spatial_shrink, "sp", axis=0, tiled=True),
        lax.all_gather(spatial_vectors, "sp", axis=1, tiled=True),
    )
    video_grad, spatial_terms = spatial_backward(
        middle_grad, residual, spatial, frame_mod, spatial_kept
    )
    spatial_shards = (
        lax.psum_scatter(spatial_terms[0], "sp", scatter_dimension=0, tiled=True),
        lax.psum_scatter(spatial_terms[1], "sp", scatter_dimension=0, tiled=True),
        lax.psum_scatter(spatial_terms[2], "sp", scatter_dimension=0, tiled=True),
        lax.psum_scatter(spatial_terms[3], "sp", scatter_dimension=0, tiled=True),
        lax.psum_scatter(spatial_terms[4], "sp", scatter_dimension=1, tiled=True),
    )
    halves = (
        lax.psum_scatter(
            null_grad.astype(jnp.bfloat16), "seq", scatter_dimension=0, tiled=True
        ).astype(jnp.float32),
        lax.psum_scatter(
            caption_weight_grad.astype(jnp.bfloat16), "seq", scatter_dimension=1, tiled=True
        ).astype(jnp.float32),
        lax.psum_scatter(
            spatial_shards[0].astype(jnp.bfloat16), "seq", scatter_dimension=1, tiled=True
        ).astype(jnp.float32),
        lax.psum_scatter(
            spatial_shards[1].astype(jnp.bfloat16), "seq", scatter_dimension=1, tiled=True
        ).astype(jnp.float32),
        lax.psum_scatter(
            spatial_shards[2].astype(jnp.bfloat16), "seq", scatter_dimension=1, tiled=True
        ).astype(jnp.float32),
        lax.psum_scatter(
            spatial_shards[3].astype(jnp.bfloat16), "seq", scatter_dimension=1, tiled=True
        ).astype(jnp.float32),
        lax.psum_scatter(
            spatial_shards[4].astype(jnp.bfloat16), "seq", scatter_dimension=0, tiled=True
        ).astype(jnp.float32),
        lax.psum_scatter(
            temporal_shards[0].astype(jnp.bfloat16), "seq", scatter_dimension=1, tiled=True
        ).astype(jnp.float32),
        lax.psum_scatter(
            temporal_shards[1].astype(jnp.bfloat16), "seq", scatter_dimension=1, tiled=True
        ).astype(jnp.float32),
        lax.psum_scatter(
            temporal_shards[2].astype(jnp.bfloat16), "seq", scatter_dimension=1, tiled=True
        ).astype(jnp.float32),
        lax.psum_scatter(
            temporal_shards[3].astype(jnp.bfloat16), "seq", scatter_dimension=1, tiled=True
        ).astype(jnp.float32),
        lax.psum_scatter(
            temporal_shards[4].astype(jnp.bfloat16), "seq", scatter_dimension=1, tiled=True
        ).astype(jnp.float32),
        lax.psum_scatter(
            keyval_weight_grad.astype(jnp.bfloat16), "seq", scatter_dimension=1, tiled=True
        ).astype(jnp.float32),
        lax.psum_scatter(
            temporal_shards[5].astype(jnp.bfloat16), "seq", scatter_dimension=1, tiled=True
        ).astype(jnp.float32),
        lax.psum_scatter(
            (temporal_shards[6] + vector_fix).astype(jnp.bfloat16),
            "seq",
            scatter_dimension=0,
            tiled=True,
        ).astype(jnp.float32),
    )
    totals = (
        lax.all_gather(halves[0].astype(jnp.bfloat16), "seq", axis=0, tiled=True).astype(
            jnp.float32
        ),
        lax.all_gather(halves[1].astype(jnp.bfloat16), "seq", axis=1, tiled=True).astype(
            jnp.float32
        ),
        lax.all_gather(halves[2].astype(jnp.bfloat16), "seq", axis=1, tiled=True).astype(
            jnp.float32
        ),
        lax.all_gather(halves[3].astype(jnp.bfloat16), "seq", axis=1, tiled=True).astype(
            jnp.float32
        ),
        lax.all_gather(halves[4].astype(jnp.bfloat16), "seq", axis=1, tiled=True).astype(
            jnp.float32
        ),
        lax.all_gather(halves[5].astype(jnp.bfloat16), "seq", axis=1, tiled=True).astype(
            jnp.float32
        ),
        lax.all_gather(halves[6].astype(jnp.bfloat16), "seq", axis=0, tiled=True).astype(
            jnp.float32
        ),
        lax.all_gather(halves[7].astype(jnp.bfloat16), "seq", axis=1, tiled=True).astype(
            jnp.float32
        ),
        lax.all_gather(halves[8].astype(jnp.bfloat16), "seq", axis=1, tiled=True).astype(
            jnp.float32
        ),
        lax.all_gather(halves[9].astype(jnp.bfloat16), "seq", axis=1, tiled=True).astype(
            jnp.float32
        ),
        lax.all_gather(halves[10].astype(jnp.bfloat16), "seq", axis=1, tiled=True).astype(
            jnp.float32
        ),
        lax.all_gather(halves[11].astype(jnp.bfloat16), "seq", axis=1, tiled=True).astype(
            jnp.float32
        ),
        lax.all_gather(halves[12].astype(jnp.bfloat16), "seq", axis=1, tiled=True).astype(
            jnp.float32
        ),
        lax.all_gather(halves[13].astype(jnp.bfloat16), "seq", axis=1, tiled=True).astype(
            jnp.float32
        ),
        lax.all_gather(halves[14].astype(jnp.bfloat16), "seq", axis=0, tiled=True).astype(
            jnp.float32
        ),
    )
    return (
        output,
        video_grad.astype(jnp.bfloat16),
        totals[0],
        totals[1],
        totals[2],
        totals[3],
        totals[4],
        totals[5],
        totals[6],
        totals[7],
        totals[8],
        totals[9],
        totals[10],
        totals[11],
        totals[12],
        totals[13],
        totals[14],
    )


def solution(mesh):
    return jax.shard_map(
        on_device,
        mesh=mesh,
        in_specs=(
            P("seq", None, "sp", None),
            P("seq", None),
            P("seq", None),
            P("seq", None),
            P("seq", None, None, "sp"),
            P(None, "sp"),
            P("sp", None),
            P("sp", None),
            P("sp", None),
            P("sp", None),
            P("sp", None),
            P(None, "sp"),
            P("sp", None),
            P("sp", None),
            P("sp", None),
            P("sp", None),
            P("sp", None),
            P("sp", None),
            P("sp", None),
            P(None, "sp"),
            P("seq", None, "sp", None),
        ),
        out_specs=(
            P("seq", None, "sp", None),
            P("seq", None, "sp", None),
            P(None, "sp"),
            P("sp", None),
            P("sp", None),
            P("sp", None),
            P("sp", None),
            P("sp", None),
            P(None, "sp"),
            P("sp", None),
            P("sp", None),
            P("sp", None),
            P("sp", None),
            P("sp", None),
            P("sp", None),
            P("sp", None),
            P(None, "sp"),
        ),
        check_vma=False,
    )
```

profile of v0, /device:TPU:0, one launch (start us, length us, event | category | flops | bytes accessed | tf_op | source)
XLA Modules:
  0.0 2925.4 jit_solution(9453978804358284563)
XLA Ops:
  19.6 23.7 all-gather
  44.2 18.5 all-gather.1
  70.3 15.5 all-gather.25.cloned.1.call-done
  128.2 24.8 all-to-all-done
  165.1 14.3 all-to-all-start.1
  179.4 43.0 %all-reduce.21.cloned.1.call-done = f32[2,240,1152]{2,1,0:T(8,128)} async-done(((f32[2,240,1152]{2,1,0:T(8,128)}), f32[2,240,1152]{2,1,0:T(8,128)}) %all-reduce.21.cloned.1.call-update) | async-done | bytes 2211856 | tf_op jit(solution)/shard_map/psum | solution.py:514
  224.2 57.0 %all-gather.37.cloned.1.call-done = bf16[1152,2304]{1,0:T(8,128)(2,1)} async-done(((bf16[72,2304]{1,0:T(8,128)(2,1)}), bf16[1152,2304]{1,0:T(8,128)(2,1)}) %all-gather.37.cloned.1.call-update) | async-done | bytes 5308432 | tf_op jit(solution)/shard_map/all_gather | solution.py:527
  296.5 28.7 all-gather.27.cloned.1.call-done
  329.4 85.3 %all-gather.29.cloned.1.call-done = bf16[1152,4608]{1,0:T(8,128)(2,1)} async-done(((bf16[72,4608]{1,0:T(8,128)(2,1)}), bf16[1152,4608]{1,0:T(8,128)(2,1)}) %all-gather.29.cloned.1.call-update) | async-done | bytes 10616848 | tf_op jit(solution)/shard_map/all_gather | solution.py:507
  424.0 79.8 %all-gather.31.cloned.1.call-done = bf16[4608,1152]{1,0:T(8,128)(2,1)} async-done(((bf16[288,1152]{1,0:T(8,128)(2,1)}), bf16[4608,1152]{1,0:T(8,128)(2,1)}) %all-gather.31.cloned.1.call-update) | async-done | bytes 10616848 | tf_op jit(solution)/shard_map/all_gather | solution.py:508
  515.0 61.4 %all-gather.33.cloned.1.call-done = bf16[1152,3456]{1,0:T(8,128)(2,1)} async-done(((bf16[72,3456]{1,0:T(8,128)(2,1)}), bf16[1152,3456]{1,0:T(8,128)(2,1)}) %all-gather.33.cloned.1.call-update) | async-done | bytes 7962640 | tf_op jit(solution)/shard_map/all_gather | solution.py:522
  607.1 13.1 all-gather.35.cloned.1.call-done
  623.1 41.3 %all-gather.39.cloned.1.call-done = bf16[1152,1152]{1,0:T(8,128)(2,1)} async-done(((bf16[72,1152]{1,0:T(8,128)(2,1)}), bf16[1152,1152]{1,0:T(8,128)(2,1)}) %all-gather.39.cloned.1.call-update) | async-done | bytes 2654224 | tf_op jit(solution)/shard_map/all_gather | solution.py:526
  683.0 25.4 all-gather.41.cloned.1.call-done
  713.4 84.7 %all-gather.43.cloned.1.call-done = bf16[1152,4608]{1,0:T(8,128)(2,1)} async-done(((bf16[72,4608]{1,0:T(8,128)(2,1)}), bf16[1152,4608]{1,0:T(8,128)(2,1)}) %all-gather.43.cloned.1.call-update) | async-done | bytes 10616848 | tf_op jit(solution)/shard_map/all_gather | solution.py:524
  807.9 79.3 %all-gather.45.cloned.1.call-done = bf16[4608,1152]{1,0:T(8,128)(2,1)} async-done(((bf16[288,1152]{1,0:T(8,128)(2,1)}), bf16[4608,1152]{1,0:T(8,128)(2,1)}) %all-gather.45.cloned.1.call-update) | async-done | bytes 10616848 | tf_op jit(solution)/shard_map/all_gather | solution.py:525
  1042.9 36.5 %all_to_all.68 = bf16[16,32,8,72]{3,2,1,0:T(8,128)(2,1)S(1)} all-to-all(bf16[16,32,8,72]{3,2,1,0:T(8,128)(2,1)S(1)} %bitcast.552), channel_id=1, replica_groups=mesh['seq'=2,'sp'=16] {'sp'}, dimensions={0} | all-to-all | bytes 1179648 | tf_op jit(solution)/shard_map/all_to_all | solution.py:182
  1088.3 77.0 %all_to_all.69 = bf16[1,32,128,216]{3,1,0,2:T(8,128)(2,1)S(1)} all-to-all(bf16[1,32,128,216]{3,1,0,2:T(8,128)(2,1)S(1)} %copy.350), channel_id=1, replica_groups=mesh['seq'=2,'sp'=16] {'sp'}, dimensions={2} | all-to-all | bytes 3538944 | tf_op jit(solution)/shard_map/all_to_all | solution.py:163
  1183.8 14.4 convolution_bitcast_fusion
  1199.3 14.5 convolution_bitcast_fusion.1
  1231.4 12.1 convolution_bitcast_fusion.2
  1278.1 126.0 %all-reduce.24 = (bf16[2,240,2304]{2,1,0:T(8,128)(2,1)S(1)}, bf16[14,1152]{1,0:T(8,128)(2,1)}) all-reduce(f32[2,240,2304]{2,1,0:T(8,128)} %copy.356, f32[14,1152]{1,0:T(8,128)S(1)} %concatenate.56), channel_id=1, replica_groups=mesh['seq'=2,'sp'=16] {'sp'}, use_global_device_ids=true, to_apply=%region_26.27 | all-reduce | flops 1122048 | bytes 6732288 | tf_op jit(solution)/shard_map/psum | solution.py:400
  1432.1 123.1 %reduce-scatter.95.cloned.1.call-done = f32[72,3456]{1,0:T(8,128)} async-done(((f32[1152,3456]{1,0:T(8,128)}), f32[72,3456]{1,0:T(8,128)}) %reduce-scatter.95.cloned.1.call-update) | async-done | bytes 995344
  1559.6 170.6 %reduce-scatter.91.cloned.1.call-done = f32[72,3456]{1,0:T(8,128)} async-done(((f32[1152,3456]{1,0:T(8,128)}), f32[72,3456]{1,0:T(8,128)}) %reduce-scatter.91.cloned.1.call-update) | async-done | bytes 995344
  1734.6 211.7 %reduce-scatter.71.cloned.1.call-done = f32[288,1152]{1,0:T(8,128)} async-done(((f32[4608,1152]{1,0:T(8,128)}), f32[288,1152]{1,0:T(8,128)}) %reduce-scatter.71.cloned.1.call-update) | async-done | bytes 1327120 | tf_op jit(solution)/shard_map/reduce_scatter | solution.py:569
  1951.0 211.9 %reduce-scatter.65.cloned.1.call-done = f32[288,1152]{1,0:T(8,128)} async-done(((f32[4608,1152]{1,0:T(8,128)}), f32[288,1152]{1,0:T(8,128)}) %reduce-scatter.65.cloned.1.call-update) | async-done | bytes 1327120 | tf_op jit(solution)/shard_map/reduce_scatter | solution.py:595
  2179.7 199.4 %reduce-scatter.61.cloned.1.call-done = f32[72,4608]{1,0:T(8,128)} async-done(((f32[1152,4608]{1,0:T(8,128)}), f32[72,4608]{1,0:T(8,128)}) %reduce-scatter.61.cloned.1.call-update) | async-done | bytes 1327120 | tf_op jit(solution)/shard_map/reduce_scatter | solution.py:594
  2381.4 86.5 %all-reduce.23.cloned.1.call-done = f32[18,1152]{1,0:T(8,128)} async-done(((f32[18,1152]{1,0:T(8,128)}), f32[18,1152]{1,0:T(8,128)}) %all-reduce.23.cloned.1.call-update) | async-done | bytes 82960
  2500.3 187.1 %reduce-scatter.67.cloned.1.call-done = f32[72,4608]{1,0:T(8,128)} async-done(((f32[1152,4608]{1,0:T(8,128)}), f32[72,4608]{1,0:T(8,128)}) %reduce-scatter.67.cloned.1.call-update) | async-done | bytes 1327120 | tf_op jit(solution)/shard_map/reduce_scatter | solution.py:568
  2788.0 13.8 reduce-scatter.79.cloned.1.call-done
  2845.9 13.6 all-gather.9
  2868.7 13.7 all-gather.5
  (713 shorter events, 698.6 us)
Async XLA Ops:
  13.6 311.6 %all-gather.27.cloned.1.call-start = ((), (), s32[]{:S(2)}) async-start(), calls=%async_computation.27 | async-start | bytes 2820096 | tf_op jit(solution)/shard_map/all_gather | solution.py:506
  14.2 400.5 %all-gather.29.cloned.1.call-start = ((), (), s32[]{:S(2)}) async-start(), calls=%async_computation.28 | async-start | bytes 11280384 | tf_op jit(solution)/shard_map/all_gather | solution.py:507
  14.8 489.0 %all-gather.31.cloned.1.call-start = ((), (), s32[]{:S(2)}) async-start(), calls=%async_computation.29 | async-start | bytes 11280384 | tf_op jit(solution)/shard_map/all_gather | solution.py:508
  15.4 560.9 %all-gather.33.cloned.1.call-start = ((), (), s32[]{:S(2)}) async-start(), calls=%async_computation.30 | async-start | bytes 8460288 | tf_op jit(solution)/shard_map/all_gather | solution.py:522
  16.1 604.0 %all-gather.35.cloned.1.call-start = ((), (), s32[]{:S(2)}) async-start(), calls=%async_computation.31 | async-start | bytes 2820096 | tf_op jit(solution)/shard_map/all_gather | solution.py:523
  16.9 647.5 %all-gather.39.cloned.1.call-start = ((), (), s32[]{:S(2)}) async-start(), calls=%async_computation.34 | async-start | bytes 2820096 | tf_op jit(solution)/shard_map/all_gather | solution.py:526
  17.6 690.8 %all-gather.41.cloned.1.call-start = ((), (), s32[]{:S(2)}) async-start(), calls=%async_computation.35 | async-start | bytes 2820096 | tf_op jit(solution)/shard_map/all_gather | solution.py:528
  18.2 779.9 %all-gather.43.cloned.1.call-start = ((), (), s32[]{:S(2)}) async-start(), calls=%async_computation.36 | async-start | bytes 11280384 | tf_op jit(solution)/shard_map/all_gather | solution.py:524
  19.0 868.2 %all-gather.45.cloned.1.call-start = ((), (), s32[]{:S(2)}) async-start(), calls=%async_computation.37 | async-start | bytes 11280384 | tf_op jit(solution)/shard_map/all_gather | solution.py:525
  179.4 1238.4 %reduce-scatter.93.cloned.1.call-start = ((), (), s32[]{:S(2)}) async-start(), calls=%async_computation.56 | async-start | bytes 5640192
  1001.7 419.7 %reduce-scatter.99.cloned.1.call-start = ((), (), s32[]{:S(2)}) async-start(), calls=%async_computation.59 | async-start | bytes 5640192
  1007.6 417.5 %reduce-scatter.101.cloned.1.call-start = ((), (), s32[]{:S(2)}) async-start(), calls=%async_computation.60 | async-start | bytes 5640192
  1013.4 415.2 %reduce-scatter.97.cloned.1.call-start = ((), (), s32[]{:S(2)}) async-start(), calls=%async_computation.58 | async-start | bytes 5640192
  1019.2 536.1 %reduce-scatter.95.cloned.1.call-start = ((), (), s32[]{:S(2)}) async-start(), calls=%async_computation.57 | async-start | bytes 16920576
  1034.9 695.4 %reduce-scatter.91.cloned.1.call-start = ((), (), s32[]{:S(2)}) async-start(), calls=%async_computation.55 | async-start | bytes 16920576
  1182.8 763.6 %reduce-scatter.71.cloned.1.call-start = ((), (), s32[]{:S(2)}) async-start(), calls=%async_computation.44 | async-start | bytes 22560768 | tf_op jit(solution)/shard_map/reduce_scatter | solution.py:569
  1198.2 964.7 %reduce-scatter.65.cloned.1.call-start = ((), (), s32[]{:S(2)}) async-start(), calls=%async_computation.41 | async-start | bytes 22560768 | tf_op jit(solution)/shard_map/reduce_scatter | solution.py:595
  1213.9 1165.2 %reduce-scatter.61.cloned.1.call-start = ((), (), s32[]{:S(2)}) async-start(), calls=%async_computation.39 | async-start | bytes 22560768 | tf_op jit(solution)/shard_map/reduce_scatter | solution.py:594
  1227.3 1240.6 %all-reduce.23.cloned.1.call-start = ((), (), s32[]{:S(2)}) async-start(), calls=%async_computation.54 | async-start | bytes 221184
  1231.3 1456.1 %reduce-scatter.67.cloned.1.call-start = ((), (), s32[]{:S(2)}) async-start(), calls=%async_computation.42 | async-start | bytes 22560768 | tf_op jit(solution)/shard_map/reduce_scatter | solution.py:568
  1243.5 1461.1 %reduce-scatter.87.cloned.1.call-start = ((), (), s32[]{:S(2)}) async-start(), calls=%async_computation.52 | async-start | bytes 884736
  1408.4 1313.5 %reduce-scatter.59.cloned.1.call-start = ((), (), s32[]{:S(2)}) async-start(), calls=%async_computation.38 | async-start | bytes 884736 | tf_op jit(solution)/shard_map/reduce_scatter | solution.py:602
  1417.7 1318.9 %reduce-scatter.75.cloned.1.call-start = ((), (), s32[]{:S(2)}) async-start(), calls=%async_computation.46 | async-start | bytes 442368
  1421.4 1330.0 %reduce-scatter.85.cloned.1.call-start = ((), (), s32[]{:S(2)}) async-start(), calls=%async_computation.51 | async-start | bytes 442368
  1425.0 1340.8 %reduce-scatter.89.cloned.1.call-start = ((), (), s32[]{:S(2)}) async-start(), calls=%async_computation.53 | async-start | bytes 442368
  1428.5 1352.1 %reduce-scatter.81.cloned.1.call-start = ((), (), s32[]{:S(2)}) async-start(), calls=%async_computation.49 | async-start | bytes 442368
  1432.1 1369.8 %reduce-scatter.79.cloned.1.call-start = ((), (), s32[]{:S(2)}) async-start(), calls=%async_computation.48 | async-start | bytes 1327104
  1559.6 1263.7 %reduce-scatter.73.cloned.1.call-start = ((), (), s32[]{:S(2)}) async-start(), calls=%async_computation.45 | async-start | bytes 1327104
  1734.6 1110.1 %reduce-scatter.83.cloned.1.call-start = ((), (), s32[]{:S(2)}) async-start(), calls=%async_computation.50 | async-start | bytes 1327104
  1951.0 916.4 %reduce-scatter.77.cloned.1.call-start = ((), (), s32[]{:S(2)}) async-start(), calls=%async_computation.47 | async-start | bytes 1327104
  2167.5 720.6 %reduce-scatter.63.cloned.1.call-start = ((), (), s32[]{:S(2)}) async-start(), calls=%async_computation.40 | async-start | bytes 995328 | tf_op jit(solution)/shard_map/reduce_scatter | solution.py:611
  2381.3 525.5 %reduce-scatter.69.cloned.1.call-start = ((), (), s32[]{:S(2)}) async-start(), calls=%async_computation.43 | async-start | bytes 995328 | tf_op jit(solution)/shard_map/reduce_scatter | solution.py:626
  (171 other events, 4786.2 us)
Sparse Core Ops, SparseCore 0:
  10.2 75.5 all-gather.24
  89.3 133.0 all-reduce.20
  224.6 56.5 all-gather.36
  283.3 41.8 all-gather.26
  327.3 87.3 all-gather.28
  416.9 86.8 all-gather.30
  505.9 70.3 all-gather.32
  578.5 41.6 all-gather.34
  622.3 42.0 all-gather.38
  666.4 42.0 all-gather.40
  710.7 87.3 all-gather.42
  800.3 86.8 all-gather.44
  1001.8 91.4 reduce-scatter.92
  1097.2 89.6 reduce-scatter.98
  1190.7 78.5 reduce-scatter.100
  1273.2 104.3 reduce-scatter.96
  1381.6 173.6 reduce-scatter.94
  1559.3 170.9 reduce-scatter.90
  1734.4 211.9 reduce-scatter.70
  1950.9 211.9 reduce-scatter.64
  2167.0 211.9 reduce-scatter.60
  2383.5 84.3 all-reduce.22
  2472.5 214.8 reduce-scatter.66
  2689.5 15.0 reduce-scatter.86
  2707.0 14.8 reduce-scatter.58
  2739.3 12.0 reduce-scatter.84
  2783.3 18.5 reduce-scatter.78
  2804.7 18.5 reduce-scatter.72
  2826.1 18.5 reduce-scatter.82
  2847.3 20.0 reduce-scatter.76
  2870.3 17.7 reduce-scatter.62
  2890.4 16.3 reduce-scatter.68
  (3 shorter events, 35.9 us)
where the time goes:
time: 2940 us; the launch traced here: 2930 us
  waiting for transfers between devices  1920 us (65%)
  blocking collectives  412 us (14%)
  matrix products  276 us (9%)
  local copies, waits for them, and re-layouts  209 us (7%)
  other arithmetic  61 us (2%)
    unnamed x53, waiting for transfers between devices  455 us
    reduce_scatter x1, waiting for transfers between devices, on_device(): lax.psum_scatter(spatial_terms[3], 'sp', scatter_dimension=0, tiled=True)  212 us
    reduce_scatter x1, waiting for transfers between devices, on_device(): lax.psum_scatter(temporal_terms[3], 'sp', scatter_dimension=0, tiled=True)  212 us
    reduce_scatter x1, waiting for transfers between devices, on_device(): lax.psum_scatter(spatial_terms[2], 'sp', scatter_dimension=0, tiled=True)  199 us
    reduce_scatter x1, waiting for transfers between devices, on_device(): lax.psum_scatter(temporal_terms[2], 'sp', scatter_dimension=0, tiled=True)  187 us
    psum x1, blocking collectives, temporal_backward(): keyval_grad = lax.psum(keyval_grad, 'sp').astype(jnp.bfloat16)  126 us
    dot_general x12, matrix products, weight_grad(): lax.dot_general(left_rows, right_rows, (((0,), (0,)), ((), ())), preferre...  88.6 us
    all_gather x1, waiting for transfers between devices, on_device(): lax.all_gather(spatial_expand, 'sp', axis=0, tiled=True)  85.3 us
  transfers between devices with their start and end apart: 39, of which 32 were waited for; matrix products, arithmetic and copies ran while one was open for 14% of the time, Pallas kernels for 0%

commit v1 on v0

--- a/solution.py
+++ b/solution.py
@@ -1,8 +1,11 @@
+import functools
 import math
 
 import jax
 import jax.numpy as jnp
 from jax import lax
+from jax.experimental import pallas as pl
+from jax.experimental.pallas import tpu as pltpu
 from jax.sharding import PartitionSpec as P
 
 D = 1152
@@ -66,6 +69,272 @@
 
 def column_sum(gradients):
     return jnp.sum(gradients.astype(jnp.float32).reshape(-1, gradients.shape[-1]), axis=0)
+
+
+def index_bits():
+    return lax.axis_size("sp").bit_length() - 1
+
+
+def swap_sp(values, bit):
+    size = lax.axis_size("sp")
+    return lax.ppermute(values, "sp", [(i, i ^ (1 << bit)) for i in range(size)])
+
+
+def swap_seq(values):
+    return lax.ppermute(values, "seq", [(0, 1), (1, 0)])
+
+
+def far_bits():
+    return list(range(index_bits() - 1, 1, -1))
+
+
+def gather_chip_rows(half, seq_first):
+    blocks = half[None]
+    for bit in far_bits():
+        blocks = jnp.concatenate([blocks, swap_sp(blocks, bit)], axis=0)
+    if seq_first:
+        other = swap_seq(blocks)
+        other = jnp.concatenate([other, swap_sp(other, 1)], axis=0)
+        blocks = jnp.concatenate([blocks, swap_sp(blocks, 1)], axis=0)
+    else:
+        blocks = jnp.concatenate([blocks, swap_sp(blocks, 1)], axis=0)
+        other = swap_seq(blocks)
+    return blocks, other
+
+
+def place_kernel(bits, moves, n_in, n_out, *refs):
+    sources, outs, sems = refs[:n_in], refs[n_in : n_in + n_out], refs[n_in + n_out :]
+    local_sem, send_sem, recv_sem = sems
+    me = lax.axis_index("sp")
+    plane = lax.axis_index("seq")
+    sibling = me + 1 - 2 * (me % 2)
+    barrier = pltpu.get_barrier_semaphore()
+    pl.semaphore_signal(
+        barrier, inc=1, device_id=(plane, sibling), device_id_type=pl.DeviceIdType.MESH
+    )
+    pl.semaphore_wait(barrier, 1)
+    count = sources[0].shape[0]
+
+    def block_at(p):
+        block = me
+        for i, bit in enumerate(bits):
+            mine = (me // (1 << bit)) % 2
+            block = block + ((p // (1 << i)) % 2) * ((1 << bit) * (1 - 2 * mine))
+        return block
+
+    for own_half in (0, 1):
+
+        @pl.when(plane == own_half)
+        def _():
+            def copies(p):
+                block = block_at(p)
+                result = []
+                for side in (0, 1):
+                    half = own_half if side == 0 else 1 - own_half
+                    for pair, first, width, out, place in moves[half]:
+                        source = sources[2 * pair + side]
+                        target = outs[out]
+                        if first is None:
+                            src, dst = source.at[p], target.at[block, place]
+                        else:
+                            src = source.at[p, :, pl.ds(first, width)]
+                            dst = target.at[block, :, pl.ds(place, width)]
+                        k = len(result)
+                        result.append(
+                            (
+                                pltpu.make_async_copy(src, dst, local_sem.at[p, k]),
+                                pltpu.make_async_remote_copy(
+                                    src_ref=src,
+                                    dst_ref=dst,
+                                    send_sem=send_sem.at[p, k],
+                                    recv_sem=recv_sem.at[p, k],
+                                    device_id=(plane, sibling),
+                                    device_id_type=pl.DeviceIdType.MESH,
+                                ),
+                            )
+                        )
+                return result
+
+            def begin(p, carry):
+                for local, remote in copies(p):
+                    remote.start()
+                    local.start()
+                return carry
+
+            def finish(p, carry):
+                for local, remote in copies(p):
+                    local.wait()
+                    remote.wait()
+                return carry
+
+            lax.fori_loop(0, count, begin, 0)
+            lax.fori_loop(0, count, finish, 0)
+
+
+def place_blocks(pairs, moves, shapes, collective_id):
+    arrays = [member for pair in pairs for member in pair]
+    bits = far_bits() + [1]
+    count = arrays[0].shape[0]
+    copies = len(moves[0]) + len(moves[1])
+    any_space = pl.BlockSpec(memory_space=pl.ANY)
+    total = sum(2 * math.prod(shape) for shape in shapes)
+    return pl.pallas_call(
+        functools.partial(place_kernel, bits, moves, len(arrays), len(shapes)),
+        out_shape=[jax.ShapeDtypeStruct(shape, jnp.bfloat16) for shape in shapes],
+        in_specs=[pl.BlockSpec(memory_space=pltpu.VMEM)] * len(arrays),
+        out_specs=[any_space] * len(shapes),
+        scratch_shapes=[pltpu.SemaphoreType.DMA((count, copies))] * 3,
+        compiler_params=pltpu.CompilerParams(
+            collective_id=collective_id, has_side_effects=True, vmem_limit_bytes=32 << 20
+        ),
+        cost_estimate=pl.CostEstimate(flops=0, bytes_accessed=2 * total, transcendentals=0),
+    )(*arrays)
+
+
+def pick_half(first, second):
+    return jnp.where(lax.axis_index("seq") == 0, first, second)
+
+
+def gather_full(shard):
+    return lax.all_gather(shard, "sp", axis=0, tiled=True)
+
+
+def gather_columns(members, parts, orders, collective_id):
+    rows = members[0].shape[0]
+    size = lax.axis_size("sp")
+    if rows % 8 or lax.axis_size("seq") != 2:
+        return [gather_full(member) for member in members]
+    pairs, moves = [], ([], [])
+    for number, (halves, seq_first) in enumerate(zip(parts, orders)):
+        picked = []
+        for half, pieces in enumerate(halves):
+            columns = [members[w][:, first : first + width] for w, first, width in pieces]
+            picked.append(columns[0] if len(columns) == 1 else jnp.concatenate(columns, axis=1))
+            place = 0
+            for w, first, width in pieces:
+                moves[half].append((number, place, width, w, first))
+                place += width
+        pairs.append(gather_chip_rows(pick_half(*picked), seq_first))
+    shapes = [(size, rows, member.shape[1]) for member in members]
+    placed = place_blocks(pairs, moves, shapes, collective_id)
+    return [full.reshape(size * rows, -1) for full in placed]
+
+
+def gather_tall(shard, seq_first, collective_id):
+    rows, columns = shard.shape
+    size = lax.axis_size("sp")
+    if rows % 32 or lax.axis_size("seq") != 2:
+        return gather_full(shard)
+    pair = gather_chip_rows(pick_half(shard[: rows // 2], shard[rows // 2 :]), seq_first)
+    moves = ([(0, None, None, 0, 0)], [(0, None, None, 0, 1)])
+    shape = (size, 2, rows // 2, columns)
+    (full,) = place_blocks([pair], moves, [shape], collective_id)
+    return full.reshape(size * rows, columns)
+
+
+def low_sum(*members):
+    total = members[0].astype(jnp.float32)
+    for member in members[1:]:
+        total = total + member.astype(jnp.float32)
+    return total.astype(jnp.bfloat16)
+
+
+def pick(values, index, axis):
+    return lax.dynamic_index_in_dim(values, index, axis, keepdims=False)
+
+
+def split_blocks(values, bit_value):
+    paired = values.reshape(values.shape[0] // 2, 2, *values.shape[1:])
+    return pick(paired, 1 - bit_value, 1), pick(paired, bit_value, 1)
+
+
+def scatter_grad(inputs, gradients, by_rows, seq_first):
+    size = lax.axis_size("sp")
+    me = lax.axis_index("sp")
+    plane = lax.axis_index("seq")
+    bits = [(me // (1 << b)) % 2 for b in range(index_bits())]
+    left = inputs.reshape(-1, inputs.shape[-1])
+    right = gradients.reshape(-1, gradients.shape[-1])
+    tokens, depth = left.shape
+    columns = right.shape[1]
+    rows = depth // size
+    half = (rows if by_rows else columns) // 2
+    grouped = left.reshape(tokens, size // 2, 2, rows)
+    sides = [pick_core(grouped, 1 - bits[0]), pick_core(grouped, bits[0])]
+    if by_rows:
+        sides = [
+            jnp.stack(
+                [
+                    pick_half(side[:, :, :half], side[:, :, half:]),
+                    pick_half(side[:, :, half:], side[:, :, :half]),
+                ],
+                axis=1,
+            )
+            for side in sides
+        ]
+    else:
+        padded = -(-half // 128) * 128
+        fill = ((0, 0), (0, padded - half))
+        right = jnp.concatenate(
+            [
+                jnp.pad(pick_half(right[:, :half], right[:, half:]), fill),
+                jnp.pad(pick_half(right[:, half:], right[:, :half]), fill),
+            ],
+            axis=1,
+        )
+
+    def product(side):
+        flat = side.reshape(tokens, depth // 2)
+        total = lax.dot_general(
+            flat, right, (((0,), (0,)), ((), ())), preferred_element_type=jnp.float32
+        ).astype(jnp.bfloat16)
+        if by_rows:
+            total = total.reshape(2, size // 2, half, columns)
+            return total[0], total[1]
+        total = total.reshape(size // 2, rows, -1)
+        return total
+
+    sent = product(sides[0])
+    kept = product(sides[1])
+    if by_rows:
+        came = [swap_sp(member, 0) for member in sent]
+        own, other = (kept[0], came[0]), (kept[1], came[1])
+    else:
+        came = swap_sp(sent, 0)
+        own = (kept[:, :, :padded], came[:, :, :padded])
+        other = (kept[:, :, padded:], came[:, :, padded:])
+    if seq_first:
+        current = (*own, swap_seq(low_sum(*other)))
+        current = halve(current, bits[1], 1)
+    else:
+        own = halve(own, bits[1], 1)
+        other = halve(other, bits[1], 1)
+        current = (*own, swap_seq(low_sum(*other)))
+    for bit in range(2, index_bits()):
+        current = halve(current, bits[bit], bit)
+    mine = low_sum(*current)[0]
+    theirs = swap_seq(mine)
+    if not by_rows:
+        mine, theirs = mine[:, :half], theirs[:, :half]
+    axis = 0 if by_rows else 1
+    return pick_half(
+        jnp.concatenate([mine, theirs], axis=axis), jnp.concatenate([theirs, mine], axis=axis)
+    ).astype(jnp.float32)
+
+
+def pick_core(grouped, which):
+    return jnp.where(which == 0, grouped[:, :, 0], grouped[:, :, 1])
+
+
+def halve(members, bit_value, bit):
+    parts = [split_blocks(member, bit_value) for member in members]
+    sent = low_sum(*[part[0] for part in parts])
+    return (low_sum(*[part[1] for part in parts]), swap_sp(sent, bit))
+
+
+def sum_seq(values):
+    mine = values.astype(jnp.bfloat16)
+    return mine.astype(jnp.float32) + swap_seq(mine).astype(jnp.float32)
 
 
 def triple_bias(query_bias, value_bias):
@@ -166,19 +435,17 @@
 def pair_attention(triple):
     groups, frames, patches = triple.shape[:3]
     shaped = triple.reshape(groups, frames, patches, HEADS, 3 * HEAD_DIM)
-    exchanged = attend_pairs(
-        lax.all_to_all(to_pairs(shaped), "sp", split_axis=0, concat_axis=2, tiled=True)
-    )
-    return from_pairs(exchanged, groups, frames).reshape(groups, frames, patches, D)
-
-
-def pair_attention_back(triple, mixture_grad):
-    groups, frames, patches = triple.shape[:3]
-    shaped = triple.reshape(groups, frames, patches, HEADS, 3 * HEAD_DIM)
+    pairs = lax.all_to_all(to_pairs(shaped), "sp", split_axis=0, concat_axis=2, tiled=True)
+    exchanged = attend_pairs(pairs)
+    return from_pairs(exchanged, groups, frames).reshape(groups, frames, patches, D), pairs
+
+
+def pair_attention_back(pairs, mixture_grad):
+    groups, frames, patches = mixture_grad.shape[:3]
     grad_shaped = mixture_grad.reshape(groups, frames, patches, HEADS, HEAD_DIM)
     returned = pair_backward(
         (
-            lax.all_to_all(to_pairs(shaped), "sp", split_axis=0, concat_axis=2, tiled=True),
+            pairs,
             lax.all_to_all(to_pairs(grad_shaped), "sp", split_axis=0, concat_axis=2, tiled=True),
         )
     )
@@ -196,11 +463,11 @@
 def feed_backward(grad_out, residual, offset, scaling, gating, stored, expand, shrink):
     hidden, inner_sum, active, branch = stored
     branch_grad, gate_grad = gated_back(grad_out, gating, branch)
-    shrink_grad = weight_grad(active, branch_grad)
+    shrink_grad = scatter_grad(active, branch_grad, True, True)
     active_grad = input_grad(branch_grad, shrink)
     gelu_value, gelu_back = jax.vjp(gelu_tanh, inner_sum)
     inner_grad = gelu_back(active_grad)[0].astype(jnp.bfloat16)
-    expand_grad = weight_grad(hidden, inner_grad)
+    expand_grad = scatter_grad(hidden, inner_grad, False, False)
     hidden_grad = input_grad(inner_grad, expand)
     norm_value, norm_back = jax.vjp(modulate, residual, offset, scaling)
     residual_grad, offset_grad, scaling_grad = norm_back(hidden_grad)
@@ -223,28 +490,34 @@
     triple = (project(hidden, qkv_weight) + triple_bias(vectors_f[0], vectors_f[1])).astype(
         jnp.bfloat16
     )
-    mixture = pair_attention(triple)
+    mixture, pairs = pair_attention(triple)
     branch = project(mixture, out_weight) + vectors_f[2]
     middle = residual + pieces[2] * branch
     stored_ffn, result = feed_forward(
         middle, pieces[3], pieces[4], pieces[5], expand, shrink, vectors_f, 10
     )
-    return (result, (hidden, triple, mixture, branch, middle, stored_ffn))
+    return (result, (hidden, pairs, mixture, branch, middle, stored_ffn))
 
 
 def spatial_backward(grad_out, residual, weights, frame_mod, stored):
     qkv_weight, out_weight, expand, shrink, vectors = weights
     pieces = block_pieces(as_float(vectors)[4:10], frame_mod)
-    hidden, triple, mixture, branch, middle, stored_ffn = stored
+    hidden, pairs, mixture, branch, middle, stored_ffn = stored
     middle_grad, ffn_table, ffn_grads = feed_backward(
         grad_out, middle, pieces[3], pieces[4], pieces[5], stored_ffn, expand, shrink
     )
     branch_grad, gate_grad = gated_back(middle_grad, pieces[2], branch)
-    out_weight_grad = weight_grad(mixture, branch_grad)
+    out_weight_grad = scatter_grad(mixture, branch_grad, False, True)
     out_bias = column_sum(branch_grad)
     mixture_grad = input_grad(branch_grad, out_weight).astype(jnp.bfloat16)
-    triple_grad = pair_attention_back(triple, mixture_grad)
-    qkv_grad = weight_grad(hidden, triple_grad)
+    triple_grad = pair_attention_back(pairs, mixture_grad)
+    qkv_grad = jnp.concatenate(
+        [
+            scatter_grad(hidden, triple_grad[..., : 3 * D // 2], False, True),
+            scatter_grad(hidden, triple_grad[..., 3 * D // 2 :], False, False),
+        ],
+        axis=1,
+    )
     query_bias, value_bias = triple_bias_grad(column_sum(triple_grad))
     hidden_grad = input_grad(triple_grad, qkv_weight)
     norm_value, norm_back = jax.vjp(modulate, residual, pieces[0], pieces[1])
@@ -368,7 +641,7 @@
         grad_out, crossed, pieces[3], pieces[4], pieces[5], stored_ffn, expand, shrink
     )
     cross_branch_grad = crossed_grad.astype(jnp.bfloat16)
-    cross_weight_grad = weight_grad(cross_mix, cross_branch_grad)
+    cross_weight_grad = scatter_grad(cross_mix, cross_branch_grad, False, True)
     cross_bias = column_sum(cross_branch_grad)
     mix_grad = input_grad(cross_branch_grad, cross_weight).astype(jnp.bfloat16)
     mix_grad = mix_grad.reshape(groups, frames, patches, HEADS, HEAD_DIM)
@@ -397,12 +670,12 @@
         "sfphr,sfphe->srhe", rounded, mix_grad, preferred_element_type=jnp.float32
     )
     keyval_grad = jnp.concatenate([key_grad, value_grad], axis=-1).reshape(groups, -1, 2 * D)
-    keyval_grad = lax.psum(keyval_grad, "sp").astype(jnp.bfloat16)
-    query_weight_grad = weight_grad(lowered, query_grad)
+    keyval_grad = lax.psum(keyval_grad.astype(jnp.bfloat16), "sp")
+    query_weight_grad = scatter_grad(lowered, query_grad, False, False)
     cross_query_bias = column_sum(query_grad)
     middle_grad = crossed_grad + input_grad(query_grad, query_weight)
     branch_grad, gate_grad = gated_back(middle_grad, pieces[2], branch)
-    out_weight_grad = weight_grad(mixture, branch_grad)
+    out_weight_grad = scatter_grad(mixture, branch_grad, False, True)
     out_bias = column_sum(branch_grad)
     mixture_grad = input_grad(branch_grad, out_weight).astype(jnp.bfloat16)
     mixture_grad = mixture_grad.reshape(groups, frames, patches, HEADS, HEAD_DIM)
@@ -439,7 +712,7 @@
     )
     triple_grad = jnp.concatenate([query_part, key_part, value_part], axis=-1).astype(jnp.bfloat16)
     triple_grad = triple_grad.reshape(groups, frames, patches, 3 * D)
-    qkv_grad = weight_grad(hidden, triple_grad)
+    qkv_grad = scatter_grad(hidden, triple_grad, False, False)
     query_bias, value_bias = triple_bias_grad(column_sum(triple_grad))
     hidden_grad = input_grad(triple_grad, qkv_weight)
     norm_value, norm_back = jax.vjp(modulate, residual, pieces[0], pieces[1])
@@ -501,12 +774,61 @@
     cotangent,
 ):
     groups, frames, patches = video.shape[:3]
-    spatial = (
-        lax.all_gather(spatial_qkv, "sp", axis=0, tiled=True),
-        lax.all_gather(spatial_out, "sp", axis=0, tiled=True),
-        lax.all_gather(spatial_expand, "sp", axis=0, tiled=True),
-        lax.all_gather(spatial_shrink, "sp", axis=0, tiled=True),
-        lax.all_gather(spatial_vectors, "sp", axis=1, tiled=True),
+    size = lax.axis_size("sp")
+    third = D
+    full_sqkv, full_sout = gather_columns(
+        [spatial_qkv, spatial_out],
+        [
+            ([(0, 0, third)], [(0, 2 * third, third)]),
+            ([(0, third, third)], [(1, 0, third)]),
+        ],
+        [False, True],
+        0,
+    )
+    (full_sexp,) = gather_columns(
+        [spatial_expand], [([(0, 0, FF // 2)], [(0, FF // 2, FF // 2)])], [False], 1
+    )
+    full_sshr = gather_tall(spatial_shrink, True, 2)
+    full_tqkv, full_tout = gather_columns(
+        [temporal_qkv, temporal_out],
+        [
+            (
+                [(0, 0, 2 * third)],
+                [(0, 2 * third, third), (1, 0, third)],
+            ),
+        ],
+        [False],
+        3,
+    )
+    full_cq, full_ckv, full_cout = gather_columns(
+        [cross_query, cross_keyval, cross_out],
+        [
+            (
+                [(0, 0, third), (1, 0, third)],
+                [(1, third, third), (2, 0, third)],
+            ),
+        ],
+        [True],
+        4,
+    )
+    (full_texp,) = gather_columns(
+        [temporal_expand], [([(0, 0, FF // 2)], [(0, FF // 2, FF // 2)])], [False], 5
+    )
+    full_tshr = gather_tall(temporal_shrink, True, 6)
+    all_vectors = lax.all_gather(
+        jnp.concatenate([spatial_vectors, temporal_vectors], axis=0), "sp", axis=1, tiled=True
+    )
+    n_spatial = spatial_vectors.shape[0]
+    spatial = (full_sqkv, full_sout, full_sexp, full_sshr, all_vectors[:n_spatial])
+    temporal = (
+        full_tqkv,
+        full_tout,
+        full_texp,
+        full_tshr,
+        full_cq,
+        full_ckv,
+        full_cout,
+        all_vectors[n_spatial:],
     )
     dropped = (drop_mask > 0).astype(jnp.float32)
     text_local = jnp.where(drop_mask[:, :, None, None] > 0, null_caption[None, None], captions)
@@ -518,31 +840,11 @@
     allowed = (segment_ids[:, :, None] == row_clip[None, None, :])[:, :, None, None, :]
     residual = video.astype(jnp.float32)
     middle, spatial_kept = spatial_forward(residual, spatial, frame_mod)
-    temporal = (
-        lax.all_gather(temporal_qkv, "sp", axis=0, tiled=True),
-        lax.all_gather(temporal_out, "sp", axis=0, tiled=True),
-        lax.all_gather(temporal_expand, "sp", axis=0, tiled=True),
-        lax.all_gather(temporal_shrink, "sp", axis=0, tiled=True),
-        lax.all_gather(cross_query, "sp", axis=0, tiled=True),
-        lax.all_gather(cross_keyval, "sp", axis=0, tiled=True),
-        lax.all_gather(cross_out, "sp", axis=0, tiled=True),
-        lax.all_gather(temporal_vectors, "sp", axis=1, tiled=True),
-    )
     context = (caption_sum + as_float(temporal[7])[7]).astype(jnp.bfloat16)
     result, temporal_kept = temporal_forward(
         middle, temporal, frame_mod, same_clip, allowed, context
     )
     output = result.astype(jnp.bfloat16)
-    temporal = (
-        lax.all_gather(temporal_qkv, "sp", axis=0, tiled=True),
-        lax.all_gather(temporal_out, "sp", axis=0, tiled=True),
-        lax.all_gather(temporal_expand, "sp", axis=0, tiled=True),
-        lax.all_gather(temporal_shrink, "sp", axis=0, tiled=True),
-        lax.all_gather(cross_query, "sp", axis=0, tiled=True),
-        lax.all_gather(cross_keyval, "sp", axis=0, tiled=True),
-        lax.all_gather(cross_out, "sp", axis=0, tiled=True),
-        lax.all_gather(temporal_vectors, "sp", axis=1, tiled=True),
-    )
     middle_grad, temporal_terms, keyval_grad = temporal_backward(
         cotangent.astype(jnp.float32),
         middle,
@@ -562,154 +864,37 @@
     caption_weight_grad = weight_grad(text_rows, context_grad)
     text_grad = input_grad(context_grad, caption_weight).reshape(groups, CLIPS, CAP, -1)
     null_grad = jnp.sum(text_grad * dropped[:, :, None, None], axis=(0, 1))
-    temporal_shards = (
-        lax.psum_scatter(temporal_terms[0], "sp", scatter_dimension=0, tiled=True),
-        lax.psum_scatter(temporal_terms[1], "sp", scatter_dimension=0, tiled=True),
-        lax.psum_scatter(temporal_terms[2], "sp", scatter_dimension=0, tiled=True),
-        lax.psum_scatter(temporal_terms[3], "sp", scatter_dimension=0, tiled=True),
-        lax.psum_scatter(temporal_terms[4], "sp", scatter_dimension=0, tiled=True),
-        lax.psum_scatter(temporal_terms[5], "sp", scatter_dimension=0, tiled=True),
-        lax.psum_scatter(temporal_terms[6], "sp", scatter_dimension=1, tiled=True),
-    )
-    vector_fix = jnp.zeros((18, shard_rows), jnp.float32)
-    vector_fix = vector_fix.at[5].set(
-        lax.dynamic_slice_in_dim(value_bias_full, first_row, shard_rows, 0)
-    )
-    vector_fix = vector_fix.at[7].set(
-        lax.dynamic_slice_in_dim(caption_bias_full, first_row, shard_rows, 0)
-    )
-    spatial = (
-        lax.all_gather(spatial_qkv, "sp", axis=0, tiled=True),
-        lax.all_gather(spatial_out, "sp", axis=0, tiled=True),
-        lax.all_gather(spatial_expand, "sp", axis=0, tiled=True),
-        lax.all_gather(spatial_shrink, "sp", axis=0, tiled=True),
-        lax.all_gather(spatial_vectors, "sp", axis=1, tiled=True),
-    )
     video_grad, spatial_terms = spatial_backward(
         middle_grad, residual, spatial, frame_mod, spatial_kept
     )
-    spatial_shards = (
-        lax.psum_scatter(spatial_terms[0], "sp", scatter_dimension=0, tiled=True),
-        lax.psum_scatter(spatial_terms[1], "sp", scatter_dimension=0, tiled=True),
-        lax.psum_scatter(spatial_terms[2], "sp", scatter_dimension=0, tiled=True),
-        lax.psum_scatter(spatial_terms[3], "sp", scatter_dimension=0, tiled=True),
-        lax.psum_scatter(spatial_terms[4], "sp", scatter_dimension=1, tiled=True),
-    )
-    halves = (
-        lax.psum_scatter(
-            null_grad.astype(jnp.bfloat16), "seq", scatter_dimension=0, tiled=True
-        ).astype(jnp.float32),
-        lax.psum_scatter(
-            caption_weight_grad.astype(jnp.bfloat16), "seq", scatter_dimension=1, tiled=True
-        ).astype(jnp.float32),
-        lax.psum_scatter(
-            spatial_shards[0].astype(jnp.bfloat16), "seq", scatter_dimension=1, tiled=True
-        ).astype(jnp.float32),
-        lax.psum_scatter(
-            spatial_shards[1].astype(jnp.bfloat16), "seq", scatter_dimension=1, tiled=True
-        ).astype(jnp.float32),
-        lax.psum_scatter(
-            spatial_shards[2].astype(jnp.bfloat16), "seq", scatter_dimension=1, tiled=True
-        ).astype(jnp.float32),
-        lax.psum_scatter(
-            spatial_shards[3].astype(jnp.bfloat16), "seq", scatter_dimension=1, tiled=True
-        ).astype(jnp.float32),
-        lax.psum_scatter(
-            spatial_shards[4].astype(jnp.bfloat16), "seq", scatter_dimension=0, tiled=True
-        ).astype(jnp.float32),
-        lax.psum_scatter(
-            temporal_shards[0].astype(jnp.bfloat16), "seq", scatter_dimension=1, tiled=True
-        ).astype(jnp.float32),
-        lax.psum_scatter(
-            temporal_shards[1].astype(jnp.bfloat16), "seq", scatter_dimension=1, tiled=True
-        ).astype(jnp.float32),
-        lax.psum_scatter(
-            temporal_shards[2].astype(jnp.bfloat16), "seq", scatter_dimension=1, tiled=True
-        ).astype(jnp.float32),
-        lax.psum_scatter(
-            temporal_shards[3].astype(jnp.bfloat16), "seq", scatter_dimension=1, tiled=True
-        ).astype(jnp.float32),
-        lax.psum_scatter(
-            temporal_shards[4].astype(jnp.bfloat16), "seq", scatter_dimension=1, tiled=True
-        ).astype(jnp.float32),
-        lax.psum_scatter(
-            keyval_weight_grad.astype(jnp.bfloat16), "seq", scatter_dimension=1, tiled=True
-        ).astype(jnp.float32),
-        lax.psum_scatter(
-            temporal_shards[5].astype(jnp.bfloat16), "seq", scatter_dimension=1, tiled=True
-        ).astype(jnp.float32),
-        lax.psum_scatter(
-            (temporal_shards[6] + vector_fix).astype(jnp.bfloat16),
-            "seq",
-            scatter_dimension=0,
-            tiled=True,
-        ).astype(jnp.float32),
-    )
-    totals = (
-        lax.all_gather(halves[0].astype(jnp.bfloat16), "seq", axis=0, tiled=True).astype(
-            jnp.float32
-        ),
-        lax.all_gather(halves[1].astype(jnp.bfloat16), "seq", axis=1, tiled=True).astype(
-            jnp.float32
-        ),
-        lax.all_gather(halves[2].astype(jnp.bfloat16), "seq", axis=1, tiled=True).astype(
-            jnp.float32
-        ),
-        lax.all_gather(halves[3].astype(jnp.bfloat16), "seq", axis=1, tiled=True).astype(
-            jnp.float32
-        ),
-        lax.all_gather(halves[4].astype(jnp.bfloat16), "seq", axis=1, tiled=True).astype(
-            jnp.float32
-        ),
-        lax.all_gather(halves[5].astype(jnp.bfloat16), "seq", axis=1, tiled=True).astype(
-            jnp.float32
-        ),
-        lax.all_gather(halves[6].astype(jnp.bfloat16), "seq", axis=0, tiled=True).astype(
-            jnp.float32
-        ),
-        lax.all_gather(halves[7].astype(jnp.bfloat16), "seq", axis=1, tiled=True).astype(
-            jnp.float32
-        ),
-        lax.all_gather(halves[8].astype(jnp.bfloat16), "seq", axis=1, tiled=True).astype(
-            jnp.float32
-        ),
-        lax.all_gather(halves[9].astype(jnp.bfloat16), "seq", axis=1, tiled=True).astype(
-            jnp.float32
-        ),
-        lax.all_gather(halves[10].astype(jnp.bfloat16), "seq", axis=1, tiled=True).astype(
-            jnp.float32
-        ),
-        lax.all_gather(halves[11].astype(jnp.bfloat16), "seq", axis=1, tiled=True).astype(
-            jnp.float32
-        ),
-        lax.all_gather(halves[12].astype(jnp.bfloat16), "seq", axis=1, tiled=True).astype(
-            jnp.float32
-        ),
-        lax.all_gather(halves[13].astype(jnp.bfloat16), "seq", axis=1, tiled=True).astype(
-            jnp.float32
-        ),
-        lax.all_gather(halves[14].astype(jnp.bfloat16), "seq", axis=0, tiled=True).astype(
-            jnp.float32
-        ),
-    )
+    vector_fix = jnp.zeros((18, D), jnp.float32)
+    vector_fix = vector_fix.at[5].set(value_bias_full)
+    vector_fix = vector_fix.at[7].set(caption_bias_full)
+    vector_terms = lax.psum(
+        jnp.concatenate([spatial_terms[4], temporal_terms[6]], axis=0), "sp"
+    )
+    vector_terms = vector_terms + jnp.concatenate(
+        [jnp.zeros((n_spatial, D), jnp.float32), vector_fix], axis=0
+    )
+    vector_total = sum_seq(lax.dynamic_slice_in_dim(vector_terms, first_row, shard_rows, 1))
     return (
         output,
         video_grad.astype(jnp.bfloat16),
-        totals[0],
-        totals[1],
-        totals[2],
-        totals[3],
-        totals[4],
-        totals[5],
-        totals[6],
-        totals[7],
-        totals[8],
-        totals[9],
-        totals[10],
-        totals[11],
-        totals[12],
-        totals[13],
-        totals[14],
+        sum_seq(null_grad),
+        sum_seq(caption_weight_grad),
+        spatial_terms[0],
+        spatial_terms[1],
+        spatial_terms[2],
+        spatial_terms[3],
+        vector_total[:n_spatial],
+        temporal_terms[0],
+        temporal_terms[1],
+        temporal_terms[2],
+        temporal_terms[3],
+        temporal_terms[4],
+        sum_seq(keyval_weight_grad),
+        temporal_terms[5],
+        vector_total[n_spatial:],
     )
 
 

time: 2940 us -> 1870 us (0.64)
  waiting for transfers between devices: 1920 us -> 830 us
  blocking collectives: 412 us -> 40 us
  starting transfers between devices: 26.8 us -> 180 us
  other arithmetic: 61 us -> 189 us
  local copies, waits for them, and re-layouts: 209 us -> 317 us
  Pallas kernels: 0 us -> 72.3 us
  matrix products: 276 us -> 217 us
    reduce_scatter x7 -> x0, waiting for transfers between devices: 828 us -> none  [the longest x1 212 us: on_device(): lax.psum_scatter(spatial_terms[3], 'sp', scatter_dimension=0, tiled=True)]
    ppermute x0 -> x113, waiting for transfers between devices: none -> 753 us  [the longest x79 544 us: swap_sp(): return lax.ppermute(values, 'sp', [(i, i ^ 1 << bit) for i in range(size)])]
    all_gather x11 -> x0, waiting for transfers between devices: 571 us -> none  [the longest x1 85.3 us: on_device(): lax.all_gather(spatial_expand, 'sp', axis=0, tiled=True)]
    unnamed x53 -> x3, waiting for transfers between devices: 455 us -> 0.05 us
    ppermute x0 -> x113, starting transfers between devices: none -> 160 us  [the longest x79 128 us: swap_sp(): return lax.ppermute(values, 'sp', [(i, i ^ 1 << bit) for i in range(size)])]
    psum x1 -> x0, blocking collectives: 126 us -> none  [temporal_backward(): keyval_grad = lax.psum(keyval_grad, 'sp').astype(jnp.bfloat16)]
    all_gather x17 -> x1, blocking collectives: 160 us -> 40 us  [on_device(): lax.all_gather(jnp.concatenate([spatial_vectors, temporal_vectors], axis=...]
    all_to_all x2 -> x0, blocking collectives: 113 us -> none  [the longest x1 77 us: pair_backward(): lax.all_to_all(gradients, 'sp', split_axis=2, concat_axis=0, tiled=True)]
  transfers between devices with their start and end apart: 39 -> 120, of which waited for: 32 -> 63; matrix products, arithmetic and copies ran while one was open for 14% -> 20% of each run, Pallas kernels for 0% -> 4%
where the time goes in v1:
time: 1870 us; the launch traced here: 1860 us
  waiting for transfers between devices  830 us (44%)
  local copies, waits for them, and re-layouts  317 us (17%)
  matrix products  217 us (12%)
  other arithmetic  189 us (10%)
  starting transfers between devices  180 us (10%)
  Pallas kernels  72.3 us (4%)
  blocking collectives  40 us (2%)
    ppermute x79, waiting for transfers between devices, swap_sp(): return lax.ppermute(values, 'sp', [(i, i ^ 1 << bit) for i in range(size)])  544 us
    ppermute x34, waiting for transfers between devices, swap_seq(): return lax.ppermute(values, 'seq', [(0, 1), (1, 0)])  208 us
    ppermute x79, starting transfers between devices, swap_sp(): return lax.ppermute(values, 'sp', [(i, i ^ 1 << bit) for i in range(size)])  128 us
    psum x1, waiting for transfers between devices, on_device(): lax.psum(jnp.concatenate([spatial_terms[4], temporal_terms[6]], axis=0),...  77.5 us
    pallas_call x7, Pallas kernels, place_blocks(): pl.pallas_call(functools.partial(place_kernel, bits, moves, len(arrays),...  72.3 us
    dot_general x12, matrix products, project(): return jnp.dot(inputs, weight, preferred_element_type=jnp.float32)  68.1 us
    select_n x20, local copies, waits for them, and re-layouts, pick_core(): return jnp.where(which == 0, grouped[:, :, 0], grouped[:, :, 1])  68 us
    unnamed x579, local copies, waits for them, and re-layouts  58.9 us
  transfers between devices with their start and end apart: 120, of which 63 were waited for; matrix products, arithmetic and copies ran while one was open for 20% of the time, Pallas kernels for 4%

profile of v1, /device:TPU:0, one launch (start us, length us, event | category | flops | bytes accessed | tf_op | source)
XLA Modules:
  0.0 1863.8 jit_solution(4378523231854261395)
XLA Ops:
  24.3 40.0 %all-gather = bf16[16,72,32]{1,2,0:T(8,128)(2,1)S(1)} all-gather(bf16[1,72,32]{1,2,0:T(8,128)(2,1)S(1)} %maximum_bitcast_fusion), channel_id=1, replica_groups=mesh['seq'=2,'sp'=16] {'sp'}, dimensions={0}, use_global_device_ids=true | all-gather | bytes 78336 | tf_op jit(solution)/shard_map/all_gather | solution.py:818
  107.4 35.4 %collective-permute-start.13 = (bf16[1,144,1152]{2,1,0:T(8,128)(2,1)S(1)}, bf16[1,144,1152]{2,1,0:T(8,128)(2,1)S(1)}, u32[]{:S(2)}, u32[]{:S(2)}) collective-permute-start(bf16[1,144,1152]{2,1,0:T(8,128)(2,1)S(1)} %select_bitcast_fusion.10), channel_id=1, source_target_pairs={{0,8},{1,9},{2,10},{3,11},{4,12},{5,13},{6,14},{7,15},{8,0},{9,1},... | collective-permute-start | bytes 995336 | tf_op jit(solution)/shard_map/ppermute | solution.py:80
  148.9 30.9 %collective-permute-done.18 = bf16[1,72,2304]{2,1,0:T(8,128)(2,1)S(1)} collective-permute-done((bf16[1,72,2304]{2,1,0:T(8,128)(2,1)S(1)}, bf16[1,72,2304]{2,1,0:T(8,128)(2,1)S(1)}, u32[]{:S(2)}, u32[]{:S(2)}) %collective-permute-start.18) | collective-permute-done | bytes 331808 | tf_op jit(solution)/shard_map/ppermute | solution.py:80
  201.9 13.1 collective-permute-done.23
  217.4 40.2 %collective-permute-done.19 = bf16[2,72,2304]{2,1,0:T(8,128)(2,1)S(1)} collective-permute-done((bf16[2,72,2304]{2,1,0:T(8,128)(2,1)S(1)}, bf16[2,72,2304]{2,1,0:T(8,128)(2,1)S(1)}, u32[]{:S(2)}, u32[]{:S(2)}) %collective-permute-start.19) | collective-permute-done | bytes 663584 | tf_op jit(solution)/shard_map/ppermute | solution.py:80
  296.0 66.8 %collective-permute-done.8 = bf16[4,72,1152]{2,1,0:T(8,128)(2,1)S(1)} collective-permute-done((bf16[4,72,1152]{2,1,0:T(8,128)(2,1)S(1)}, bf16[4,72,1152]{2,1,0:T(8,128)(2,1)S(1)}, u32[]{:S(2)}, u32[]{:S(2)}) %collective-permute-start.8) | collective-permute-done | bytes 663584 | tf_op jit(solution)/shard_map/ppermute | solution.py:80
  411.0 29.5 %collective-permute-done.15 = bf16[4,144,1152]{2,1,0:T(8,128)(2,1)} collective-permute-done((bf16[4,144,1152]{2,1,0:T(8,128)(2,1)}, bf16[4,144,1152]{2,1,0:T(8,128)(2,1)}, u32[]{:S(2)}, u32[]{:S(2)}) %collective-permute-start.15) | collective-permute-done | bytes 1327136 | tf_op jit(solution)/shard_map/ppermute | solution.py:80
  444.9 29.4 %collective-permute-done.11 = bf16[4,72,2304]{2,1,0:T(8,128)(2,1)S(1)} collective-permute-done((bf16[4,72,2304]{2,1,0:T(8,128)(2,1)}, bf16[4,72,2304]{2,1,0:T(8,128)(2,1)S(1)}, u32[]{:S(2)}, u32[]{:S(2)}) %collective-permute-start.11) | collective-permute-done | bytes 1327136 | tf_op jit(solution)/shard_map/ppermute | solution.py:80
  477.7 25.1 %collective-permute-done.24 = bf16[4,72,2304]{2,1,0:T(8,128)(2,1)S(1)} collective-permute-done((bf16[4,72,2304]{2,1,0:T(8,128)(2,1)}, bf16[4,72,2304]{2,1,0:T(8,128)(2,1)S(1)}, u32[]{:S(2)}, u32[]{:S(2)}) %collective-permute-start.24) | collective-permute-done | bytes 1327136 | tf_op jit(solution)/shard_map/ppermute | solution.py:80
  507.7 23.6 %collective-permute-done.26 = bf16[4,72,2304]{2,1,0:T(8,128)(2,1)S(1)} collective-permute-done((bf16[4,72,2304]{2,1,0:T(8,128)(2,1)}, bf16[4,72,2304]{2,1,0:T(8,128)(2,1)S(1)}, u32[]{:S(2)}, u32[]{:S(2)}) %collective-permute-start.26) | collective-permute-done | bytes 1327136 | tf_op jit(solution)/shard_map/ppermute | solution.py:80
  579.0 16.5 collective-permute-done.17
  626.4 16.3 collective-permute-done.30.refs_1_
  642.7 11.7 shard_map.337
  658.4 11.7 shard_map.333
  674.2 11.1 shard_map.335
  700.4 10.4 multiply_convert_fusion.1
  936.0 10.6 broadcast_select_fusion.1
  1174.3 12.2 collective-permute-done.101
  1216.6 12.6 collective-permute-done.108
  1245.0 13.2 collective-permute-done.52
  1370.1 77.5 %all-reduce.25.cloned.1.call-done = f32[32,1152]{1,0:T(8,128)} async-done(((f32[32,1152]{1,0:T(8,128)}), f32[32,1152]{1,0:T(8,128)}) %all-reduce.25.cloned.1.call-update) | async-done | bytes 147472 | tf_op jit(solution)/shard_map/psum | solution.py:873
  1469.8 45.6 %collective-permute-done.66 = bf16[8,144,1152]{2,1,0:T(8,128)(2,1)} collective-permute-done((bf16[8,144,1152]{2,1,0:T(8,128)(2,1)}, bf16[8,144,1152]{2,1,0:T(8,128)(2,1)}, u32[]{:S(2)}, u32[]{:S(2)}) %collective-permute-start.66) | collective-permute-done | bytes 2654240 | tf_op jit(solution)/shard_map/ppermute | solution.py:84
  1525.0 47.3 %collective-permute-done.94 = bf16[8,144,1152]{2,1,0:T(8,128)(2,1)} collective-permute-done((bf16[8,144,1152]{2,1,0:T(8,128)(2,1)S(1)}, bf16[8,144,1152]{2,1,0:T(8,128)(2,1)}, u32[]{:S(2)}, u32[]{:S(2)}) %collective-permute-start.94) | collective-permute-done | bytes 2654240 | tf_op jit(solution)/shard_map/ppermute | solution.py:84
  1579.0 15.0 collective-permute-done.75
  1615.3 17.7 collective-permute-done.59
  1636.8 24.6 %collective-permute-done.67 = bf16[4,144,1152]{2,1,0:T(8,128)(2,1)S(1)} collective-permute-done((bf16[4,144,1152]{2,1,0:T(8,128)(2,1)}, bf16[4,144,1152]{2,1,0:T(8,128)(2,1)S(1)}, u32[]{:S(2)}, u32[]{:S(2)}) %collective-permute-start.67) | collective-permute-done | bytes 1327136 | tf_op jit(solution)/shard_map/ppermute | solution.py:80
  1665.8 24.0 %collective-permute-done.95 = bf16[4,144,1152]{2,1,0:T(8,128)(2,1)S(1)} collective-permute-done((bf16[4,144,1152]{2,1,0:T(8,128)(2,1)}, bf16[4,144,1152]{2,1,0:T(8,128)(2,1)S(1)}, u32[]{:S(2)}, u32[]{:S(2)}) %collective-permute-start.95) | collective-permute-done | bytes 1327136 | tf_op jit(solution)/shard_map/ppermute | solution.py:80
  1732.0 11.1 collective-permute-done.97
  1754.3 14.6 collective-permute-done.58
  1769.4 12.2 collective-permute-done.60
  1787.7 21.3 %collective-permute-done.41 = bf16[2,72,896]{2,1,0:T(8,128)(2,1)S(1)} collective-permute-done((bf16[2,72,896]{2,1,0:T(8,128)(2,1)S(1)}, bf16[2,72,896]{2,1,0:T(8,128)(2,1)S(1)}, u32[]{:S(2)}, u32[]{:S(2)}) %collective-permute-start.41) | collective-permute-done | bytes 258080 | tf_op jit(solution)/shard_map/ppermute | solution.py:80
  1812.0 12.4 collective-permute-done.42
  (1212 shorter events, 1061.9 us)
Async XLA Ops:
  7.2 390.9 %all-reduce.21.cloned.1.call-start = ((), (), s32[]{:S(2)}) async-start(), calls=%async_computation.4 | async-start | bytes 4423680 | tf_op jit(solution)/shard_map/psum | solution.py:836
  9.2 134.6 %collective-permute-start.4 = (bf16[1,72,1152]{2,1,0:T(8,128)(2,1)S(1)}, bf16[1,72,1152]{2,1,0:T(8,128)(2,1)}, u32[]{:S(2)}, u32[]{:S(2)}) collective-permute-start(bf16[1,72,1152]{2,1,0:T(8,128)(2,1)S(1)} %get-tuple-element.255), channel_id=1, source_target_pairs={{0,8},{1,9},{2,10},{3,11},{4,12},{5,13},{6,14},{7,15},{8,0},{9,1},... | collective-permute-start | bytes 497672 | tf_op jit(solution)/shard_map/ppermute | solution.py:80
  15.5 164.5 %collective-permute-start.22 = (bf16[1,72,2304]{2,1,0:T(8,128)(2,1)S(1)}, bf16[1,72,2304]{2,1,0:T(8,128)(2,1)}, u32[]{:S(2)}, u32[]{:S(2)}) collective-permute-start(bf16[1,72,2304]{2,1,0:T(8,128)(2,1)S(1)} %maximum_select_fusion.6), channel_id=1, source_target_pairs={{0,8},{1,9},{2,10},{3,11},{4,12},{5,13},{6,14},{7,15},{8,0},{9,1},... | collective-permute-start | bytes 995336 | tf_op jit(solution)/shard_map/ppermute | solution.py:80
  18.5 126.4 %collective-permute-start.31 = (bf16[1,144,1152]{2,1,0:T(8,128)(2,1)S(1)}, bf16[1,144,1152]{2,1,0:T(8,128)(2,1)}, u32[]{:S(2)}, u32[]{:S(2)}) collective-permute-start(bf16[1,144,1152]{2,1,0:T(8,128)(2,1)S(1)} %select_bitcast_fusion.8), channel_id=1, source_target_pairs={{0,8},{1,9},{2,10},{3,11},{4,12},{5,13},{6,14},{7,15},{8,0},{9,1},... | collective-permute-start | bytes 995336 | tf_op jit(solution)/shard_map/ppermute | solution.py:80
  18.6 168.0 %collective-permute-start.27 = (bf16[1,72,2304]{2,1,0:T(8,128)(2,1)S(1)}, bf16[1,72,2304]{2,1,0:T(8,128)(2,1)}, u32[]{:S(2)}, u32[]{:S(2)}) collective-permute-start(bf16[1,72,2304]{2,1,0:T(8,128)(2,1)S(1)} %select_bitcast_fusion.9), channel_id=1, source_target_pairs={{0,8},{1,9},{2,10},{3,11},{4,12},{5,13},{6,14},{7,15},{8,0},{9,1},... | collective-permute-start | bytes 995336 | tf_op jit(solution)/shard_map/ppermute | solution.py:80
  281.3 119.6 %collective-permute-start.29 = (bf16[4,72,2304]{2,1,0:T(8,128)(2,1)}, bf16[4,72,2304]{2,1,0:T(8,128)(2,1)}, u32[]{:S(2)}, u32[]{:S(2)}) collective-permute-start(bf16[4,72,2304]{2,1,0:T(8,128)(2,1)} %pad_maximum_fusion.24), channel_id=1, source_target_pairs={{0,2},{1,3},{2,0},{3,1},{4,6},{5,7},{6,4},{7,5},{8,10},{9,11},{10,... | collective-permute-start | bytes 3981320 | tf_op jit(solution)/shard_map/ppermute | solution.py:80
  286.0 122.9 %collective-permute-start.20 = (bf16[4,72,2304]{2,1,0:T(8,128)(2,1)}, bf16[4,72,2304]{2,1,0:T(8,128)(2,1)}, u32[]{:S(2)}, u32[]{:S(2)}) collective-permute-start(bf16[4,72,2304]{2,1,0:T(8,128)(2,1)} %pad_maximum_fusion.22), channel_id=1, source_target_pairs={{0,2},{1,3},{2,0},{3,1},{4,6},{5,7},{6,4},{7,5},{8,10},{9,11},{10,... | collective-permute-start | bytes 3981320 | tf_op jit(solution)/shard_map/ppermute | solution.py:80
  293.3 117.2 %collective-permute-start.25 = (bf16[4,72,2304]{2,1,0:T(8,128)(2,1)}, bf16[4,72,2304]{2,1,0:T(8,128)(2,1)}, u32[]{:S(2)}, u32[]{:S(2)}) collective-permute-start(bf16[4,72,2304]{2,1,0:T(8,128)(2,1)} %pad_maximum_fusion.23), channel_id=1, source_target_pairs={{0,16},{16,0},{1,17},{17,1},{2,18},{18,2},{3,19},{19,3},{4,20},{20... | collective-permute-start | bytes 3981320 | tf_op jit(solution)/shard_map/ppermute | solution.py:84
  393.1 156.2 %all-to-all-start = ((bf16[16,32,8,216]{3,2,1,0:T(8,128)(2,1)}), bf16[16,32,8,216]{3,2,1,0:T(8,128)(2,1)}, u32[]{:S(2)}, u32[]{:S(2)}) async-start(bf16[16,32,8,216]{3,2,1,0:T(8,128)(2,1)} %bitcast.11), calls=%async_computation | async-start | bytes 4194304 | tf_op jit(solution)/shard_map/all_to_all | solution.py:438
  405.7 97.2 %collective-permute-start.24 = (bf16[4,72,2304]{2,1,0:T(8,128)(2,1)}, bf16[4,72,2304]{2,1,0:T(8,128)(2,1)S(1)}, u32[]{:S(2)}, u32[]{:S(2)}) collective-permute-start(bf16[4,72,2304]{2,1,0:T(8,128)(2,1)} %pad_maximum_fusion.23), channel_id=1, source_target_pairs={{0,2},{1,3},{2,0},{3,1},{4,6},{5,7},{6,4},{7,5},{8,10},{9,11},{10,... | collective-permute-start | bytes 3981320 | tf_op jit(solution)/shard_map/ppermute | solution.py:80
  474.4 199.8 %collective-permute-start.21 = (bf16[8,72,2304]{2,1,0:T(8,128)(2,1)S(1)}, bf16[8,72,2304]{2,1,0:T(8,128)(2,1)}, u32[]{:S(2)}, u32[]{:S(2)}) collective-permute-start(bf16[8,72,2304]{2,1,0:T(8,128)(2,1)S(1)} %pad_maximum_fusion.3.refs_0_), channel_id=1, source_target_pairs={{0,16},{16,0},{1,17},{17,1},{2,18},{18,2},{3,19},{19,3},{4,20},{20... | collective-permute-start | bytes 7962632 | tf_op jit(solution)/shard_map/ppermute | solution.py:84
  502.8 155.6 %collective-permute-start.12 = (bf16[8,72,2304]{2,1,0:T(8,128)(2,1)}, bf16[8,72,2304]{2,1,0:T(8,128)(2,1)}, u32[]{:S(2)}, u32[]{:S(2)}) collective-permute-start(bf16[8,72,2304]{2,1,0:T(8,128)(2,1)} %pad_maximum_fusion.refs_0_), channel_id=1, source_target_pairs={{0,16},{16,0},{1,17},{17,1},{2,18},{18,2},{3,19},{19,3},{4,20},{20... | collective-permute-start | bytes 7962632 | tf_op jit(solution)/shard_map/ppermute | solution.py:84
  505.7 137.0 %collective-permute-start.30 = (bf16[8,72,2304]{2,1,0:T(8,128)(2,1)}, bf16[8,72,2304]{2,1,0:T(8,128)(2,1)}, u32[]{:S(2)}, u32[]{:S(2)}) collective-permute-start(bf16[8,72,2304]{2,1,0:T(8,128)(2,1)} %pad_maximum_fusion.6.refs_0_), channel_id=1, source_target_pairs={{0,16},{16,0},{1,17},{17,1},{2,18},{18,2},{3,19},{19,3},{4,20},{20... | collective-permute-start | bytes 7962632 | tf_op jit(solution)/shard_map/ppermute | solution.py:84
  506.2 104.5 %collective-permute-start.35 = (bf16[4,144,1152]{2,1,0:T(8,128)(2,1)}, bf16[4,144,1152]{2,1,0:T(8,128)(2,1)}, u32[]{:S(2)}, u32[]{:S(2)}) collective-permute-start(bf16[4,144,1152]{2,1,0:T(8,128)(2,1)} %collective-permute-done.34), channel_id=1, source_target_pairs={{0,2},{1,3},{2,0},{3,1},{4,6},{5,7},{6,4},{7,5},{8,10},{9,11},{10,... | collective-permute-start | bytes 3981320 | tf_op jit(solution)/shard_map/ppermute | solution.py:80
  563.1 126.8 %all-to-all-start.1 = ((bf16[1,32,128,72]{3,1,0,2:T(8,128)(2,1)}), bf16[1,32,128,72]{3,1,0,2:T(8,128)(2,1)}, u32[]{:S(2)}, u32[]{:S(2)}) async-start(bf16[1,32,128,72]{3,1,0,2:T(8,128)(2,1)} %copy.707), calls=%async_computation.1 | async-start | bytes 2097152 | tf_op jit(solution)/shard_map/all_to_all | solution.py:404
  567.5 559.7 %all-reduce.23.cloned.1.call-start = ((), (), s32[]{:S(2)}) async-start(), calls=%async_computation.5 | async-start | bytes 4423680 | tf_op jit(solution)/shard_map/psum | solution.py:673
  987.0 202.1 %collective-permute-start.107 = (bf16[8,72,1280]{2,1,0:T(8,128)(2,1)}, bf16[8,72,1280]{2,1,0:T(8,128)(2,1)}, u32[]{:S(2)}, u32[]{:S(2)}) collective-permute-start(bf16[8,72,1280]{2,1,0:T(8,128)(2,1)} %bitcast.321), channel_id=1, source_target_pairs={{0,1},{1,0},{2,3},{3,2},{4,5},{5,4},{6,7},{7,6},{8,9},{9,8},{10,11... | collective-permute-start | bytes 4423688 | tf_op jit(solution)/shard_map/ppermute | solution.py:80
  1026.9 134.3 %collective-permute-start.99 = (bf16[8,72,1280]{2,1,0:T(8,128)(2,1)}, bf16[8,72,1280]{2,1,0:T(8,128)(2,1)}, u32[]{:S(2)}, u32[]{:S(2)}) collective-permute-start(bf16[8,72,1280]{2,1,0:T(8,128)(2,1)} %bitcast.300), channel_id=1, source_target_pairs={{0,1},{1,0},{2,3},{3,2},{4,5},{5,4},{6,7},{7,6},{8,9},{9,8},{10,11... | collective-permute-start | bytes 4423688 | tf_op jit(solution)/shard_map/ppermute | solution.py:80
  1027.3 163.9 %collective-permute-start.79 = (bf16[8,72,1280]{2,1,0:T(8,128)(2,1)}, bf16[8,72,1280]{2,1,0:T(8,128)(2,1)}, u32[]{:S(2)}, u32[]{:S(2)}) collective-permute-start(bf16[8,72,1280]{2,1,0:T(8,128)(2,1)} %bitcast.245), channel_id=1, source_target_pairs={{0,1},{1,0},{2,3},{3,2},{4,5},{5,4},{6,7},{7,6},{8,9},{9,8},{10,11... | collective-permute-start | bytes 4423688 | tf_op jit(solution)/shard_map/ppermute | solution.py:80
  1073.8 128.0 %collective-permute-start.51 = (bf16[8,72,1280]{2,1,0:T(8,128)(2,1)}, bf16[8,72,1280]{2,1,0:T(8,128)(2,1)}, u32[]{:S(2)}, u32[]{:S(2)}) collective-permute-start(bf16[8,72,1280]{2,1,0:T(8,128)(2,1)} %bitcast.169), channel_id=1, source_target_pairs={{0,1},{1,0},{2,3},{3,2},{4,5},{5,4},{6,7},{7,6},{8,9},{9,8},{10,11... | collective-permute-start | bytes 4423688 | tf_op jit(solution)/shard_map/ppermute | solution.py:80
  1145.8 193.3 %all-to-all-start.3 = ((bf16[1,32,128,216]{3,1,0,2:T(8,128)(2,1)}), bf16[1,32,128,216]{3,1,0,2:T(8,128)(2,1)}, u32[]{:S(2)}, u32[]{:S(2)}) async-start(bf16[1,32,128,216]{3,1,0,2:T(8,128)(2,1)} %copy.734), calls=%async_computation.3 | async-start | bytes 4194304 | tf_op jit(solution)/shard_map/all_to_all | solution.py:432
  1151.7 296.0 %all-reduce.25.cloned.1.call-start = ((), (), s32[]{:S(2)}) async-start(), calls=%async_computation.6 | async-start | bytes 294912 | tf_op jit(solution)/shard_map/psum | solution.py:873
  1159.3 118.3 %collective-permute-start.65 = (bf16[8,144,1152]{2,1,0:T(8,128)(2,1)}, bf16[8,144,1152]{2,1,0:T(8,128)(2,1)S(1)}, u32[]{:S(2)}, u32[]{:S(2)}) collective-permute-start(bf16[8,144,1152]{2,1,0:T(8,128)(2,1)} %bitcast.950), channel_id=1, source_target_pairs={{0,1},{1,0},{2,3},{3,2},{4,5},{5,4},{6,7},{7,6},{8,9},{9,8},{10,11... | collective-permute-start | bytes 7962632 | tf_op jit(solution)/shard_map/ppermute | solution.py:80
  1273.6 195.3 %collective-permute-start.64 = (bf16[8,144,1152]{2,1,0:T(8,128)(2,1)}, bf16[8,144,1152]{2,1,0:T(8,128)(2,1)}, u32[]{:S(2)}, u32[]{:S(2)}) collective-permute-start(bf16[8,144,1152]{2,1,0:T(8,128)(2,1)} %bitcast.208), channel_id=1, source_target_pairs={{0,1},{1,0},{2,3},{3,2},{4,5},{5,4},{6,7},{7,6},{8,9},{9,8},{10,11... | collective-permute-start | bytes 7962632 | tf_op jit(solution)/shard_map/ppermute | solution.py:80
  1277.5 180.6 %collective-permute-start.85 = (bf16[8,72,4608]{2,1,0:T(8,128)(2,1)}, bf16[8,72,4608]{2,1,0:T(8,128)(2,1)}, u32[]{:S(2)}, u32[]{:S(2)}) collective-permute-start(bf16[8,72,4608]{2,1,0:T(8,128)(2,1)} %bitcast.260), channel_id=1, source_target_pairs={{0,1},{1,0},{2,3},{3,2},{4,5},{5,4},{6,7},{7,6},{8,9},{9,8},{10,11... | collective-permute-start | bytes 15925256 | tf_op jit(solution)/shard_map/ppermute | solution.py:80
  1293.8 168.4 %collective-permute-start.57 = (bf16[8,72,4608]{2,1,0:T(8,128)(2,1)}, bf16[8,72,4608]{2,1,0:T(8,128)(2,1)}, u32[]{:S(2)}, u32[]{:S(2)}) collective-permute-start(bf16[8,72,4608]{2,1,0:T(8,128)(2,1)} %bitcast.184), channel_id=1, source_target_pairs={{0,1},{1,0},{2,3},{3,2},{4,5},{5,4},{6,7},{7,6},{8,9},{9,8},{10,11... | collective-permute-start | bytes 15925256 | tf_op jit(solution)/shard_map/ppermute | solution.py:80
  1336.3 118.4 %collective-permute-start.74 = (bf16[4,72,1792]{2,1,0:T(8,128)(2,1)}, bf16[4,72,1792]{2,1,0:T(8,128)(2,1)}, u32[]{:S(2)}, u32[]{:S(2)}) collective-permute-start(bf16[4,72,1792]{2,1,0:T(8,128)(2,1)} %fusion.105), channel_id=1, source_target_pairs={{0,2},{1,3},{2,0},{3,1},{4,6},{5,7},{6,4},{7,5},{8,10},{9,11},{10,... | collective-permute-start | bytes 3096584 | tf_op jit(solution)/shard_map/ppermute | solution.py:80
  1458.1 114.2 %collective-permute-start.94 = (bf16[8,144,1152]{2,1,0:T(8,128)(2,1)S(1)}, bf16[8,144,1152]{2,1,0:T(8,128)(2,1)}, u32[]{:S(2)}, u32[]{:S(2)}) collective-permute-start(bf16[8,144,1152]{2,1,0:T(8,128)(2,1)S(1)} %copy-done.108), channel_id=1, source_target_pairs={{0,16},{16,0},{1,17},{17,1},{2,18},{18,2},{3,19},{19,3},{4,20},{20... | collective-permute-start | bytes 7962632 | tf_op jit(solution)/shard_map/ppermute | solution.py:84
  1462.3 134.6 %collective-permute-start.44 = (bf16[8,72,1792]{2,1,0:T(8,128)(2,1)}, bf16[8,72,1792]{2,1,0:T(8,128)(2,1)}, u32[]{:S(2)}, u32[]{:S(2)}) collective-permute-start(bf16[8,72,1792]{2,1,0:T(8,128)(2,1)} %bitcast.148), channel_id=1, source_target_pairs={{0,1},{1,0},{2,3},{3,2},{4,5},{5,4},{6,7},{7,6},{8,9},{9,8},{10,11... | collective-permute-start | bytes 6193160 | tf_op jit(solution)/shard_map/ppermute | solution.py:80
  1468.9 109.0 %collective-permute-start.73 = (bf16[4,72,1792]{2,1,0:T(8,128)(2,1)S(1)}, bf16[4,72,1792]{2,1,0:T(8,128)(2,1)}, u32[]{:S(2)}, u32[]{:S(2)}) collective-permute-start(bf16[4,72,1792]{2,1,0:T(8,128)(2,1)S(1)} %copy-done.165), channel_id=1, source_target_pairs={{0,2},{1,3},{2,0},{3,1},{4,6},{5,7},{6,4},{7,5},{8,10},{9,11},{10,... | collective-permute-start | bytes 3096584 | tf_op jit(solution)/shard_map/ppermute | solution.py:80
  1469.8 130.4 %collective-permute-start.38 = (bf16[8,72,1792]{2,1,0:T(8,128)(2,1)}, bf16[8,72,1792]{2,1,0:T(8,128)(2,1)S(1)}, u32[]{:S(2)}, u32[]{:S(2)}) collective-permute-start(bf16[8,72,1792]{2,1,0:T(8,128)(2,1)} %bitcast.135), channel_id=1, source_target_pairs={{0,1},{1,0},{2,3},{3,2},{4,5},{5,4},{6,7},{7,6},{8,9},{9,8},{10,11... | collective-permute-start | bytes 6193160 | tf_op jit(solution)/shard_map/ppermute | solution.py:80
  1614.6 97.4 %collective-permute-start.45 = (bf16[4,72,896]{2,1,0:T(8,128)(2,1)S(1)}, bf16[4,72,896]{2,1,0:T(8,128)(2,1)S(1)}, u32[]{:S(2)}, u32[]{:S(2)}) collective-permute-start(bf16[4,72,896]{2,1,0:T(8,128)(2,1)S(1)} %get-tuple-element.167), channel_id=1, source_target_pairs={{0,2},{1,3},{2,0},{3,1},{4,6},{5,7},{6,4},{7,5},{8,10},{9,11},{10,... | collective-permute-start | bytes 1548296 | tf_op jit(solution)/shard_map/ppermute | solution.py:80
  (373 other events, 6451.5 us)
Sparse Core Ops, SparseCore 0:
  23.7 119.5 all-reduce.20
  1017.7 106.3 all-reduce.22
  1361.1 86.5 all-reduce.24

commit v2 on v1

--- a/solution.py
+++ b/solution.py
@@ -75,161 +75,198 @@
     return lax.axis_size("sp").bit_length() - 1
 
 
-def swap_sp(values, bit):
+def after(values, earlier):
+    if not earlier:
+        return values
+    return lax.optimization_barrier((values, tuple(earlier)))[0]
+
+
+def in_turn(links, key, values, exchange):
+    last = links.get(key)
+    result = exchange(values if last is None else after(values, [last]))
+    links[key] = result
+    return result
+
+
+def swap_sp(values, bit, links):
     size = lax.axis_size("sp")
-    return lax.ppermute(values, "sp", [(i, i ^ (1 << bit)) for i in range(size)])
-
-
-def swap_seq(values):
-    return lax.ppermute(values, "seq", [(0, 1), (1, 0)])
-
-
-def far_bits():
-    return list(range(index_bits() - 1, 1, -1))
-
-
-def gather_chip_rows(half, seq_first):
-    blocks = half[None]
-    for bit in far_bits():
-        blocks = jnp.concatenate([blocks, swap_sp(blocks, bit)], axis=0)
-    if seq_first:
-        other = swap_seq(blocks)
-        other = jnp.concatenate([other, swap_sp(other, 1)], axis=0)
-        blocks = jnp.concatenate([blocks, swap_sp(blocks, 1)], axis=0)
-    else:
-        blocks = jnp.concatenate([blocks, swap_sp(blocks, 1)], axis=0)
-        other = swap_seq(blocks)
-    return blocks, other
-
-
-def place_kernel(bits, moves, n_in, n_out, *refs):
-    sources, outs, sems = refs[:n_in], refs[n_in : n_in + n_out], refs[n_in + n_out :]
-    local_sem, send_sem, recv_sem = sems
+    pairs = [(i, i ^ (1 << bit)) for i in range(size)]
+    return in_turn(links, min(bit, 2), values, lambda v: lax.ppermute(v, "sp", pairs))
+
+
+def swap_seq(values, links, key="seq"):
+    return in_turn(links, key, values, lambda v: lax.ppermute(v, "seq", [(0, 1), (1, 0)]))
+
+
+def gather_kernel(rounds, n_in, n_out, *refs):
+    shards, outs = refs[:n_in], refs[n_in : n_in + n_out]
+    local_sem, send_sem, recv_sem = refs[n_in + n_out :]
     me = lax.axis_index("sp")
     plane = lax.axis_index("seq")
-    sibling = me + 1 - 2 * (me % 2)
+    count = index_bits()
+    place = [(me // (1 << (count - 1 - d))) % 2 for d in range(count)]
+
+    def flip(bit):
+        mine = (me // (1 << bit)) % 2
+        return (plane, me + (1 << bit) * (1 - 2 * mine))
+
+    across = (1 - plane, me)
+    partners = [flip(bit) for bit in range(count)] + [across]
     barrier = pltpu.get_barrier_semaphore()
-    pl.semaphore_signal(
-        barrier, inc=1, device_id=(plane, sibling), device_id_type=pl.DeviceIdType.MESH
-    )
-    pl.semaphore_wait(barrier, 1)
-    count = sources[0].shape[0]
-
-    def block_at(p):
-        block = me
-        for i, bit in enumerate(bits):
-            mine = (me // (1 << bit)) % 2
-            block = block + ((p // (1 << i)) % 2) * ((1 << bit) * (1 - 2 * mine))
-        return block
+    for partner in partners:
+        pl.semaphore_signal(
+            barrier, inc=1, device_id=partner, device_id_type=pl.DeviceIdType.MESH
+        )
+    pl.semaphore_wait(barrier, len(partners))
+
+    def part(ref, lead, piece):
+        weight, rows, columns = piece
+        if rows is None:
+            return ref.at[(*lead, slice(None), pl.ds(*columns))]
+        half, first, size = rows
+        return ref.at[(*lead, half, pl.ds(first, size), slice(None))]
+
+    def stage_places(stage):
+        return tuple(
+            slice(None) if d < stage else place[d] for d in range(count)
+        )
 
     for own_half in (0, 1):
 
         @pl.when(plane == own_half)
         def _():
-            def copies(p):
-                block = block_at(p)
-                result = []
-                for side in (0, 1):
-                    half = own_half if side == 0 else 1 - own_half
-                    for pair, first, width, out, place in moves[half]:
-                        source = sources[2 * pair + side]
-                        target = outs[out]
-                        if first is None:
-                            src, dst = source.at[p], target.at[block, place]
-                        else:
-                            src = source.at[p, :, pl.ds(first, width)]
-                            dst = target.at[block, :, pl.ds(place, width)]
-                        k = len(result)
-                        result.append(
-                            (
-                                pltpu.make_async_copy(src, dst, local_sem.at[p, k]),
-                                pltpu.make_async_remote_copy(
-                                    src_ref=src,
-                                    dst_ref=dst,
-                                    send_sem=send_sem.at[p, k],
-                                    recv_sem=recv_sem.at[p, k],
-                                    device_id=(plane, sibling),
-                                    device_id_type=pl.DeviceIdType.MESH,
-                                ),
-                            )
-                        )
-                return result
-
-            def begin(p, carry):
-                for local, remote in copies(p):
-                    remote.start()
-                    local.start()
-                return carry
-
-            def finish(p, carry):
-                for local, remote in copies(p):
-                    local.wait()
-                    remote.wait()
-                return carry
-
-            lax.fori_loop(0, count, begin, 0)
-            lax.fori_loop(0, count, finish, 0)
-
-
-def place_blocks(pairs, moves, shapes, collective_id):
-    arrays = [member for pair in pairs for member in pair]
-    bits = far_bits() + [1]
-    count = arrays[0].shape[0]
-    copies = len(moves[0]) + len(moves[1])
-    any_space = pl.BlockSpec(memory_space=pl.ANY)
+            started = []
+
+            def send(number, stage, slot, source, target, partner):
+                copy = pltpu.make_async_remote_copy(
+                    src_ref=source,
+                    dst_ref=target,
+                    send_sem=send_sem.at[number, stage, slot],
+                    recv_sem=recv_sem.at[number, stage, slot],
+                    device_id=partner,
+                    device_id_type=pl.DeviceIdType.MESH,
+                )
+                copy.start()
+                return copy
+
+            def own(chunk):
+                return chunk[own_half]
+
+            def other(chunk):
+                return chunk[1 - own_half]
+
+            def step(number, stage):
+                first, second = rounds[number]
+                lead = stage_places(min(stage, count - 2))
+                if stage < count - 2:
+                    moves = [(own(first), flip(count - 1 - stage)), (own(second), flip(count - 1 - stage))]
+                elif stage == count - 2:
+                    moves = [(own(first), flip(1)), (own(second), across)]
+                elif stage == count - 1:
+                    moves = [
+                        (own(first), across),
+                        (own(second), flip(1)),
+                        (other(second), flip(1)),
+                    ]
+                else:
+                    moves = [
+                        (piece, flip(0))
+                        for chunk in (first, second)
+                        for piece in (own(chunk), other(chunk))
+                    ]
+                copies = []
+                for slot, (piece, partner) in enumerate(moves):
+                    places = lead
+                    if stage == count - 1 and partner is across or stage == count:
+                        places = stage_places(count - 1)
+                    target = part(outs[piece[0]], places, piece)
+                    source = target
+                    if stage == 0:
+                        source = part(shards[piece[0]], (), piece)
+                    copies.append(send(number, stage, slot, source, target, partner))
+                return copies
+
+            copies = {}
+            local = []
+            for number, pair in enumerate(rounds):
+                for slot, chunk in enumerate(pair):
+                    piece = own(chunk)
+                    copy = pltpu.make_async_copy(
+                        part(shards[piece[0]], (), piece),
+                        part(outs[piece[0]], stage_places(0), piece),
+                        local_sem.at[number, slot],
+                    )
+                    copy.start()
+                    local.append(copy)
+            lags = list(range(count - 1)) + [count - 1, count + 1]
+            for time in range(len(rounds) + lags[-1]):
+                for stage, lag in enumerate(lags):
+                    number = time - lag
+                    if not 0 <= number < len(rounds):
+                        continue
+                    if stage == 1 and number == 0:
+                        for copy in local:
+                            copy.wait()
+                    if stage:
+                        for copy in copies[number, stage - 1]:
+                            copy.wait_recv()
+                    copies[number, stage] = step(number, stage)
+            for number in range(len(rounds)):
+                for copy in copies[number, count]:
+                    copy.wait_recv()
+                for stage in range(count + 1):
+                    for copy in copies[number, stage]:
+                        copy.wait_send()
+
+
+def gather_weights(shards, rounds, collective_id):
+    size = lax.axis_size("sp")
+    lead = (2,) * index_bits()
+    shapes = [lead + shard.shape for shard in shards]
     total = sum(2 * math.prod(shape) for shape in shapes)
-    return pl.pallas_call(
-        functools.partial(place_kernel, bits, moves, len(arrays), len(shapes)),
+    stages = index_bits() + 1
+    placed = pl.pallas_call(
+        functools.partial(gather_kernel, rounds, len(shards), len(shards)),
         out_shape=[jax.ShapeDtypeStruct(shape, jnp.bfloat16) for shape in shapes],
-        in_specs=[pl.BlockSpec(memory_space=pltpu.VMEM)] * len(arrays),
-        out_specs=[any_space] * len(shapes),
-        scratch_shapes=[pltpu.SemaphoreType.DMA((count, copies))] * 3,
+        in_specs=[pl.BlockSpec(memory_space=pltpu.VMEM)] * len(shards),
+        out_specs=[pl.BlockSpec(memory_space=pl.ANY)] * len(shards),
+        scratch_shapes=[
+            pltpu.SemaphoreType.DMA((len(rounds), 2)),
+            pltpu.SemaphoreType.DMA((len(rounds), stages, 4)),
+            pltpu.SemaphoreType.DMA((len(rounds), stages, 4)),
+        ],
         compiler_params=pltpu.CompilerParams(
             collective_id=collective_id, has_side_effects=True, vmem_limit_bytes=32 << 20
         ),
-        cost_estimate=pl.CostEstimate(flops=0, bytes_accessed=2 * total, transcendentals=0),
-    )(*arrays)
+        cost_estimate=pl.CostEstimate(flops=0, bytes_accessed=total, transcendentals=0),
+    )(*shards)
+    return [full.reshape(size * math.prod(full.shape[index_bits() : -1]), -1) for full in placed]
+
+
+def columns_round(*quarters):
+    pieces = [(weight, None, (first, width)) for weight, first, width in quarters]
+    return ((pieces[0], pieces[2]), (pieces[1], pieces[3]))
+
+
+def rows_round(weight, rows):
+    cut = rows // 32 * 16 + (rows // 16 % 2) * 16
+    return (
+        ((weight, (0, 0, cut), None), (weight, (1, 0, cut), None)),
+        ((weight, (0, cut, rows - cut), None), (weight, (1, cut, rows - cut), None)),
+    )
+
+
+def gather_all(tall, wide, rounds_of, collective_id):
+    if wide[0].shape[0] % 8 or lax.axis_size("seq") != 2:
+        return [lax.all_gather(shard, "sp", axis=0, tiled=True) for shard in wide + tall]
+    shards = list(wide) + [
+        shard.reshape(2, shard.shape[0] // 2, shard.shape[1]) for shard in tall
+    ]
+    return gather_weights(shards, rounds_of(tall[0].shape[0] // 2), collective_id)
 
 
 def pick_half(first, second):
     return jnp.where(lax.axis_index("seq") == 0, first, second)
-
-
-def gather_full(shard):
-    return lax.all_gather(shard, "sp", axis=0, tiled=True)
-
-
-def gather_columns(members, parts, orders, collective_id):
-    rows = members[0].shape[0]
-    size = lax.axis_size("sp")
-    if rows % 8 or lax.axis_size("seq") != 2:
-        return [gather_full(member) for member in members]
-    pairs, moves = [], ([], [])
-    for number, (halves, seq_first) in enumerate(zip(parts, orders)):
-        picked = []
-        for half, pieces in enumerate(halves):
-            columns = [members[w][:, first : first + width] for w, first, width in pieces]
-            picked.append(columns[0] if len(columns) == 1 else jnp.concatenate(columns, axis=1))
-            place = 0
-            for w, first, width in pieces:
-                moves[half].append((number, place, width, w, first))
-                place += width
-        pairs.append(gather_chip_rows(pick_half(*picked), seq_first))
-    shapes = [(size, rows, member.shape[1]) for member in members]
-    placed = place_blocks(pairs, moves, shapes, collective_id)
-    return [full.reshape(size * rows, -1) for full in placed]
-
-
-def gather_tall(shard, seq_first, collective_id):
-    rows, columns = shard.shape
-    size = lax.axis_size("sp")
-    if rows % 32 or lax.axis_size("seq") != 2:
-        return gather_full(shard)
-    pair = gather_chip_rows(pick_half(shard[: rows // 2], shard[rows // 2 :]), seq_first)
-    moves = ([(0, None, None, 0, 0)], [(0, None, None, 0, 1)])
-    shape = (size, 2, rows // 2, columns)
-    (full,) = place_blocks([pair], moves, [shape], collective_id)
-    return full.reshape(size * rows, columns)
 
 
 def low_sum(*members):
@@ -248,31 +285,18 @@
     return pick(paired, 1 - bit_value, 1), pick(paired, bit_value, 1)
 
 
-def scatter_grad(inputs, gradients, by_rows, seq_first):
+def scatter_grad(inputs, gradients, by_rows, seq_first, links):
     size = lax.axis_size("sp")
     me = lax.axis_index("sp")
     plane = lax.axis_index("seq")
     bits = [(me // (1 << b)) % 2 for b in range(index_bits())]
     left = inputs.reshape(-1, inputs.shape[-1])
     right = gradients.reshape(-1, gradients.shape[-1])
-    tokens, depth = left.shape
+    depth = left.shape[1]
     columns = right.shape[1]
     rows = depth // size
     half = (rows if by_rows else columns) // 2
-    grouped = left.reshape(tokens, size // 2, 2, rows)
-    sides = [pick_core(grouped, 1 - bits[0]), pick_core(grouped, bits[0])]
-    if by_rows:
-        sides = [
-            jnp.stack(
-                [
-                    pick_half(side[:, :, :half], side[:, :, half:]),
-                    pick_half(side[:, :, half:], side[:, :, :half]),
-                ],
-                axis=1,
-            )
-            for side in sides
-        ]
-    else:
+    if not by_rows:
         padded = -(-half // 128) * 128
         fill = ((0, 0), (0, padded - half))
         right = jnp.concatenate(
@@ -282,38 +306,33 @@
             ],
             axis=1,
         )
-
-    def product(side):
-        flat = side.reshape(tokens, depth // 2)
-        total = lax.dot_general(
-            flat, right, (((0,), (0,)), ((), ())), preferred_element_type=jnp.float32
-        ).astype(jnp.bfloat16)
-        if by_rows:
-            total = total.reshape(2, size // 2, half, columns)
-            return total[0], total[1]
-        total = total.reshape(size // 2, rows, -1)
-        return total
-
-    sent = product(sides[0])
-    kept = product(sides[1])
+    total = lax.dot_general(
+        left, right, (((0,), (0,)), ((), ())), preferred_element_type=jnp.float32
+    ).astype(jnp.bfloat16)
     if by_rows:
-        came = [swap_sp(member, 0) for member in sent]
-        own, other = (kept[0], came[0]), (kept[1], came[1])
+        total = total.reshape(size, 2, half, columns)
     else:
-        came = swap_sp(sent, 0)
+        total = total.reshape(size, rows, 2 * padded)
+    sent, kept = split_blocks(total, bits[0])
+    came = swap_sp(sent, 0, links)
+    if by_rows:
+        own, other = [
+            (pick(kept, which, 1), pick(came, which, 1)) for which in (plane, 1 - plane)
+        ]
+    else:
         own = (kept[:, :, :padded], came[:, :, :padded])
         other = (kept[:, :, padded:], came[:, :, padded:])
     if seq_first:
-        current = (*own, swap_seq(low_sum(*other)))
-        current = halve(current, bits[1], 1)
+        current = (*own, swap_seq(low_sum(*other), links))
+        current = halve(current, bits[1], 1, links)
     else:
-        own = halve(own, bits[1], 1)
-        other = halve(other, bits[1], 1)
-        current = (*own, swap_seq(low_sum(*other)))
+        own = halve(own, bits[1], 1, links)
+        other = halve(other, bits[1], 1, links)
+        current = (*own, swap_seq(low_sum(*other), links))
     for bit in range(2, index_bits()):
-        current = halve(current, bits[bit], bit)
+        current = halve(current, bits[bit], bit, links)
     mine = low_sum(*current)[0]
-    theirs = swap_seq(mine)
+    theirs = swap_seq(mine, links, "last")
     if not by_rows:
         mine, theirs = mine[:, :half], theirs[:, :half]
     axis = 0 if by_rows else 1
@@ -322,19 +341,15 @@
     ).astype(jnp.float32)
 
 
-def pick_core(grouped, which):
-    return jnp.where(which == 0, grouped[:, :, 0], grouped[:, :, 1])
-
-
-def halve(members, bit_value, bit):
+def halve(members, bit_value, bit, links):
     parts = [split_blocks(member, bit_value) for member in members]
     sent = low_sum(*[part[0] for part in parts])
-    return (low_sum(*[part[1] for part in parts]), swap_sp(sent, bit))
+    return (low_sum(*[part[1] for part in parts]), swap_sp(sent, bit, links))
 
 
 def sum_seq(values):
     mine = values.astype(jnp.bfloat16)
-    return mine.astype(jnp.float32) + swap_seq(mine).astype(jnp.float32)
+    return mine.astype(jnp.float32) + swap_seq(mine, {}).astype(jnp.float32)
 
 
 def triple_bias(query_bias, value_bias):
@@ -460,14 +475,14 @@
     return ((hidden, inner_sum, active, branch), residual + gating * branch)
 
 
-def feed_backward(grad_out, residual, offset, scaling, gating, stored, expand, shrink):
+def feed_backward(grad_out, residual, offset, scaling, gating, stored, expand, shrink, links):
     hidden, inner_sum, active, branch = stored
     branch_grad, gate_grad = gated_back(grad_out, gating, branch)
-    shrink_grad = scatter_grad(active, branch_grad, True, True)
+    shrink_grad = scatter_grad(active, branch_grad, True, True, links)
     active_grad = input_grad(branch_grad, shrink)
     gelu_value, gelu_back = jax.vjp(gelu_tanh, inner_sum)
     inner_grad = gelu_back(active_grad)[0].astype(jnp.bfloat16)
-    expand_grad = scatter_grad(hidden, inner_grad, False, False)
+    expand_grad = scatter_grad(hidden, inner_grad, False, False, links)
     hidden_grad = input_grad(inner_grad, expand)
     norm_value, norm_back = jax.vjp(modulate, residual, offset, scaling)
     residual_grad, offset_grad, scaling_grad = norm_back(hidden_grad)
@@ -499,22 +514,22 @@
     return (result, (hidden, pairs, mixture, branch, middle, stored_ffn))
 
 
-def spatial_backward(grad_out, residual, weights, frame_mod, stored):
+def spatial_backward(grad_out, residual, weights, frame_mod, stored, links):
     qkv_weight, out_weight, expand, shrink, vectors = weights
     pieces = block_pieces(as_float(vectors)[4:10], frame_mod)
     hidden, pairs, mixture, branch, middle, stored_ffn = stored
     middle_grad, ffn_table, ffn_grads = feed_backward(
-        grad_out, middle, pieces[3], pieces[4], pieces[5], stored_ffn, expand, shrink
+        grad_out, middle, pieces[3], pieces[4], pieces[5], stored_ffn, expand, shrink, links
     )
     branch_grad, gate_grad = gated_back(middle_grad, pieces[2], branch)
-    out_weight_grad = scatter_grad(mixture, branch_grad, False, True)
+    out_weight_grad = scatter_grad(mixture, branch_grad, False, True, links)
     out_bias = column_sum(branch_grad)
     mixture_grad = input_grad(branch_grad, out_weight).astype(jnp.bfloat16)
     triple_grad = pair_attention_back(pairs, mixture_grad)
     qkv_grad = jnp.concatenate(
         [
-            scatter_grad(hidden, triple_grad[..., : 3 * D // 2], False, True),
-            scatter_grad(hidden, triple_grad[..., 3 * D // 2 :], False, False),
+            scatter_grad(hidden, triple_grad[..., : 3 * D // 2], False, True, links),
+            scatter_grad(hidden, triple_grad[..., 3 * D // 2 :], False, False, links),
         ],
         axis=1,
     )
@@ -617,7 +632,7 @@
     )
 
 
-def temporal_backward(grad_out, residual, weights, frame_mod, same_clip, allowed, stored):
+def temporal_backward(grad_out, residual, weights, frame_mod, same_clip, allowed, stored, links):
     qkv_weight, out_weight, expand, shrink, query_weight, keyval_weight, cross_weight, vectors = (
         weights
     )
@@ -638,10 +653,10 @@
     groups, frames, patches = residual.shape[:3]
     scaling = HEAD_DIM ** (-0.5)
     crossed_grad, ffn_table, ffn_grads = feed_backward(
-        grad_out, crossed, pieces[3], pieces[4], pieces[5], stored_ffn, expand, shrink
+        grad_out, crossed, pieces[3], pieces[4], pieces[5], stored_ffn, expand, shrink, links
     )
     cross_branch_grad = crossed_grad.astype(jnp.bfloat16)
-    cross_weight_grad = scatter_grad(cross_mix, cross_branch_grad, False, True)
+    cross_weight_grad = scatter_grad(cross_mix, cross_branch_grad, False, True, links)
     cross_bias = column_sum(cross_branch_grad)
     mix_grad = input_grad(cross_branch_grad, cross_weight).astype(jnp.bfloat16)
     mix_grad = mix_grad.reshape(groups, frames, patches, HEADS, HEAD_DIM)
@@ -671,11 +686,11 @@
     )
     keyval_grad = jnp.concatenate([key_grad, value_grad], axis=-1).reshape(groups, -1, 2 * D)
     keyval_grad = lax.psum(keyval_grad.astype(jnp.bfloat16), "sp")
-    query_weight_grad = scatter_grad(lowered, query_grad, False, False)
+    query_weight_grad = scatter_grad(lowered, query_grad, False, False, links)
     cross_query_bias = column_sum(query_grad)
     middle_grad = crossed_grad + input_grad(query_grad, query_weight)
     branch_grad, gate_grad = gated_back(middle_grad, pieces[2], branch)
-    out_weight_grad = scatter_grad(mixture, branch_grad, False, True)
+    out_weight_grad = scatter_grad(mixture, branch_grad, False, True, links)
     out_bias = column_sum(branch_grad)
     mixture_grad = input_grad(branch_grad, out_weight).astype(jnp.bfloat16)
     mixture_grad = mixture_grad.reshape(groups, frames, patches, HEADS, HEAD_DIM)
@@ -712,7 +727,7 @@
     )
     triple_grad = jnp.concatenate([query_part, key_part, value_part], axis=-1).astype(jnp.bfloat16)
     triple_grad = triple_grad.reshape(groups, frames, patches, 3 * D)
-    qkv_grad = scatter_grad(hidden, triple_grad, False, False)
+    qkv_grad = scatter_grad(hidden, triple_grad, False, False, links)
     query_bias, value_bias = triple_bias_grad(column_sum(triple_grad))
     hidden_grad = input_grad(triple_grad, qkv_weight)
     norm_value, norm_back = jax.vjp(modulate, residual, pieces[0], pieces[1])
@@ -776,45 +791,51 @@
     groups, frames, patches = video.shape[:3]
     size = lax.axis_size("sp")
     third = D
-    full_sqkv, full_sout = gather_columns(
-        [spatial_qkv, spatial_out],
-        [
-            ([(0, 0, third)], [(0, 2 * third, third)]),
-            ([(0, third, third)], [(1, 0, third)]),
-        ],
-        [False, True],
-        0,
-    )
-    (full_sexp,) = gather_columns(
-        [spatial_expand], [([(0, 0, FF // 2)], [(0, FF // 2, FF // 2)])], [False], 1
-    )
-    full_sshr = gather_tall(spatial_shrink, True, 2)
-    full_tqkv, full_tout = gather_columns(
-        [temporal_qkv, temporal_out],
-        [
-            (
-                [(0, 0, 2 * third)],
-                [(0, 2 * third, third), (1, 0, third)],
-            ),
-        ],
-        [False],
-        3,
-    )
-    full_cq, full_ckv, full_cout = gather_columns(
-        [cross_query, cross_keyval, cross_out],
-        [
-            (
-                [(0, 0, third), (1, 0, third)],
-                [(1, third, third), (2, 0, third)],
-            ),
-        ],
-        [True],
-        4,
-    )
-    (full_texp,) = gather_columns(
-        [temporal_expand], [([(0, 0, FF // 2)], [(0, FF // 2, FF // 2)])], [False], 5
-    )
-    full_tshr = gather_tall(temporal_shrink, True, 6)
+    wide = [
+        spatial_qkv,
+        spatial_out,
+        spatial_expand,
+        temporal_qkv,
+        temporal_out,
+        cross_query,
+        cross_keyval,
+        cross_out,
+        temporal_expand,
+    ]
+
+    def rounds_of(rows):
+        def block_round(qkv, out):
+            return columns_round(
+                (qkv, 0, third), (qkv, third, third), (qkv, 2 * third, third), (out, 0, third)
+            )
+
+        def expand_round(weight):
+            quarter = FF // 4
+            return columns_round(*[(weight, k * quarter, quarter) for k in range(4)])
+
+        return [
+            block_round(0, 1),
+            expand_round(2),
+            rows_round(9, rows),
+            block_round(3, 4),
+            columns_round((5, 0, third), (6, 0, third), (6, third, third), (7, 0, third)),
+            expand_round(8),
+            rows_round(10, rows),
+        ]
+
+    (
+        full_sqkv,
+        full_sout,
+        full_sexp,
+        full_tqkv,
+        full_tout,
+        full_cq,
+        full_ckv,
+        full_cout,
+        full_texp,
+        full_sshr,
+        full_tshr,
+    ) = gather_all([spatial_shrink, temporal_shrink], wide, rounds_of, 0)
     all_vectors = lax.all_gather(
         jnp.concatenate([spatial_vectors, temporal_vectors], axis=0), "sp", axis=1, tiled=True
     )
@@ -845,6 +866,7 @@
         middle, temporal, frame_mod, same_clip, allowed, context
     )
     output = result.astype(jnp.bfloat16)
+    links = {}
     middle_grad, temporal_terms, keyval_grad = temporal_backward(
         cotangent.astype(jnp.float32),
         middle,
@@ -853,6 +875,7 @@
         same_clip,
         allowed,
         temporal_kept,
+        links,
     )
     shard_rows = D // lax.axis_size("sp")
     first_row = lax.axis_index("sp") * shard_rows
@@ -865,7 +888,7 @@
     text_grad = input_grad(context_grad, caption_weight).reshape(groups, CLIPS, CAP, -1)
     null_grad = jnp.sum(text_grad * dropped[:, :, None, None], axis=(0, 1))
     video_grad, spatial_terms = spatial_backward(
-        middle_grad, residual, spatial, frame_mod, spatial_kept
+        middle_grad, residual, spatial, frame_mod, spatial_kept, links
     )
     vector_fix = jnp.zeros((18, D), jnp.float32)
     vector_fix = vector_fix.at[5].set(value_bias_full)

time: 1870 us -> 1640 us (0.88)
  waiting for transfers between devices: 830 us -> 524 us
  Pallas kernels: 72.3 us -> 369 us
  other arithmetic: 189 us -> 108 us
  starting transfers between devices: 180 us -> 103 us
  local copies, waits for them, and re-layouts: 317 us -> 268 us
    ppermute x113 -> x75, waiting for transfers between devices: 753 us -> 447 us  [the longest x49 233 us: swap_sp(): lax.ppermute(v, 'sp', pairs)]
    pallas_call x7 -> x1, Pallas kernels: 72.3 us -> 369 us  [gather_weights(): pl.pallas_call(functools.partial(gather_kernel, rounds, len(shards), len(...]
    ppermute x113 -> x75, starting transfers between devices: 160 us -> 72 us  [the longest x49 40.6 us: swap_sp(): lax.ppermute(v, 'sp', pairs)]
    psum x1, waiting for transfers between devices: 77.5 us -> 0.01 us  [on_device(): lax.psum(jnp.concatenate([spatial_terms[4], temporal_terms[6]], axis=0),...]
    select_n x20 -> x0, local copies, waits for them, and re-layouts: 68 us -> none  [pick_core(): return jnp.where(which == 0, grouped[:, :, 0], grouped[:, :, 1])]
    psum x1, waiting for transfers between devices: 0.02 us -> 53.9 us  [on_device(): caption_sum = lax.psum(project(text_rows, caption_weight), 'sp')]
    select_n x10 -> x0, other arithmetic: 47.4 us -> none  [pick_core(): return jnp.where(which == 0, grouped[:, :, 0], grouped[:, :, 1])]
    squeeze x0 -> x11, local copies, waits for them, and re-layouts: none -> 43.7 us  [pick(): return lax.dynamic_index_in_dim(values, index, axis, keepdims=False)]
  transfers between devices with their start and end apart: 120 -> 82, of which waited for: 63 -> 45; matrix products, arithmetic and copies ran while one was open for 20% -> 20% of each run, Pallas kernels for 4% -> 0%
where the time goes in v2:
time: 1640 us; the launch traced here: 1630 us
  waiting for transfers between devices  524 us (32%)
  Pallas kernels  369 us (22%)
  local copies, waits for them, and re-layouts  268 us (16%)
  matrix products  217 us (13%)
  other arithmetic  108 us (7%)
  starting transfers between devices  103 us (6%)
  blocking collectives  23.4 us (1%)
  between operations  17.3 us (1%)
    pallas_call x1, Pallas kernels, gather_weights(): pl.pallas_call(functools.partial(gather_kernel, rounds, len(shards), len(...  369 us
    ppermute x49, waiting for transfers between devices, swap_sp(): lax.ppermute(v, 'sp', pairs)  233 us
    ppermute x26, waiting for transfers between devices, swap_seq(): lax.ppermute(v, 'seq', [(0, 1), (1, 0)])  214 us
    dot_general x12, matrix products, input_grad(): lax.dot_general(gradients, weight, (((gradients.ndim - 1,), (1,)), ((), (...  70.4 us
    dot_general x12, matrix products, project(): return jnp.dot(inputs, weight, preferred_element_type=jnp.float32)  60 us
    psum x1, waiting for transfers between devices, on_device(): caption_sum = lax.psum(project(text_rows, caption_weight), 'sp')  53.9 us
    convert_element_type x49, other arithmetic, low_sum(): return total.astype(jnp.bfloat16)  50.3 us
    squeeze x11, local copies, waits for them, and re-layouts, pick(): return lax.dynamic_index_in_dim(values, index, axis, keepdims=False)  43.7 us
  transfers between devices with their start and end apart: 82, of which 45 were waited for; matrix products, arithmetic and copies ran while one was open for 20% of the time, Pallas kernels for 0%

profile of v2, /device:TPU:0, one launch (start us, length us, event | category | flops | bytes accessed | tf_op | source)
XLA Modules:
  0.0 1629.0 jit_solution(13310000738132879813)
XLA Ops:
  8.0 23.4 %all-gather = bf16[16,72,32]{1,2,0:T(8,128)(2,1)S(1)} all-gather(bf16[1,72,32]{1,2,0:T(8,128)(2,1)S(1)} %maximum_bitcast_fusion), channel_id=1, replica_groups=mesh['seq'=2,'sp'=16] {'sp'}, dimensions={0}, use_global_device_ids=true | all-gather | bytes 78336 | tf_op jit(solution)/shard_map/all_gather | solution.py:839
  42.9 368.6 %shard_map.332 = (bf16[2,2,2,2,72,3456]{5,4,3,2,1,0:T(8,128)(2,1)}, bf16[2,2,2,2,72,1152]{5,4,3,2,1,0:T(8,128)(2,1)S(1)}, bf16[2,2,2,2,72,4608]{5,4,3,2,1,0:T(8,...) custom-call(bf16[72,3456]{1,0:T(8,128)(2,1)S(1)} %copy-done.13, ...), custom_call_target="tpu_custom_call" | custom-call | bytes 74317824 | tf_op jit(solution)/shard_map/pallas_call | solution.py:228
  418.3 7.9 fusion.7
  426.2 8.5 reshape.1372
  471.0 22.5 %all-to-all-done = bf16[16,32,8,216]{3,2,1,0:T(8,128)(2,1)} async-done(((bf16[16,32,8,216]{3,2,1,0:T(8,128)(2,1)}), bf16[16,32,8,216]{3,2,1,0:T(8,128)(2,1)}, u32[]{:S(2)}, u32[]{:S(2)}) %all-to-all-start) | async-done | bytes 1769504 | tf_op jit(solution)/shard_map/all_to_all | solution.py:453
  508.0 16.2 all-to-all-start.1
  524.4 53.9 %all-reduce.21.cloned.1.call-done = f32[2,240,1152]{2,1,0:T(8,128)} async-done(((f32[2,240,1152]{2,1,0:T(8,128)}), f32[2,240,1152]{2,1,0:T(8,128)}) %all-reduce.21.cloned.1.call-update) | async-done | bytes 2211856 | tf_op jit(solution)/shard_map/psum | solution.py:857
  623.0 8.1 reshape.1383
  682.1 10.2 convert_reduce_fusion
  692.4 9.8 multiply_reduce_fusion.3
  702.2 9.6 fusion.98
  771.6 10.8 fusion.4
  793.1 10.2 convert_reduce_fusion.1
  872.1 9.0 dynamic-slice_bitcast_fusion
  891.9 9.2 dynamic-slice_bitcast_fusion.1
  927.9 43.5 %collective-permute-done.12 = bf16[8,144,1152]{2,1,0:T(8,128)(2,1)} collective-permute-done((bf16[8,144,1152]{2,1,0:T(8,128)(2,1)}, bf16[8,144,1152]{2,1,0:T(8,128)(2,1)}, u32[]{:S(2)}, u32[]{:S(2)}) %collective-permute-start.12) | collective-permute-done | bytes 2654240 | tf_op jit(solution)/shard_map/ppermute | solution.py:98
  1018.0 18.4 %collective-permute-done.14 = bf16[4,72,2304]{2,1,0:T(8,128)(2,1)} collective-permute-done((bf16[4,72,2304]{2,1,0:T(8,128)(2,1)}, bf16[4,72,2304]{2,1,0:T(8,128)(2,1)}, u32[]{:S(2)}, u32[]{:S(2)}) %collective-permute-start.14) | collective-permute-done | bytes 1327136 | tf_op jit(solution)/shard_map/ppermute | solution.py:94
  1061.8 16.8 %collective-permute-done.15 = bf16[4,72,2304]{2,1,0:T(8,128)(2,1)} collective-permute-done((bf16[4,72,2304]{2,1,0:T(8,128)(2,1)}, bf16[4,72,2304]{2,1,0:T(8,128)(2,1)}, u32[]{:S(2)}, u32[]{:S(2)}) %collective-permute-start.15) | collective-permute-done | bytes 1327136 | tf_op jit(solution)/shard_map/ppermute | solution.py:94
  1090.4 24.7 %collective-permute-done = bf16[120,256]{1,0:T(8,128)(2,1)} collective-permute-done((bf16[120,256]{1,0:T(8,128)(2,1)}, bf16[120,256]{1,0:T(8,128)(2,1)}, u32[]{:S(2)}, u32[]{:S(2)}) %collective-permute-start) | collective-permute-done | bytes 61472 | tf_op jit(solution)/shard_map/ppermute | solution.py:98
  1189.8 14.1 collective-permute-done.22
  1219.6 17.3 %collective-permute-done.24 = bf16[4,72,1792]{2,1,0:T(8,128)(2,1)S(1)} collective-permute-done((bf16[4,72,1792]{2,1,0:T(8,128)(2,1)S(1)}, bf16[4,72,1792]{2,1,0:T(8,128)(2,1)S(1)}, u32[]{:S(2)}, u32[]{:S(2)}) %collective-permute-start.24) | collective-permute-done | bytes 1032224 | tf_op jit(solution)/shard_map/ppermute | solution.py:94
  1241.7 16.7 %collective-permute-done.25 = bf16[4,72,1792]{2,1,0:T(8,128)(2,1)S(1)} collective-permute-done((bf16[4,72,1792]{2,1,0:T(8,128)(2,1)S(1)}, bf16[4,72,1792]{2,1,0:T(8,128)(2,1)S(1)}, u32[]{:S(2)}, u32[]{:S(2)}) %collective-permute-start.25) | collective-permute-done | bytes 1032224 | tf_op jit(solution)/shard_map/ppermute | solution.py:94
  1266.6 10.5 collective-permute-done.37
  1288.8 52.9 %collective-permute-done.73 = bf16[32,72]{1,0:T(8,128)(2,1)S(1)} collective-permute-done((bf16[32,72]{1,0:T(8,128)(2,1)S(1)}, bf16[32,72]{1,0:T(8,128)(2,1)S(1)}, u32[]{:S(2)}, u32[]{:S(2)}) %collective-permute-start.73) | collective-permute-done | bytes 4640 | tf_op jit(solution)/shard_map/ppermute | solution.py:98
  1348.4 12.4 collective-permute-done.39
  1373.7 24.8 %collective-permute-done.28 = bf16[4,144,1152]{2,1,0:T(8,128)(2,1)S(1)} collective-permute-done((bf16[4,144,1152]{2,1,0:T(8,128)(2,1)S(1)}, bf16[4,144,1152]{2,1,0:T(8,128)(2,1)S(1)}, u32[]{:S(2)}, u32[]{:S(2)}) %collective-permute-start.28) | collective-permute-done | bytes 1327136 | tf_op jit(solution)/shard_map/ppermute | solution.py:94
  1403.2 25.2 %collective-permute-done.29 = bf16[4,72,2304]{2,1,0:T(8,128)(2,1)S(1)} collective-permute-done((bf16[4,72,2304]{2,1,0:T(8,128)(2,1)S(1)}, bf16[4,72,2304]{2,1,0:T(8,128)(2,1)S(1)}, u32[]{:S(2)}, u32[]{:S(2)}) %collective-permute-start.29) | collective-permute-done | bytes 1327136 | tf_op jit(solution)/shard_map/ppermute | solution.py:94
  1468.1 24.1 %collective-permute-done.60 = bf16[72,640]{1,0:T(8,128)(2,1)S(1)} collective-permute-done((bf16[72,640]{1,0:T(8,128)(2,1)S(1)}, bf16[72,640]{1,0:T(8,128)(2,1)S(1)}, u32[]{:S(2)}, u32[]{:S(2)}) %collective-permute-start.60) | collective-permute-done | bytes 92192 | tf_op jit(solution)/shard_map/ppermute | solution.py:98
  1498.0 16.8 %collective-permute-done.32 = bf16[8,72,640]{2,1,0:T(8,128)(2,1)S(1)} collective-permute-done((bf16[8,72,640]{2,1,0:T(8,128)(2,1)S(1)}, bf16[8,72,640]{2,1,0:T(8,128)(2,1)S(1)}, u32[]{:S(2)}, u32[]{:S(2)}) %collective-permute-start.32) | collective-permute-done | bytes 737312 | tf_op jit(solution)/shard_map/ppermute | solution.py:98
  1517.0 15.7 collective-permute-done.49
  1534.6 7.9 collective-permute-done.33
  1587.5 10.7 collective-permute-done.63
  (949 shorter events, 681.3 us)
Async XLA Ops:
  438.5 55.0 %all-to-all-start = ((bf16[16,32,8,216]{3,2,1,0:T(8,128)(2,1)}), bf16[16,32,8,216]{3,2,1,0:T(8,128)(2,1)}, u32[]{:S(2)}, u32[]{:S(2)}) async-start(bf16[16,32,8,216]{3,2,1,0:T(8,128)(2,1)} %bitcast.770), calls=%async_computation | async-start | bytes 4194304 | tf_op jit(solution)/shard_map/all_to_all | solution.py:453
  443.4 134.9 %all-reduce.21.cloned.1.call-start = ((), (), s32[]{:S(2)}) async-start(), calls=%async_computation.4 | async-start | bytes 4423680 | tf_op jit(solution)/shard_map/psum | solution.py:857
  508.0 84.0 %all-to-all-start.1 = ((bf16[1,32,128,72]{3,1,0,2:T(8,128)(2,1)}), bf16[1,32,128,72]{3,1,0,2:T(8,128)(2,1)}, u32[]{:S(2)}, u32[]{:S(2)}) async-start(bf16[1,32,128,72]{3,1,0,2:T(8,128)(2,1)} %copy.273), calls=%async_computation.1 | async-start | bytes 2097152 | tf_op jit(solution)/shard_map/all_to_all | solution.py:419
  524.2 513.4 %all-reduce.23.cloned.1.call-start = ((), (), s32[]{:S(2)}) async-start(), calls=%async_computation.5 | async-start | bytes 4423680 | tf_op jit(solution)/shard_map/psum | solution.py:688
  838.6 169.4 %all-to-all-start.2 = ((bf16[16,32,8,72]{3,2,1,0:T(8,128)(2,1)}), bf16[16,32,8,72]{3,2,1,0:T(8,128)(2,1)}, u32[]{:S(2)}, u32[]{:S(2)}) async-start(bf16[16,32,8,72]{3,2,1,0:T(8,128)(2,1)} %bitcast.91), calls=%async_computation.2 | async-start | bytes 2097152 | tf_op jit(solution)/shard_map/all_to_all | solution.py:464
  848.5 32.6 %collective-permute-start.2 = (bf16[8,2,144,1152]{3,2,0,1:T(8,128)(2,1)}, bf16[8,2,144,1152]{3,2,0,1:T(8,128)(2,1)}, u32[]{:S(2)}, u32[]{:S(2)}) collective-permute-start(bf16[8,2,144,1152]{3,2,0,1:T(8,128)(2,1)} %copy_bitcast_fusion), channel_id=1, source_target_pairs={{0,1},{1,0},{2,3},{3,2},{4,5},{5,4},{6,7},{7,6},{8,9},{9,8},{10,11... | collective-permute-start | bytes 15925256 | tf_op jit(solution)/shard_map/ppermute | solution.py:94
  881.1 38.8 %collective-permute-start.3 = (bf16[8,72,4608]{2,1,0:T(8,128)(2,1)}, bf16[8,72,4608]{2,1,0:T(8,128)(2,1)}, u32[]{:S(2)}, u32[]{:S(2)}) collective-permute-start(bf16[8,72,4608]{2,1,0:T(8,128)(2,1)} %get-tuple-element.129), channel_id=1, source_target_pairs={{0,1},{1,0},{2,3},{3,2},{4,5},{5,4},{6,7},{7,6},{8,9},{9,8},{10,11... | collective-permute-start | bytes 15925256 | tf_op jit(solution)/shard_map/ppermute | solution.py:94
  911.3 60.0 %collective-permute-start.12 = (bf16[8,144,1152]{2,1,0:T(8,128)(2,1)}, bf16[8,144,1152]{2,1,0:T(8,128)(2,1)}, u32[]{:S(2)}, u32[]{:S(2)}) collective-permute-start(bf16[8,144,1152]{2,1,0:T(8,128)(2,1)} %fusion.5), channel_id=1, source_target_pairs={{0,16},{16,0},{1,17},{17,1},{2,18},{18,2},{3,19},{19,3},{4,20},{20... | collective-permute-start | bytes 7962632 | tf_op jit(solution)/shard_map/ppermute | solution.py:98
  920.0 76.0 %collective-permute-start.4 = (bf16[8,72,1280]{2,1,0:T(8,128)(2,1)}, bf16[8,72,1280]{2,1,0:T(8,128)(2,1)}, u32[]{:S(2)}, u32[]{:S(2)}) collective-permute-start(bf16[8,72,1280]{2,1,0:T(8,128)(2,1)} %get-tuple-element.130), channel_id=1, source_target_pairs={{0,1},{1,0},{2,3},{3,2},{4,5},{5,4},{6,7},{7,6},{8,9},{9,8},{10,11... | collective-permute-start | bytes 4423688 | tf_op jit(solution)/shard_map/ppermute | solution.py:94
  975.7 30.8 %collective-permute-start.13 = (bf16[4,144,1152]{2,1,0:T(8,128)(2,1)}, bf16[4,144,1152]{2,1,0:T(8,128)(2,1)}, u32[]{:S(2)}, u32[]{:S(2)}) collective-permute-start(bf16[4,144,1152]{2,1,0:T(8,128)(2,1)} %get-tuple-element.254), channel_id=1, source_target_pairs={{0,2},{1,3},{2,0},{3,1},{4,6},{5,7},{6,4},{7,5},{8,10},{9,11},{10,... | collective-permute-start | bytes 3981320 | tf_op jit(solution)/shard_map/ppermute | solution.py:94
  1012.0 42.0 %collective-permute-start.6 = (bf16[8,72,1280]{2,1,0:T(8,128)(2,1)}, bf16[8,72,1280]{2,1,0:T(8,128)(2,1)}, u32[]{:S(2)}, u32[]{:S(2)}) collective-permute-start(bf16[8,72,1280]{2,1,0:T(8,128)(2,1)} %get-tuple-element.132), channel_id=1, source_target_pairs={{0,1},{1,0},{2,3},{3,2},{4,5},{5,4},{6,7},{7,6},{8,9},{9,8},{10,11... | collective-permute-start | bytes 4423688 | tf_op jit(solution)/shard_map/ppermute | solution.py:94
  1036.4 42.2 %collective-permute-start.15 = (bf16[4,72,2304]{2,1,0:T(8,128)(2,1)}, bf16[4,72,2304]{2,1,0:T(8,128)(2,1)}, u32[]{:S(2)}, u32[]{:S(2)}) collective-permute-start(bf16[4,72,2304]{2,1,0:T(8,128)(2,1)} %fusion.73), channel_id=1, source_target_pairs={{0,2},{1,3},{2,0},{3,1},{4,6},{5,7},{6,4},{7,5},{8,10},{9,11},{10,... | collective-permute-start | bytes 3981320 | tf_op jit(solution)/shard_map/ppermute | solution.py:94
  1048.5 82.7 %all-to-all-start.3 = ((bf16[1,32,128,216]{3,1,0,2:T(8,128)(2,1)}), bf16[1,32,128,216]{3,1,0,2:T(8,128)(2,1)}, u32[]{:S(2)}, u32[]{:S(2)}) async-start(bf16[1,32,128,216]{3,1,0,2:T(8,128)(2,1)} %copy.301), calls=%async_computation.3 | async-start | bytes 4194304 | tf_op jit(solution)/shard_map/all_to_all | solution.py:447
  1053.5 232.1 %all-reduce.25.cloned.1.call-start = ((), (), s32[]{:S(2)}) async-start(), calls=%async_computation.6 | async-start | bytes 294912 | tf_op jit(solution)/shard_map/psum | solution.py:896
  1053.9 98.8 %collective-permute-start.7 = (bf16[8,72,3584]{2,1,0:T(8,128)(2,1)}, bf16[8,72,3584]{2,1,0:T(8,128)(2,1)}, u32[]{:S(2)}, u32[]{:S(2)}) collective-permute-start(bf16[8,72,3584]{2,1,0:T(8,128)(2,1)} %get-tuple-element.133), channel_id=1, source_target_pairs={{0,1},{1,0},{2,3},{3,2},{4,5},{5,4},{6,7},{7,6},{8,9},{9,8},{10,11... | collective-permute-start | bytes 12386312 | tf_op jit(solution)/shard_map/ppermute | solution.py:94
  1081.4 37.4 %collective-permute-start.16 = (bf16[4,72,2304]{2,1,0:T(8,128)(2,1)}, bf16[4,72,2304]{2,1,0:T(8,128)(2,1)}, u32[]{:S(2)}, u32[]{:S(2)}) collective-permute-start(bf16[4,72,2304]{2,1,0:T(8,128)(2,1)} %fusion.32), channel_id=1, source_target_pairs={{0,16},{16,0},{1,17},{17,1},{2,18},{18,2},{3,19},{19,3},{4,20},{20... | collective-permute-start | bytes 3981320 | tf_op jit(solution)/shard_map/ppermute | solution.py:98
  1087.6 34.6 %collective-permute-start.74 = (bf16[72,2304]{1,0:T(8,128)(2,1)S(1)}, bf16[72,2304]{1,0:T(8,128)(2,1)}, u32[]{:S(2)}, u32[]{:S(2)}) collective-permute-start(bf16[72,2304]{1,0:T(8,128)(2,1)S(1)} %fusion.29), channel_id=1, source_target_pairs={{0,16},{16,0},{1,17},{17,1},{2,18},{18,2},{3,19},{19,3},{4,20},{20... | collective-permute-start | bytes 995336 | tf_op jit(solution)/shard_map/ppermute | solution.py:98
  1089.7 39.2 %collective-permute-start.1 = (bf16[256,1152]{1,0:T(8,128)(2,1)S(1)}, bf16[256,1152]{1,0:T(8,128)(2,1)}, u32[]{:S(2)}, u32[]{:S(2)}) collective-permute-start(bf16[256,1152]{1,0:T(8,128)(2,1)S(1)} %convolution_convert_fusion.13), channel_id=1, source_target_pairs={{0,16},{16,0},{1,17},{17,1},{2,18},{18,2},{3,19},{19,3},{4,20},{20... | collective-permute-start | bytes 1769480 | tf_op jit(solution)/shard_map/ppermute | solution.py:98
  1152.7 87.3 %collective-permute-start.8 = (bf16[8,2,144,1152]{3,2,0,1:T(8,128)(2,1)}, bf16[8,2,144,1152]{3,2,0,1:T(8,128)(2,1)}, u32[]{:S(2)}, u32[]{:S(2)}) collective-permute-start(bf16[8,2,144,1152]{3,2,0,1:T(8,128)(2,1)} %copy_bitcast_fusion.1), channel_id=1, source_target_pairs={{0,1},{1,0},{2,3},{3,2},{4,5},{5,4},{6,7},{7,6},{8,9},{9,8},{10,11... | collective-permute-start | bytes 15925256 | tf_op jit(solution)/shard_map/ppermute | solution.py:94
  1240.0 129.8 %collective-permute-start.9 = (bf16[8,72,4608]{2,1,0:T(8,128)(2,1)}, bf16[8,72,4608]{2,1,0:T(8,128)(2,1)}, u32[]{:S(2)}, u32[]{:S(2)}) collective-permute-start(bf16[8,72,4608]{2,1,0:T(8,128)(2,1)} %get-tuple-element.135), channel_id=1, source_target_pairs={{0,1},{1,0},{2,3},{3,2},{4,5},{5,4},{6,7},{7,6},{8,9},{9,8},{10,11... | collective-permute-start | bytes 15925256 | tf_op jit(solution)/shard_map/ppermute | solution.py:94
  1277.1 65.8 %collective-permute-start.38 = (bf16[2,72,2304]{2,1,0:T(8,128)(2,1)}, bf16[2,72,2304]{2,1,0:T(8,128)(2,1)}, u32[]{:S(2)}, u32[]{:S(2)}) collective-permute-start(bf16[2,72,2304]{2,1,0:T(8,128)(2,1)} %get-tuple-element.161), channel_id=1, source_target_pairs={{0,4},{1,5},{2,6},{3,7},{4,0},{5,1},{6,2},{7,3},{8,12},{9,13},{10,... | collective-permute-start | bytes 1990664 | tf_op jit(solution)/shard_map/ppermute | solution.py:94
  1281.9 83.8 %collective-permute-start.27 = (bf16[8,144,1152]{2,1,0:T(8,128)(2,1)}, bf16[8,144,1152]{2,1,0:T(8,128)(2,1)}, u32[]{:S(2)}, u32[]{:S(2)}) collective-permute-start(bf16[8,144,1152]{2,1,0:T(8,128)(2,1)} %fusion.6), channel_id=1, source_target_pairs={{0,16},{16,0},{1,17},{17,1},{2,18},{18,2},{3,19},{19,3},{4,20},{20... | collective-permute-start | bytes 7962632 | tf_op jit(solution)/shard_map/ppermute | solution.py:98
  1286.4 55.2 %collective-permute-start.73 = (bf16[32,72]{1,0:T(8,128)(2,1)S(1)}, bf16[32,72]{1,0:T(8,128)(2,1)S(1)}, u32[]{:S(2)}, u32[]{:S(2)}) collective-permute-start(bf16[32,72]{1,0:T(8,128)(2,1)S(1)} %fusion.259), channel_id=1, source_target_pairs={{0,16},{16,0},{1,17},{17,1},{2,18},{18,2},{3,19},{19,3},{4,20},{20... | collective-permute-start | bytes 13832 | tf_op jit(solution)/shard_map/ppermute | solution.py:98
  1362.0 39.6 %collective-permute-start.57 = (bf16[72,2304]{1,0:T(8,128)(2,1)S(1)}, bf16[72,2304]{1,0:T(8,128)(2,1)S(1)}, u32[]{:S(2)}, u32[]{:S(2)}) collective-permute-start(bf16[72,2304]{1,0:T(8,128)(2,1)S(1)} %fusion.213), channel_id=1, source_target_pairs={{0,16},{16,0},{1,17},{17,1},{2,18},{18,2},{3,19},{19,3},{4,20},{20... | collective-permute-start | bytes 995336 | tf_op jit(solution)/shard_map/ppermute | solution.py:98
  1369.7 31.8 %collective-permute-start.40 = (bf16[2,72,640]{2,1,0:T(8,128)(2,1)S(1)}, bf16[2,72,640]{2,1,0:T(8,128)(2,1)S(1)}, u32[]{:S(2)}, u32[]{:S(2)}) collective-permute-start(bf16[2,72,640]{2,1,0:T(8,128)(2,1)S(1)} %get-tuple-element.163), channel_id=1, source_target_pairs={{0,4},{1,5},{2,6},{3,7},{4,0},{5,1},{6,2},{7,3},{8,12},{9,13},{10,... | collective-permute-start | bytes 552968 | tf_op jit(solution)/shard_map/ppermute | solution.py:94
  1402.8 55.3 %collective-permute-start.10 = (bf16[8,72,1280]{2,1,0:T(8,128)(2,1)S(1)}, bf16[8,72,1280]{2,1,0:T(8,128)(2,1)S(1)}, u32[]{:S(2)}, u32[]{:S(2)}) collective-permute-start(bf16[8,72,1280]{2,1,0:T(8,128)(2,1)S(1)} %copy-done.106), channel_id=1, source_target_pairs={{0,1},{1,0},{2,3},{3,2},{4,5},{5,4},{6,7},{7,6},{8,9},{9,8},{10,11... | collective-permute-start | bytes 4423688 | tf_op jit(solution)/shard_map/ppermute | solution.py:94
  1458.1 37.3 %collective-permute-start.11 = (bf16[8,72,1792]{2,1,0:T(8,128)(2,1)S(1)}, bf16[8,72,1792]{2,1,0:T(8,128)(2,1)S(1)}, u32[]{:S(2)}, u32[]{:S(2)}) collective-permute-start(bf16[8,72,1792]{2,1,0:T(8,128)(2,1)S(1)} %copy-done.102), channel_id=1, source_target_pairs={{0,1},{1,0},{2,3},{3,2},{4,5},{5,4},{6,7},{7,6},{8,9},{9,8},{10,11... | collective-permute-start | bytes 6193160 | tf_op jit(solution)/shard_map/ppermute | solution.py:94
  1458.7 36.8 %collective-permute-start.31 = (bf16[4,72,2304]{2,1,0:T(8,128)(2,1)S(1)}, bf16[4,72,2304]{2,1,0:T(8,128)(2,1)S(1)}, u32[]{:S(2)}, u32[]{:S(2)}) collective-permute-start(bf16[4,72,2304]{2,1,0:T(8,128)(2,1)S(1)} %fusion.33), channel_id=1, source_target_pairs={{0,16},{16,0},{1,17},{17,1},{2,18},{18,2},{3,19},{19,3},{4,20},{20... | collective-permute-start | bytes 3981320 | tf_op jit(solution)/shard_map/ppermute | solution.py:98
  1460.6 31.6 %collective-permute-start.60 = (bf16[72,640]{1,0:T(8,128)(2,1)S(1)}, bf16[72,640]{1,0:T(8,128)(2,1)S(1)}, u32[]{:S(2)}, u32[]{:S(2)}) collective-permute-start(bf16[72,640]{1,0:T(8,128)(2,1)S(1)} %fusion.251), channel_id=1, source_target_pairs={{0,16},{16,0},{1,17},{17,1},{2,18},{18,2},{3,19},{19,3},{4,20},{20... | collective-permute-start | bytes 276488 | tf_op jit(solution)/shard_map/ppermute | solution.py:98
  1495.4 54.3 %collective-permute-start.66 = (bf16[8,72,1792]{2,1,0:T(8,128)(2,1)S(1)}, bf16[8,72,1792]{2,1,0:T(8,128)(2,1)S(1)}, u32[]{:S(2)}, u32[]{:S(2)}) collective-permute-start(bf16[8,72,1792]{2,1,0:T(8,128)(2,1)S(1)} %copy-done.101), channel_id=1, source_target_pairs={{0,1},{1,0},{2,3},{3,2},{4,5},{5,4},{6,7},{7,6},{8,9},{9,8},{10,11... | collective-permute-start | bytes 6193160 | tf_op jit(solution)/shard_map/ppermute | solution.py:94
  1496.7 36.8 %collective-permute-start.61 = (bf16[72,1792]{1,0:T(8,128)(2,1)S(1)}, bf16[72,1792]{1,0:T(8,128)(2,1)S(1)}, u32[]{:S(2)}, u32[]{:S(2)}) collective-permute-start(bf16[72,1792]{1,0:T(8,128)(2,1)S(1)} %fusion.222), channel_id=1, source_target_pairs={{0,16},{16,0},{1,17},{17,1},{2,18},{18,2},{3,19},{19,3},{4,20},{20... | collective-permute-start | bytes 774152 | tf_op jit(solution)/shard_map/ppermute | solution.py:98
  1533.5 34.5 %collective-permute-start.62 = (bf16[144,1152]{1,0:T(8,128)(2,1)S(1)}, bf16[144,1152]{1,0:T(8,128)(2,1)S(1)}, u32[]{:S(2)}, u32[]{:S(2)}) collective-permute-start(bf16[144,1152]{1,0:T(8,128)(2,1)S(1)} %fusion.212), channel_id=1, source_target_pairs={{0,16},{16,0},{1,17},{17,1},{2,18},{18,2},{3,19},{19,3},{4,20},{20... | collective-permute-start | bytes 995336 | tf_op jit(solution)/shard_map/ppermute | solution.py:98
  (283 other events, 4281.6 us)
Sparse Core Ops, SparseCore 0:
  447.8 130.4 all-reduce.20
  813.7 103.9 all-reduce.22
  1180.6 88.0 all-reduce.24

commit v3 on v2

--- a/solution.py
+++ b/solution.py
@@ -100,7 +100,7 @@
 
 def gather_kernel(rounds, n_in, n_out, *refs):
     shards, outs = refs[:n_in], refs[n_in : n_in + n_out]
-    local_sem, send_sem, recv_sem = refs[n_in + n_out :]
+    local_sem, send_sem, recv_sem, small_local, small_send, small_recv = refs[n_in + n_out :]
     me = lax.axis_index("sp")
     plane = lax.axis_index("seq")
     count = index_bits()
@@ -186,8 +186,25 @@
                     copies.append(send(number, stage, slot, source, target, partner))
                 return copies
 
+            def small_step(stage):
+                target = outs[-1].at[stage_places(stage)]
+                copy = pltpu.make_async_remote_copy(
+                    src_ref=target if stage else shards[-1],
+                    dst_ref=target,
+                    send_sem=small_send.at[stage],
+                    recv_sem=small_recv.at[stage],
+                    device_id=flip(count - 1 - stage),
+                    device_id_type=pl.DeviceIdType.MESH,
+                )
+                copy.start()
+                return copy
+
             copies = {}
-            local = []
+            small = [small_step(0)]
+            local = [
+                pltpu.make_async_copy(shards[-1], outs[-1].at[stage_places(0)], small_local)
+            ]
+            local[0].start()
             for number, pair in enumerate(rounds):
                 for slot, chunk in enumerate(pair):
                     piece = own(chunk)
@@ -204,13 +221,19 @@
                     number = time - lag
                     if not 0 <= number < len(rounds):
                         continue
-                    if stage == 1 and number == 0:
-                        for copy in local:
-                            copy.wait()
+                    if stage == 0 and 0 < number < count:
+                        if number == 1:
+                            for copy in local:
+                                copy.wait()
+                        small[-1].wait_recv()
+                        small.append(small_step(number))
                     if stage:
                         for copy in copies[number, stage - 1]:
                             copy.wait_recv()
                     copies[number, stage] = step(number, stage)
+            small[-1].wait_recv()
+            for copy in small:
+                copy.wait_send()
             for number in range(len(rounds)):
                 for copy in copies[number, count]:
                     copy.wait_recv()
@@ -234,13 +257,19 @@
             pltpu.SemaphoreType.DMA((len(rounds), 2)),
             pltpu.SemaphoreType.DMA((len(rounds), stages, 4)),
             pltpu.SemaphoreType.DMA((len(rounds), stages, 4)),
+            pltpu.SemaphoreType.DMA,
+            pltpu.SemaphoreType.DMA((index_bits(),)),
+            pltpu.SemaphoreType.DMA((index_bits(),)),
         ],
         compiler_params=pltpu.CompilerParams(
             collective_id=collective_id, has_side_effects=True, vmem_limit_bytes=32 << 20
         ),
         cost_estimate=pl.CostEstimate(flops=0, bytes_accessed=total, transcendentals=0),
     )(*shards)
-    return [full.reshape(size * math.prod(full.shape[index_bits() : -1]), -1) for full in placed]
+    *large, small = placed
+    full = [member.reshape(size * math.prod(member.shape[index_bits() : -1]), -1) for member in large]
+    small = jnp.swapaxes(small.reshape(size, *small.shape[-2:]), 0, 1)
+    return full + [small.reshape(small.shape[0], -1)]
 
 
 def columns_round(*quarters):
@@ -256,12 +285,14 @@
     )
 
 
-def gather_all(tall, wide, rounds_of, collective_id):
+def gather_all(tall, wide, small, rounds_of, collective_id):
     if wide[0].shape[0] % 8 or lax.axis_size("seq") != 2:
-        return [lax.all_gather(shard, "sp", axis=0, tiled=True) for shard in wide + tall]
+        full = [lax.all_gather(shard, "sp", axis=0, tiled=True) for shard in wide + tall]
+        return full + [lax.all_gather(small, "sp", axis=1, tiled=True)]
     shards = list(wide) + [
         shard.reshape(2, shard.shape[0] // 2, shard.shape[1]) for shard in tall
     ]
+    shards.append(small)
     return gather_weights(shards, rounds_of(tall[0].shape[0] // 2), collective_id)
 
 
@@ -341,6 +372,434 @@
     ).astype(jnp.float32)
 
 
+def scatter_kernel(pairs, full_pairs, places, left, right, small, *refs):
+    came, out, small_out = refs[:5], refs[5], refs[6]
+    scratch = refs[7:]
+    left_in, right_in, product, core_send, core_own, loaded = scratch[:6]
+    sends, keeps = scratch[6:11], scratch[11:15]
+    in_sem, load_sem, out_sem, core_send_sem, core_recv_sem, send_sem, recv_sem = scratch[15:22]
+    small_sum, small_came, small_send, small_recv = scratch[22:]
+    me = lax.axis_index("sp")
+    plane = lax.axis_index("seq")
+
+    def bit_of(bit):
+        return (me // (1 << bit)) % 2
+
+    def flip(bit):
+        return (plane, me + (1 << bit) * (1 - 2 * bit_of(bit)))
+
+    across = (1 - plane, me)
+    core = bit_of(0)
+    rows = out.shape[3]
+    barrier = pltpu.get_barrier_semaphore()
+    partners = [flip(bit) for bit in range(4)] + [across]
+    for partner in partners:
+        pl.semaphore_signal(
+            barrier, inc=1, device_id=partner, device_id_type=pl.DeviceIdType.MESH
+        )
+    pl.semaphore_wait(barrier, len(partners))
+
+    def remote(source, target, send, recv, partner):
+        return pltpu.make_async_remote_copy(
+            src_ref=source,
+            dst_ref=target,
+            send_sem=send,
+            recv_sem=recv,
+            device_id=partner,
+            device_id_type=pl.DeviceIdType.MESH,
+        )
+
+    def half_of(side):
+        return plane if side == 0 else 1 - plane
+
+    def core_copy(pair, chunk, side):
+        number = 2 * chunk + side
+        return remote(
+            core_send.at[number],
+            came[0].at[pair, number],
+            core_send_sem.at[number],
+            core_recv_sem.at[pair, number],
+            flip(0),
+        )
+
+    def stage_partner(stage, chunk):
+        if stage == 1:
+            return across if chunk == 0 else flip(1)
+        if stage == 2:
+            return flip(1) if chunk == 0 else across
+        return flip(2) if stage == 3 else flip(3) if stage == 4 else across
+
+    def stage_copy(stage, pair, chunk):
+        source = sends[stage - 1].at[pair % 2, chunk]
+        target = out.at[pair, chunk, plane] if stage == 5 else came[stage].at[pair, chunk]
+        return remote(
+            source,
+            target,
+            send_sem.at[stage - 1, pair % 2, chunk],
+            recv_sem.at[stage - 1, pair, chunk],
+            stage_partner(stage, chunk),
+        )
+
+    def out_copy(pair, chunk):
+        return pltpu.make_async_copy(
+            sends[4].at[pair % 2, chunk], out.at[pair, chunk, plane], out_sem.at[pair % 2, chunk]
+        )
+
+    def has(pair, chunk):
+        return pair < (pairs if chunk == 0 else full_pairs)
+
+    def inputs(pair, chunk, side, slot):
+        of_left, of_right = places(pair, 2 * chunk + half_of(side))
+        return (
+            pltpu.make_async_copy(left.at[of_left], left_in.at[slot], in_sem.at[slot, 0]),
+            pltpu.make_async_copy(right.at[of_right], right_in.at[slot], in_sem.at[slot, 1]),
+        )
+
+    def start_inputs(pair, chunk, side, slot):
+        for copy in inputs(pair, chunk, side, slot):
+            copy.start()
+
+    def products(pair):
+        start_inputs(pair, 0, 0, 0)
+        for chunk in (0, 1):
+
+            @pl.when(has(pair, chunk))
+            def _():
+                for side in (0, 1):
+                    number = 2 * chunk + side
+
+                    if side == 0:
+                        start_inputs(pair, chunk, 1, 1)
+                    elif chunk == 0:
+
+                        @pl.when(has(pair, 1))
+                        def _():
+                            start_inputs(pair, 1, 0, 0)
+
+                    for copy in inputs(pair, chunk, side, side):
+                        copy.wait()
+
+                    @pl.when((pair > 0))
+                    def _():
+                        core_copy(pair, chunk, side).wait_send()
+
+                    for which, target in ((1 - core, core_send), (core, core_own)):
+                        product[...] = jnp.dot(
+                            left_in[side, which],
+                            right_in[side],
+                            preferred_element_type=jnp.float32,
+                        )
+
+                        def store(block, carry):
+                            first = pl.multiple_of(block * rows, 8)
+                            target[number, block] = product[pl.ds(first, rows), :].astype(
+                                jnp.bfloat16
+                            )
+                            return carry
+
+                        lax.fori_loop(0, 8, store, 0)
+                        if target is core_send:
+                            core_copy(pair, chunk, side).start()
+
+    def add(a, b):
+        return (a.astype(jnp.float32) + b.astype(jnp.float32)).astype(jnp.bfloat16)
+
+    def load(source, slot, blocks):
+        return pltpu.make_async_copy(
+            source, loaded.at[slot, pl.ds(0, blocks)], load_sem.at[slot]
+        )
+
+    def free_send(stage, pair, chunk):
+        @pl.when(pair >= 2)
+        def _():
+            stage_copy(stage, pair, chunk).wait_send()
+
+    def add_core(pair):
+        slot = pair % 2
+        x = bit_of(1)
+        for chunk in (0, 1):
+
+            @pl.when(has(pair, chunk))
+            def _():
+                for side in (1, 0):
+                    core_copy(pair, chunk, side).wait_recv()
+                    load(came[0].at[pair, 2 * chunk + side], side, 8).start()
+                free_send(1, pair, chunk)
+                for side in (1, 0):
+                    number = 2 * chunk + side
+                    load(came[0].at[pair, number], side, 8).wait()
+                    if chunk == 0:
+                        target = sends[0] if side == 1 else keeps[0]
+
+                        def both(block, carry):
+                            target[slot, chunk, block] = add(
+                                core_own[number, block], loaded[side, block]
+                            )
+                            return carry
+
+                        lax.fori_loop(0, 8, both, 0)
+                    else:
+
+                        def split(z, carry):
+                            for target, block in (
+                                (sends[0], 2 * z + 1 - x),
+                                (keeps[0], 2 * z + x),
+                            ):
+                                target[slot, chunk, 4 * side + z] = add(
+                                    core_own[number, block], loaded[side, block]
+                                )
+                            return carry
+
+                        lax.fori_loop(0, 4, split, 0)
+                    if chunk == 0 and side == 1:
+                        stage_copy(1, pair, chunk).start()
+                if chunk == 1:
+                    stage_copy(1, pair, chunk).start()
+
+    def add_stage(stage, pair):
+        slot = pair % 2
+        blocks = 16 >> stage
+        for chunk in (0, 1):
+
+            @pl.when(has(pair, chunk))
+            def _():
+                stage_copy(stage, pair, chunk).wait_recv()
+                load(came[stage].at[pair, chunk], chunk, blocks).start()
+        for chunk in (0, 1):
+
+            @pl.when(has(pair, chunk))
+            def _():
+                free_send(stage + 1, pair, chunk)
+                if stage == 4:
+
+                    @pl.when(pair >= 2)
+                    def _():
+                        out_copy(pair, chunk).wait()
+
+                load(came[stage].at[pair, chunk], chunk, blocks).wait()
+                old, new = keeps[stage - 1], keeps[stage] if stage < 4 else None
+
+                def one(i, carry):
+                    if stage == 1 and chunk == 0:
+                        x = bit_of(1)
+                        gone, kept = 2 * i + 1 - x, 2 * i + x
+                    elif stage == 1:
+                        gone, kept = 4 + i, i
+                    elif stage == 2:
+                        low = bit_of(2)
+                        gone, kept = 2 * i + 1 - low, 2 * i + low
+                    else:
+                        gone, kept = 1 - bit_of(3), bit_of(3)
+                    sends[stage][slot, chunk, i] = add(
+                        old[slot, chunk, gone], loaded[chunk, gone]
+                    )
+                    new[slot, chunk, i] = add(old[slot, chunk, kept], loaded[chunk, kept])
+                    return carry
+
+                if stage < 4:
+                    lax.fori_loop(0, blocks // 2, one, 0)
+                else:
+                    sends[4][slot, chunk] = add(old[slot, chunk, 0], loaded[chunk, 0])
+                    out_copy(pair, chunk).start()
+                stage_copy(stage + 1, pair, chunk).start()
+
+    def small_copy(stage):
+        return remote(
+            small_sum.at[stage],
+            small_came.at[stage],
+            small_send.at[stage],
+            small_recv.at[stage],
+            partners[stage],
+        )
+
+    small_sum[0] = small[...]
+    small_copy(0).start()
+
+    def turn(time, carry):
+        for stage in range(len(partners)):
+
+            @pl.when(time == stage)
+            def _():
+                small_copy(stage).wait_recv()
+                total = small_sum[stage] + small_came[stage]
+                if stage + 1 < len(partners):
+                    small_sum[stage + 1] = total
+                    small_copy(stage + 1).start()
+                else:
+                    small_out[...] = total
+
+        for lag, work in (
+            (1, add_core),
+            (2, functools.partial(add_stage, 1)),
+            (3, functools.partial(add_stage, 2)),
+            (4, functools.partial(add_stage, 3)),
+            (5, functools.partial(add_stage, 4)),
+            (0, products),
+        ):
+            pair = time - lag
+
+            @pl.when((pair >= 0) & (pair < pairs))
+            def _():
+                work(pair)
+
+        return carry
+
+    lax.fori_loop(0, pairs + 5, turn, 0)
+    for stage in range(len(partners)):
+        small_copy(stage).wait_send()
+    for chunk in (0, 1):
+        mine = pairs if chunk == 0 else full_pairs
+        for side in (0, 1):
+            core_copy(mine - 1, chunk, side).wait_send()
+        for pair in range(max(mine - 2, 0), mine):
+            out_copy(pair, chunk).wait()
+            for stage in range(1, 6):
+                stage_copy(stage, pair, chunk).wait_send()
+        for pair in range(mine):
+            stage_copy(5, pair, chunk).wait_recv()
+
+
+def scatter_products(left, right, small, pairs, full_pairs, places, collective_id):
+    depth, tokens = left.shape[2:]
+    width = right.shape[2]
+    rows = depth // 8
+    low = jnp.bfloat16
+
+    def blocks(*lead):
+        return jax.ShapeDtypeStruct((*lead, rows, width), low)
+
+    hbm = [
+        blocks(pairs, 4, 8),
+        blocks(pairs, 2, 8),
+        blocks(pairs, 2, 4),
+        blocks(pairs, 2, 2),
+        blocks(pairs, 2, 1),
+        blocks(pairs, 2, 2),
+    ]
+    any_space = pl.BlockSpec(memory_space=pl.ANY)
+
+    def vmem(*lead):
+        return pltpu.VMEM((*lead, rows, width), low)
+
+    dma = pltpu.SemaphoreType.DMA
+    whole = pl.BlockSpec(memory_space=pltpu.VMEM)
+    *_, out, total = pl.pallas_call(
+        functools.partial(scatter_kernel, pairs, full_pairs, places),
+        out_shape=hbm + [jax.ShapeDtypeStruct(small.shape, small.dtype)],
+        in_specs=[any_space] * 2 + [whole],
+        out_specs=[any_space] * len(hbm) + [whole],
+        scratch_shapes=[
+            pltpu.VMEM((2, 2, depth, tokens), low),
+            pltpu.VMEM((2, tokens, width), low),
+            pltpu.VMEM((depth, width), jnp.float32),
+            vmem(4, 8),
+            vmem(4, 8),
+            vmem(2, 8),
+            vmem(2, 2, 8),
+            vmem(2, 2, 4),
+            vmem(2, 2, 2),
+            vmem(2, 2, 1),
+            vmem(2, 2),
+            vmem(2, 2, 8),
+            vmem(2, 2, 4),
+            vmem(2, 2, 2),
+            vmem(2, 2, 1),
+            dma((2, 2)),
+            dma((2,)),
+            dma((2, 2)),
+            dma((4,)),
+            dma((pairs, 4)),
+            dma((5, 2, 2)),
+            dma((5, pairs, 2)),
+            pltpu.VMEM((5, *small.shape), small.dtype),
+            pltpu.VMEM((5, *small.shape), small.dtype),
+            dma((5,)),
+            dma((5,)),
+        ],
+        compiler_params=pltpu.CompilerParams(
+            collective_id=collective_id, has_side_effects=True, vmem_limit_bytes=58 << 20
+        ),
+        cost_estimate=pl.CostEstimate(
+            flops=4 * left.shape[0] * depth * tokens * width,
+            bytes_accessed=2 * left.size + 2 * right.size,
+            transcendentals=0,
+        ),
+    )(left, right, small)
+    return out, total
+
+
+def core_rows(inputs):
+    flat = inputs.reshape(-1, inputs.shape[-1])
+    size = lax.axis_size("sp")
+    rows = flat.shape[1] // size
+    grouped = flat.T.reshape(size // 2, 2, rows, flat.shape[0])
+    return jnp.swapaxes(grouped, 0, 1).reshape(2, size // 2 * rows, flat.shape[0])
+
+
+def quarter_rows(inputs):
+    flat = inputs.reshape(-1, inputs.shape[-1])
+    size = lax.axis_size("sp")
+    rows = flat.shape[1] // size // 4
+    grouped = flat.T.reshape(size // 2, 2, 4, rows, flat.shape[0])
+    moved = jnp.transpose(grouped, (2, 1, 0, 3, 4))
+    return moved.reshape(4, 2, size // 2 * rows, flat.shape[0])
+
+
+def token_rows(gradients):
+    return gradients.reshape(-1, gradients.shape[-1])
+
+
+def scatter_all(terms, small):
+    size = lax.axis_size("sp")
+    if size != 16 or lax.axis_size("seq") != 2:
+        links = {}
+        flags = [(False, False), (True, True), (False, False), (False, True)]
+        blocks = [
+            [scatter_grad(*pair, *flag, links) for pair, flag in zip(block, flags)]
+            for block in terms[:2]
+        ]
+        last = [scatter_grad(*pair, False, False, links) for pair in terms[2]]
+        return blocks[0], blocks[1], last, lax.psum(small, ("seq", "sp"))
+    lefts, rights = [], []
+    for expand, shrink, qkv, out in (terms[1], terms[0]):
+        lefts.append(quarter_rows(shrink[0]))
+        lefts += [core_rows(member[0])[None] for member in (expand, qkv, out)]
+        rights.append(token_rows(shrink[1])[None])
+        for member, count in ((expand, 4), (qkv, 3)):
+            cut = token_rows(member[1])
+            rights.append(jnp.swapaxes(cut.reshape(cut.shape[0], count, -1), 0, 1))
+        rights.append(token_rows(out[1])[None])
+    lefts += [core_rows(pair[0])[None] for pair in terms[2]]
+    rights += [token_rows(pair[1])[None] for pair in terms[2]]
+
+    def places(pair, k):
+        block = pair // 3
+        kind = pair % 3
+        tail = block // 2
+        shrink = (2 - kind) // 2 * (1 - tail)
+        wide = kind // 2
+        expand = (1 - wide) * (kind % 2)
+        of_left = 7 * block + (shrink + tail) * k + expand * 4 + wide * (5 + k // 3)
+        of_right = 9 * block + tail * k + expand * (1 + k) + wide * (5 + k)
+        return of_left, of_right
+
+    left = jnp.concatenate(lefts, axis=0)
+    right = jnp.concatenate(rights, axis=0)
+    done, total = scatter_products(left, right, small, 7, 6, places, 1)
+    done = done.astype(jnp.float32)
+
+    def quarter(pair, k):
+        return done[pair, k // 2, k % 2]
+
+    results = []
+    for first in (0, 3):
+        shrink = jnp.concatenate([quarter(first, k) for k in range(4)], axis=0)
+        expand = jnp.concatenate([quarter(first + 1, k) for k in range(4)], axis=1)
+        qkv = jnp.concatenate([quarter(first + 2, k) for k in range(3)], axis=1)
+        results.append([expand, shrink, qkv, quarter(first + 2, 3)])
+    return results[1], results[0], [quarter(6, 0), quarter(6, 1)], total
+
+
 def halve(members, bit_value, bit, links):
     parts = [split_blocks(member, bit_value) for member in members]
     sent = low_sum(*[part[0] for part in parts])
@@ -475,14 +934,14 @@
     return ((hidden, inner_sum, active, branch), residual + gating * branch)
 
 
-def feed_backward(grad_out, residual, offset, scaling, gating, stored, expand, shrink, links):
+def feed_backward(grad_out, residual, offset, scaling, gating, stored, expand, shrink):
     hidden, inner_sum, active, branch = stored
     branch_grad, gate_grad = gated_back(grad_out, gating, branch)
-    shrink_grad = scatter_grad(active, branch_grad, True, True, links)
+    shrink_grad = (active, branch_grad)
     active_grad = input_grad(branch_grad, shrink)
     gelu_value, gelu_back = jax.vjp(gelu_tanh, inner_sum)
     inner_grad = gelu_back(active_grad)[0].astype(jnp.bfloat16)
-    expand_grad = scatter_grad(hidden, inner_grad, False, False, links)
+    expand_grad = (hidden, inner_grad)
     hidden_grad = input_grad(inner_grad, expand)
     norm_value, norm_back = jax.vjp(modulate, residual, offset, scaling)
     residual_grad, offset_grad, scaling_grad = norm_back(hidden_grad)
@@ -514,25 +973,19 @@
     return (result, (hidden, pairs, mixture, branch, middle, stored_ffn))
 
 
-def spatial_backward(grad_out, residual, weights, frame_mod, stored, links):
+def spatial_backward(grad_out, residual, weights, frame_mod, stored):
     qkv_weight, out_weight, expand, shrink, vectors = weights
     pieces = block_pieces(as_float(vectors)[4:10], frame_mod)
     hidden, pairs, mixture, branch, middle, stored_ffn = stored
     middle_grad, ffn_table, ffn_grads = feed_backward(
-        grad_out, middle, pieces[3], pieces[4], pieces[5], stored_ffn, expand, shrink, links
+        grad_out, middle, pieces[3], pieces[4], pieces[5], stored_ffn, expand, shrink
     )
     branch_grad, gate_grad = gated_back(middle_grad, pieces[2], branch)
-    out_weight_grad = scatter_grad(mixture, branch_grad, False, True, links)
+    out_weight_grad = (mixture, branch_grad)
     out_bias = column_sum(branch_grad)
     mixture_grad = input_grad(branch_grad, out_weight).astype(jnp.bfloat16)
     triple_grad = pair_attention_back(pairs, mixture_grad)
-    qkv_grad = jnp.concatenate(
-        [
-            scatter_grad(hidden, triple_grad[..., : 3 * D // 2], False, True, links),
-            scatter_grad(hidden, triple_grad[..., 3 * D // 2 :], False, False, links),
-        ],
-        axis=1,
-    )
+    qkv_grad = (hidden, triple_grad)
     query_bias, value_bias = triple_bias_grad(column_sum(triple_grad))
     hidden_grad = input_grad(triple_grad, qkv_weight)
     norm_value, norm_back = jax.vjp(modulate, residual, pieces[0], pieces[1])
@@ -632,7 +1085,7 @@
     )
 
 
-def temporal_backward(grad_out, residual, weights, frame_mod, same_clip, allowed, stored, links):
+def temporal_backward(grad_out, residual, weights, frame_mod, same_clip, allowed, stored):
     qkv_weight, out_weight, expand, shrink, query_weight, keyval_weight, cross_weight, vectors = (
         weights
     )
@@ -653,10 +1106,10 @@
     groups, frames, patches = residual.shape[:3]
     scaling = HEAD_DIM ** (-0.5)
     crossed_grad, ffn_table, ffn_grads = feed_backward(
-        grad_out, crossed, pieces[3], pieces[4], pieces[5], stored_ffn, expand, shrink, links
+        grad_out, crossed, pieces[3], pieces[4], pieces[5], stored_ffn, expand, shrink
     )
     cross_branch_grad = crossed_grad.astype(jnp.bfloat16)
-    cross_weight_grad = scatter_grad(cross_mix, cross_branch_grad, False, True, links)
+    cross_weight_grad = (cross_mix, cross_branch_grad)
     cross_bias = column_sum(cross_branch_grad)
     mix_grad = input_grad(cross_branch_grad, cross_weight).astype(jnp.bfloat16)
     mix_grad = mix_grad.reshape(groups, frames, patches, HEADS, HEAD_DIM)
@@ -686,11 +1139,11 @@
     )
     keyval_grad = jnp.concatenate([key_grad, value_grad], axis=-1).reshape(groups, -1, 2 * D)
     keyval_grad = lax.psum(keyval_grad.astype(jnp.bfloat16), "sp")
-    query_weight_grad = scatter_grad(lowered, query_grad, False, False, links)
+    query_weight_grad = (lowered, query_grad)
     cross_query_bias = column_sum(query_grad)
     middle_grad = crossed_grad + input_grad(query_grad, query_weight)
     branch_grad, gate_grad = gated_back(middle_grad, pieces[2], branch)
-    out_weight_grad = scatter_grad(mixture, branch_grad, False, True, links)
+    out_weight_grad = (mixture, branch_grad)
     out_bias = column_sum(branch_grad)
     mixture_grad = input_grad(branch_grad, out_weight).astype(jnp.bfloat16)
     mixture_grad = mixture_grad.reshape(groups, frames, patches, HEADS, HEAD_DIM)
@@ -727,7 +1180,7 @@
     )
     triple_grad = jnp.concatenate([query_part, key_part, value_part], axis=-1).astype(jnp.bfloat16)
     triple_grad = triple_grad.reshape(groups, frames, patches, 3 * D)
-    qkv_grad = scatter_grad(hidden, triple_grad, False, False, links)
+    qkv_grad = (hidden, triple_grad)
     query_bias, value_bias = triple_bias_grad(column_sum(triple_grad))
     hidden_grad = input_grad(triple_grad, qkv_weight)
     norm_value, norm_back = jax.vjp(modulate, residual, pieces[0], pieces[1])
@@ -835,9 +1288,13 @@
         full_texp,
         full_sshr,
         full_tshr,
-    ) = gather_all([spatial_shrink, temporal_shrink], wide, rounds_of, 0)
-    all_vectors = lax.all_gather(
-        jnp.concatenate([spatial_vectors, temporal_vectors], axis=0), "sp", axis=1, tiled=True
+        all_vectors,
+    ) = gather_all(
+        [spatial_shrink, temporal_shrink],
+        wide,
+        jnp.concatenate([spatial_vectors, temporal_vectors], axis=0),
+        rounds_of,
+        0,
     )
     n_spatial = spatial_vectors.shape[0]
     spatial = (full_sqkv, full_sout, full_sexp, full_sshr, all_vectors[:n_spatial])
@@ -855,6 +1312,8 @@
     text_local = jnp.where(drop_mask[:, :, None, None] > 0, null_caption[None, None], captions)
     text_rows = text_local.reshape(groups, CLIPS * CAP, -1)
     caption_sum = lax.psum(project(text_rows, caption_weight), "sp")
+    caption_sum, first = lax.optimization_barrier((caption_sum, spatial[0]))
+    spatial = (first, *spatial[1:])
     frame_mod = frame_modulation(segment_ids, timesteps).reshape(groups, frames, 6, D)
     same_clip = (segment_ids[:, :, None] == segment_ids[:, None, :])[:, None, None]
     row_clip = jnp.arange(CLIPS * CAP) // CAP
@@ -866,7 +1325,6 @@
         middle, temporal, frame_mod, same_clip, allowed, context
     )
     output = result.astype(jnp.bfloat16)
-    links = {}
     middle_grad, temporal_terms, keyval_grad = temporal_backward(
         cotangent.astype(jnp.float32),
         middle,
@@ -875,10 +1333,22 @@
         same_clip,
         allowed,
         temporal_kept,
-        links,
     )
     shard_rows = D // lax.axis_size("sp")
     first_row = lax.axis_index("sp") * shard_rows
+    video_grad, spatial_terms = spatial_backward(
+        middle_grad, residual, spatial, frame_mod, spatial_kept
+    )
+    spatial_sums, temporal_sums, cross_sums, vector_total = scatter_all(
+        (
+            (spatial_terms[2], spatial_terms[3], spatial_terms[0], spatial_terms[1]),
+            (temporal_terms[2], temporal_terms[3], temporal_terms[0], temporal_terms[1]),
+            (temporal_terms[4], temporal_terms[5]),
+        ),
+        jnp.concatenate([spatial_terms[4], temporal_terms[6]], axis=0),
+    )
+    vector_total = lax.dynamic_slice_in_dim(vector_total, first_row, shard_rows, 1)
+    keyval_grad, video_grad = lax.optimization_barrier((keyval_grad, video_grad))
     context_grad = input_grad(keyval_grad, temporal[5]).astype(jnp.bfloat16)
     local_context = lax.dynamic_slice_in_dim(context, first_row, shard_rows, 2)
     keyval_weight_grad = weight_grad(local_context, keyval_grad)
@@ -887,36 +1357,34 @@
     caption_weight_grad = weight_grad(text_rows, context_grad)
     text_grad = input_grad(context_grad, caption_weight).reshape(groups, CLIPS, CAP, -1)
     null_grad = jnp.sum(text_grad * dropped[:, :, None, None], axis=(0, 1))
-    video_grad, spatial_terms = spatial_backward(
-        middle_grad, residual, spatial, frame_mod, spatial_kept, links
-    )
-    vector_fix = jnp.zeros((18, D), jnp.float32)
-    vector_fix = vector_fix.at[5].set(value_bias_full)
-    vector_fix = vector_fix.at[7].set(caption_bias_full)
-    vector_terms = lax.psum(
-        jnp.concatenate([spatial_terms[4], temporal_terms[6]], axis=0), "sp"
-    )
-    vector_terms = vector_terms + jnp.concatenate(
-        [jnp.zeros((n_spatial, D), jnp.float32), vector_fix], axis=0
-    )
-    vector_total = sum_seq(lax.dynamic_slice_in_dim(vector_terms, first_row, shard_rows, 1))
+    own_rows = [
+        lax.dynamic_slice_in_dim(row, first_row, shard_rows, 0)
+        for row in (value_bias_full, caption_bias_full)
+    ]
+    width = null_grad.shape[1]
+    flat = jnp.stack([jnp.pad(row, (0, width - shard_rows)) for row in own_rows])
+    small_total = sum_seq(jnp.concatenate([null_grad, flat], axis=0))
+    null_total = small_total[: null_grad.shape[0]]
+    bias_total = small_total[null_grad.shape[0] :, :shard_rows]
+    vector_total = vector_total.at[n_spatial + 5].add(bias_total[0])
+    vector_total = vector_total.at[n_spatial + 7].add(bias_total[1])
     return (
         output,
         video_grad.astype(jnp.bfloat16),
-        sum_seq(null_grad),
+        null_total,
         sum_seq(caption_weight_grad),
-        spatial_terms[0],
-        spatial_terms[1],
-        spatial_terms[2],
-        spatial_terms[3],
+        spatial_sums[2],
+        spatial_sums[3],
+        spatial_sums[0],
+        spatial_sums[1],
         vector_total[:n_spatial],
-        temporal_terms[0],
-        temporal_terms[1],
-        temporal_terms[2],
-        temporal_terms[3],
-        temporal_terms[4],
+        temporal_sums[2],
+        temporal_sums[3],
+        temporal_sums[0],
+        temporal_sums[1],
+        cross_sums[0],
         sum_seq(keyval_weight_grad),
-        temporal_terms[5],
+        cross_sums[1],
         vector_total[n_spatial:],
     )
 

time: 1640 us -> 1400 us (0.85)
  waiting for transfers between devices: 524 us -> 52.9 us
  Pallas kernels: 369 us -> 758 us
  starting transfers between devices: 103 us -> 29.1 us
  other arithmetic: 108 us -> 52.8 us
  matrix products: 217 us -> 184 us
  local copies, waits for them, and re-layouts: 268 us -> 296 us
  blocking collectives: 23.4 us -> 0 us
    pallas_call x0 -> x1, Pallas kernels: none -> 372 us  [scatter_products(): pl.pallas_call(functools.partial(scatter_kernel, pairs, full_pairs, place...]
    ppermute x49 -> x0, waiting for transfers between devices: 233 us -> none  [swap_sp(): lax.ppermute(v, 'sp', pairs)]
    ppermute x26 -> x3, waiting for transfers between devices: 214 us -> 5.28 us  [swap_seq(): lax.ppermute(v, 'seq', [(0, 1), (1, 0)])]
    convert_element_type x60 -> x1, other arithmetic: 61.8 us -> 3.07 us  [scatter_all(): done = done.astype(jnp.float32)]
    psum x1, waiting for transfers between devices: 53.9 us -> 0.01 us  [on_device(): caption_sum = lax.psum(project(text_rows, caption_weight), 'sp')]
    ppermute x49 -> x0, starting transfers between devices: 40.6 us -> none  [swap_sp(): lax.ppermute(v, 'sp', pairs)]
    squeeze x11 -> x2, local copies, waits for them, and re-layouts: 43.7 us -> 3.48 us  [quarter(): return done[pair, k // 2, k % 2]]
    dot_general x11 -> x0, matrix products: 38.6 us -> none  [scatter_grad(): lax.dot_general(left, right, (((0,), (0,)), ((), ())), preferred_element_...]
  transfers between devices with their start and end apart: 82 -> 9, of which waited for: 45 -> 4; matrix products, arithmetic and copies ran while one was open for 20% -> 17% of each run, Pallas kernels for 0% -> 28%
where the time goes in v3:
time: 1400 us; the launch traced here: 1390 us
  Pallas kernels  758 us (54%)
  local copies, waits for them, and re-layouts  296 us (21%)
  matrix products  184 us (13%)
  waiting for transfers between devices  52.9 us (4%)
  other arithmetic  52.8 us (4%)
  starting transfers between devices  29.1 us (2%)
  between operations  16.3 us (1%)
    pallas_call x1, Pallas kernels, gather_weights(): pl.pallas_call(functools.partial(gather_kernel, rounds, len(shards), len(...  386 us
    pallas_call x1, Pallas kernels, scatter_products(): pl.pallas_call(functools.partial(scatter_kernel, pairs, full_pairs, place...  372 us
    unnamed x398, local copies, waits for them, and re-layouts  72.8 us
    dot_general x12, matrix products, input_grad(): lax.dot_general(gradients, weight, (((gradients.ndim - 1,), (1,)), ((), (...  67.7 us
    dot_general x12, matrix products, project(): return jnp.dot(inputs, weight, preferred_element_type=jnp.float32)  67.1 us
  transfers between devices with their start and end apart: 9, of which 4 were waited for; matrix products, arithmetic and copies ran while one was open for 17% of the time, Pallas kernels for 28%

profile of v3, /device:TPU:0, one launch (start us, length us, event | category | flops | bytes accessed | tf_op | source)
XLA Modules:
  0.0 1388.5 jit_solution(9033827203552349165)
XLA Ops:
  22.6 386.1 %shard_map.332 = (bf16[2,2,2,2,72,3456]{5,4,3,2,1,0:T(8,128)(2,1)}, bf16[2,2,2,2,72,1152]{5,4,3,2,1,0:T(8,128)(2,1)S(1)}, bf16[2,2,2,2,72,4608]{5,4,3,2,1,0:T(8,...) custom-call(bf16[72,3456]{1,0:T(8,128)(2,1)S(1)} %copy-done.13, ...), custom_call_target="tpu_custom_call" | custom-call | bytes 74391552 | tf_op jit(solution)/shard_map/pallas_call | solution.py:251
  429.7 7.1 fusion.10
  436.8 8.4 reshape.611
  449.1 4.8 all-to-all-start
  502.0 4.9 fusion.138
  513.3 7.4 all-to-all-start.1
  523.4 6.8 fusion.28
  534.4 9.2 all-to-all-done.1
  554.2 10.7 multiply_convert_fusion.1
  575.5 7.9 reshape.622
  622.8 10.6 multiply_convert_fusion
  633.4 8.9 convert_reduce_fusion
  642.3 8.9 multiply_reduce_fusion.3
  651.3 9.0 fusion.66
  667.8 5.0 fusion.29
  680.3 5.0 convert_reduce_fusion.10
  702.2 5.5 convert_element_type.290
  707.7 6.6 multiply_reduce_fusion.10
  717.8 9.6 convert_reduce_fusion.1
  727.4 8.2 multiply_reduce_fusion.9
  744.8 6.9 all-to-all-start.2
  751.8 4.7 fusion.47
  769.5 6.2 convert_element_type.306
  867.2 6.4 all-to-all-start.3
  890.6 27.8 %all-to-all-done.3 = bf16[1,32,128,216]{3,1,0,2:T(8,128)(2,1)} async-done(((bf16[1,32,128,216]{3,1,0,2:T(8,128)(2,1)}), bf16[1,32,128,216]{3,1,0,2:T(8,128)(2,1)}, u32[]{:S(2)}, u32[]{:S(2)}) %all-to-all-start.3) | async-done | bytes 1769504 | tf_op jit(solution)/shard_map/all_to_all | solution.py:906
  923.4 5.2 reshape.640
  928.7 6.5 fusion.64
  938.0 10.6 all-reduce.8.cloned.1.call-done
  948.5 7.4 convert_reduce_fusion.5
  958.8 6.4 reshape_reshape_reshape.4
  974.3 371.9 %shard_map.333 = (bf16[7,4,8,72,1152]{4,3,2,1,0:T(8,128)(2,1)}, bf16[7,2,8,72,1152]{4,3,2,1,0:T(8,128)(2,1)}, bf16[7,2,4,72,1152]{4,3,2,1,0:T(8,128)(2,1)}, bf16...) custom-call(bf16[16,2,576,256]{3,2,1,0:T(8,128)(2,1)} %constant_dyna, ...), custom_call_target="tpu_custom_call" | custom-call | flops 10871635968 | bytes 21233664 | tf_op jit(solution)/shard_map/pallas_call | solution.py:686
  1374.0 5.3 collective-permute-done.1
  (643 shorter events, 376.3 us)
Async XLA Ops:
  7.2 422.5 %all-reduce.6.cloned.1.call-start = ((), (), s32[]{:S(2)}) async-start(), calls=%async_computation.4 | async-start | bytes 4423680 | tf_op jit(solution)/shard_map/psum | solution.py:1314
  22.6 394.0 %copy-start.175 = (s32[2,2]{1,0:T(2,128)S(1)}, s32[2,2]{1,0:T(2,128)}, u32[]{:S(2)}) copy-start(s32[2,2]{1,0:T(2,128)} %param.27) | copy-start | bytes 52
  22.6 394.0 %copy-start.25 = (bf16[2,16,8,1152]{3,2,1,0:T(8,128)(2,1)S(1)}, bf16[2,16,8,1152]{3,2,1,0:T(8,128)(2,1)}, u32[]{:S(2)}) copy-start(bf16[2,16,8,1152]{3,2,1,0:T(8,128)(2,1)} %param.25) | copy-start | bytes 1769476
  22.6 395.0 %copy-start.163 = (s32[2,16]{1,0:T(2,128)S(1)}, s32[2,16]{1,0:T(2,128)}, u32[]{:S(2)}) copy-start(s32[2,16]{1,0:T(2,128)} %param.26) | copy-start | bytes 388
  415.6 134.4 %copy-start.1 = (bf16[2,2,2,2,72,1152]{5,4,3,2,1,0:T(8,128)(2,1)}, bf16[2,2,2,2,72,1152]{5,4,3,2,1,0:T(8,128)(2,1)S(1)}, u32[]{:S(2)}) copy-start(bf16[2,2,2,2,72,1152]{5,4,3,2,1,0:T(8,128)(2,1)S(1)} %get-tuple-element.62) | copy-start | bytes 7962628
  449.1 13.0 copy-start.143
  449.1 15.9 %copy-start.142 = (f32[1,16,72]{2,1,0:T(8,128)S(1)}, f32[1,16,72]{2,1,0:T(8,128)}, u32[]{:S(2)}) copy-start(f32[1,16,72]{2,1,0:T(8,128)} %get-tuple-element.169) | copy-start | bytes 13828
  449.1 49.7 %all-to-all-start = ((bf16[16,32,8,216]{3,2,1,0:T(8,128)(2,1)}), bf16[16,32,8,216]{3,2,1,0:T(8,128)(2,1)}, u32[]{:S(2)}, u32[]{:S(2)}) async-start(bf16[16,32,8,216]{3,2,1,0:T(8,128)(2,1)} %bitcast.526), calls=%async_computation | async-start | bytes 4194304 | tf_op jit(solution)/shard_map/all_to_all | solution.py:912
  484.3 69.5 %copy-start.53 = (f32[2,16,1,1152]{3,1,2,0:T(8,128)}, f32[2,16,1,1152]{3,1,2,0:T(8,128)S(1)}, u32[]{:S(2)}) copy-start(f32[2,16,1,1152]{3,1,2,0:T(8,128)S(1)} %copy.465) | copy-start | bytes 442372
  513.3 30.4 %all-to-all-start.1 = ((bf16[1,32,128,72]{3,1,0,2:T(8,128)(2,1)}), bf16[1,32,128,72]{3,1,0,2:T(8,128)(2,1)}, u32[]{:S(2)}, u32[]{:S(2)}) async-start(bf16[1,32,128,72]{3,1,0,2:T(8,128)(2,1)} %copy.281), calls=%async_computation.1 | async-start | bytes 2097152 | tf_op jit(solution)/shard_map/all_to_all | solution.py:878
  553.5 11.5 copy-start.23
  553.5 11.5 copy-start.117
  553.8 11.2 copy-start.129
  553.8 11.2 copy-start.125
  553.8 11.2 slice-start
  554.2 10.8 copy-start.76
  554.2 10.8 copy-start.114
  554.2 10.8 copy-start.170
  554.2 10.8 slice-start.1
  554.2 10.8 slice-start.2
  622.0 11.3 slice-start.3
  622.6 10.7 copy-start.80
  622.8 10.6 slice-start.4
  622.8 10.6 slice-start.5
  633.4 17.9 %copy-start.61 = (bf16[2,16,8,4608]{3,2,1,0:T(8,128)(2,1)}, bf16[2,16,8,4608]{3,2,1,0:T(8,128)(2,1)S(1)}, u32[]{:S(2)}) copy-start(bf16[2,16,8,4608]{3,2,1,0:T(8,128)(2,1)S(1)} %get-tuple-element.195) | copy-start | bytes 7077892
  651.3 10.9 copy-start.8
  744.8 107.2 %all-to-all-start.2 = ((bf16[16,32,8,72]{3,2,1,0:T(8,128)(2,1)}), bf16[16,32,8,72]{3,2,1,0:T(8,128)(2,1)}, u32[]{:S(2)}, u32[]{:S(2)}) async-start(bf16[16,32,8,72]{3,2,1,0:T(8,128)(2,1)} %bitcast.97), calls=%async_computation.2 | async-start | bytes 2097152 | tf_op jit(solution)/shard_map/all_to_all | solution.py:923
  751.7 196.8 %all-reduce.8.cloned.1.call-start = ((), (), s32[]{:S(2)}) async-start(), calls=%async_computation.5 | async-start | bytes 4423680 | tf_op jit(solution)/shard_map/psum | solution.py:1141
  867.2 51.3 %all-to-all-start.3 = ((bf16[1,32,128,216]{3,1,0,2:T(8,128)(2,1)}), bf16[1,32,128,216]{3,1,0,2:T(8,128)(2,1)}, u32[]{:S(2)}, u32[]{:S(2)}) async-start(bf16[1,32,128,216]{3,1,0,2:T(8,128)(2,1)} %copy.311), calls=%async_computation.3 | async-start | bytes 4194304 | tf_op jit(solution)/shard_map/all_to_all | solution.py:906
  1355.1 14.2 %collective-permute-start = (bf16[122,256]{1,0:T(8,128)(2,1)S(1)}, bf16[122,256]{1,0:T(8,128)(2,1)S(1)}, u32[]{:S(2)}, u32[]{:S(2)}) collective-permute-start(bf16[122,256]{1,0:T(8,128)(2,1)S(1)} %pad_maximum_fusion.8), channel_id=1, source_target_pairs={{0,16},{16,0},{1,17},{17,1},{2,18},{18,2},{3,19},{19,3},{4,20},{20... | collective-permute-start | bytes 187400 | tf_op jit(solution)/shard_map/ppermute | solution.py:98
  1356.6 15.4 %collective-permute-start.2 = (bf16[72,2304]{1,0:T(8,128)(2,1)}, bf16[72,2304]{1,0:T(8,128)(2,1)}, u32[]{:S(2)}, u32[]{:S(2)}) collective-permute-start(bf16[72,2304]{1,0:T(8,128)(2,1)} %fusion.32), channel_id=1, source_target_pairs={{0,16},{16,0},{1,17},{17,1},{2,18},{18,2},{3,19},{19,3},{4,20},{20... | collective-permute-start | bytes 995336 | tf_op jit(solution)/shard_map/ppermute | solution.py:98
  1359.0 20.3 %collective-permute-start.1 = (bf16[256,1152]{1,0:T(8,128)(2,1)S(1)}, bf16[256,1152]{1,0:T(8,128)(2,1)}, u32[]{:S(2)}, u32[]{:S(2)}) collective-permute-start(bf16[256,1152]{1,0:T(8,128)(2,1)S(1)} %convolution_convert_fusion.4), channel_id=1, source_target_pairs={{0,16},{16,0},{1,17},{17,1},{2,18},{18,2},{3,19},{19,3},{4,20},{20... | collective-permute-start | bytes 1769480 | tf_op jit(solution)/shard_map/ppermute | solution.py:98
  (161 other events, 551.8 us)
Sparse Core Ops, SparseCore 0:
  12.4 156.2 all-reduce.5
  831.1 117.4 all-reduce.7

commit v4 on v3

--- a/solution.py
+++ b/solution.py
@@ -217,16 +217,16 @@
                     local.append(copy)
             lags = list(range(count - 1)) + [count - 1, count + 1]
             for time in range(len(rounds) + lags[-1]):
+                if time == 1:
+                    for copy in local:
+                        copy.wait()
+                if 0 < time < count:
+                    small[-1].wait_recv()
+                    small.append(small_step(time))
                 for stage, lag in enumerate(lags):
                     number = time - lag
                     if not 0 <= number < len(rounds):
                         continue
-                    if stage == 0 and 0 < number < count:
-                        if number == 1:
-                            for copy in local:
-                                copy.wait()
-                        small[-1].wait_recv()
-                        small.append(small_step(number))
                     if stage:
                         for copy in copies[number, stage - 1]:
                             copy.wait_recv()
@@ -372,13 +372,16 @@
     ).astype(jnp.float32)
 
 
-def scatter_kernel(pairs, full_pairs, places, left, right, small, *refs):
+def scatter_kernel(pairs, full_pairs, sources, n_in, *refs):
+    factors, small = refs[:n_in], refs[n_in]
+    refs = refs[n_in + 1 :]
     came, out, small_out = refs[:5], refs[5], refs[6]
     scratch = refs[7:]
-    left_in, right_in, product, core_send, core_own, loaded = scratch[:6]
-    sends, keeps = scratch[6:11], scratch[11:15]
-    in_sem, load_sem, out_sem, core_send_sem, core_recv_sem, send_sem, recv_sem = scratch[15:22]
-    small_sum, small_came, small_send, small_recv = scratch[22:]
+    left_in, right_in, product, core_both, loaded = scratch[:5]
+    sends, keeps = scratch[5:10], scratch[10:14]
+    in_sem, load_sem, out_sem, core_send_sem, core_recv_sem, send_sem, recv_sem = scratch[14:21]
+    small_sum, small_came, small_send, small_recv = scratch[21:]
+    core_own, core_send = core_both.at[0], core_both.at[1]
     me = lax.axis_index("sp")
     plane = lax.axis_index("seq")
 
@@ -448,58 +451,73 @@
     def has(pair, chunk):
         return pair < (pairs if chunk == 0 else full_pairs)
 
-    def inputs(pair, chunk, side, slot):
-        of_left, of_right = places(pair, 2 * chunk + half_of(side))
-        return (
-            pltpu.make_async_copy(left.at[of_left], left_in.at[slot], in_sem.at[slot, 0]),
-            pltpu.make_async_copy(right.at[of_right], right_in.at[slot], in_sem.at[slot, 1]),
-        )
-
-    def start_inputs(pair, chunk, side, slot):
-        for copy in inputs(pair, chunk, side, slot):
-            copy.start()
+    width = out.shape[4]
+
+    def start_inputs(q, slot):
+        for number, source in enumerate(sources):
+
+            @pl.when(q == number)
+            def _():
+                for place, target, k in ((source[0], left_in, 0), (source[1], right_in, 1)):
+                    pltpu.make_async_copy(
+                        factors[place[0]].at[:, pl.ds(place[1], width)],
+                        target.at[slot],
+                        in_sem.at[slot, k],
+                    ).start()
+
+    def wait_inputs(slot):
+        for target, k in ((left_in, 0), (right_in, 1)):
+            pltpu.make_async_copy(
+                factors[0].at[:, pl.ds(0, width)], target.at[slot], in_sem.at[slot, k]
+            ).wait()
 
     def products(pair):
-        start_inputs(pair, 0, 0, 0)
+        start_inputs(4 * pair, 0)
+        for chunk in (0, 1):
+
+            @pl.when((pair > 0) & has(pair - 1, chunk))
+            def _():
+                for side in (0, 1):
+                    core_copy(pair - 1, chunk, side).wait_send()
+
+        last = pair // 6
+        shrink = (2 - pair % 3) // 2 * (1 - last)
+
+        def one(j, carry):
+            slot = j % 2
+
+            @pl.when(j + 1 < 4 - 2 * last)
+            def _():
+                start_inputs(4 * pair + j + 1, 1 - slot)
+
+            wait_inputs(slot)
+            product[...] = lax.dot_general(
+                left_in[slot],
+                right_in[slot],
+                (((0,), (0,)), ((), ())),
+                preferred_element_type=jnp.float32,
+            )
+
+            def store(i, carry):
+                owner = shrink * (4 * j + i // 4) + (1 - shrink) * i
+                quarter = shrink * (i % 4) + (1 - shrink) * j
+                number = quarter // 2 * 2 + (quarter % 2 + plane) % 2
+                first = pl.multiple_of(i * rows, 8)
+                core_both[(owner + core) % 2, number, owner // 2] = product[
+                    pl.ds(first, rows), :
+                ].astype(jnp.bfloat16)
+                return carry
+
+            lax.fori_loop(0, 16, store, 0)
+            return carry
+
+        lax.fori_loop(0, 4 - 2 * last, one, 0)
         for chunk in (0, 1):
 
             @pl.when(has(pair, chunk))
             def _():
                 for side in (0, 1):
-                    number = 2 * chunk + side
-
-                    if side == 0:
-                        start_inputs(pair, chunk, 1, 1)
-                    elif chunk == 0:
-
-                        @pl.when(has(pair, 1))
-                        def _():
-                            start_inputs(pair, 1, 0, 0)
-
-                    for copy in inputs(pair, chunk, side, side):
-                        copy.wait()
-
-                    @pl.when((pair > 0))
-                    def _():
-                        core_copy(pair, chunk, side).wait_send()
-
-                    for which, target in ((1 - core, core_send), (core, core_own)):
-                        product[...] = jnp.dot(
-                            left_in[side, which],
-                            right_in[side],
-                            preferred_element_type=jnp.float32,
-                        )
-
-                        def store(block, carry):
-                            first = pl.multiple_of(block * rows, 8)
-                            target[number, block] = product[pl.ds(first, rows), :].astype(
-                                jnp.bfloat16
-                            )
-                            return carry
-
-                        lax.fori_loop(0, 8, store, 0)
-                        if target is core_send:
-                            core_copy(pair, chunk, side).start()
+                    core_copy(pair, chunk, side).start()
 
     def add(a, b):
         return (a.astype(jnp.float32) + b.astype(jnp.float32)).astype(jnp.bfloat16)
@@ -649,8 +667,9 @@
         small_copy(stage).wait_send()
     for chunk in (0, 1):
         mine = pairs if chunk == 0 else full_pairs
-        for side in (0, 1):
-            core_copy(mine - 1, chunk, side).wait_send()
+        if mine == pairs:
+            for side in (0, 1):
+                core_copy(mine - 1, chunk, side).wait_send()
         for pair in range(max(mine - 2, 0), mine):
             out_copy(pair, chunk).wait()
             for stage in range(1, 6):
@@ -659,10 +678,9 @@
             stage_copy(5, pair, chunk).wait_recv()
 
 
-def scatter_products(left, right, small, pairs, full_pairs, places, collective_id):
-    depth, tokens = left.shape[2:]
-    width = right.shape[2]
-    rows = depth // 8
+def scatter_products(factors, sources, small, pairs, full_pairs, rows, width, collective_id):
+    tokens = factors[0].shape[0]
+    depth = 16 * rows
     low = jnp.bfloat16
 
     def blocks(*lead):
@@ -684,16 +702,15 @@
     dma = pltpu.SemaphoreType.DMA
     whole = pl.BlockSpec(memory_space=pltpu.VMEM)
     *_, out, total = pl.pallas_call(
-        functools.partial(scatter_kernel, pairs, full_pairs, places),
+        functools.partial(scatter_kernel, pairs, full_pairs, sources, len(factors)),
         out_shape=hbm + [jax.ShapeDtypeStruct(small.shape, small.dtype)],
-        in_specs=[any_space] * 2 + [whole],
+        in_specs=[any_space] * len(factors) + [whole],
         out_specs=[any_space] * len(hbm) + [whole],
         scratch_shapes=[
-            pltpu.VMEM((2, 2, depth, tokens), low),
+            pltpu.VMEM((2, tokens, width), low),
             pltpu.VMEM((2, tokens, width), low),
             pltpu.VMEM((depth, width), jnp.float32),
-            vmem(4, 8),
-            vmem(4, 8),
+            vmem(2, 4, 8),
             vmem(2, 8),
             vmem(2, 2, 8),
             vmem(2, 2, 4),
@@ -720,29 +737,12 @@
             collective_id=collective_id, has_side_effects=True, vmem_limit_bytes=58 << 20
         ),
         cost_estimate=pl.CostEstimate(
-            flops=4 * left.shape[0] * depth * tokens * width,
-            bytes_accessed=2 * left.size + 2 * right.size,
+            flops=2 * len(sources) * depth * tokens * width,
+            bytes_accessed=16 * len(sources) * depth * width,
             transcendentals=0,
         ),
-    )(left, right, small)
+    )(*factors, small)
     return out, total
-
-
-def core_rows(inputs):
-    flat = inputs.reshape(-1, inputs.shape[-1])
-    size = lax.axis_size("sp")
-    rows = flat.shape[1] // size
-    grouped = flat.T.reshape(size // 2, 2, rows, flat.shape[0])
-    return jnp.swapaxes(grouped, 0, 1).reshape(2, size // 2 * rows, flat.shape[0])
-
-
-def quarter_rows(inputs):
-    flat = inputs.reshape(-1, inputs.shape[-1])
-    size = lax.axis_size("sp")
-    rows = flat.shape[1] // size // 4
-    grouped = flat.T.reshape(size // 2, 2, 4, rows, flat.shape[0])
-    moved = jnp.transpose(grouped, (2, 1, 0, 3, 4))
-    return moved.reshape(4, 2, size // 2 * rows, flat.shape[0])
 
 
 def token_rows(gradients):
@@ -760,32 +760,25 @@
         ]
         last = [scatter_grad(*pair, False, False, links) for pair in terms[2]]
         return blocks[0], blocks[1], last, lax.psum(small, ("seq", "sp"))
-    lefts, rights = [], []
+    factors, sources = [], []
+
+    def add_factors(pair):
+        factors.extend(token_rows(member) for member in pair)
+        return len(factors) - 2, len(factors) - 1
+
     for expand, shrink, qkv, out in (terms[1], terms[0]):
-        lefts.append(quarter_rows(shrink[0]))
-        lefts += [core_rows(member[0])[None] for member in (expand, qkv, out)]
-        rights.append(token_rows(shrink[1])[None])
-        for member, count in ((expand, 4), (qkv, 3)):
-            cut = token_rows(member[1])
-            rights.append(jnp.swapaxes(cut.reshape(cut.shape[0], count, -1), 0, 1))
-        rights.append(token_rows(out[1])[None])
-    lefts += [core_rows(pair[0])[None] for pair in terms[2]]
-    rights += [token_rows(pair[1])[None] for pair in terms[2]]
-
-    def places(pair, k):
-        block = pair // 3
-        kind = pair % 3
-        tail = block // 2
-        shrink = (2 - kind) // 2 * (1 - tail)
-        wide = kind // 2
-        expand = (1 - wide) * (kind % 2)
-        of_left = 7 * block + (shrink + tail) * k + expand * 4 + wide * (5 + k // 3)
-        of_right = 9 * block + tail * k + expand * (1 + k) + wide * (5 + k)
-        return of_left, of_right
-
-    left = jnp.concatenate(lefts, axis=0)
-    right = jnp.concatenate(rights, axis=0)
-    done, total = scatter_products(left, right, small, 7, 6, places, 1)
+        left, right = add_factors(shrink)
+        sources += [((left, j * D), (right, 0)) for j in range(4)]
+        left, right = add_factors(expand)
+        sources += [((left, 0), (right, j * D)) for j in range(4)]
+        left, right = add_factors(qkv)
+        sources += [((left, 0), (right, j * D)) for j in range(3)]
+        left, right = add_factors(out)
+        sources.append(((left, 0), (right, 0)))
+    for pair in terms[2]:
+        left, right = add_factors(pair)
+        sources.append(((left, 0), (right, 0)))
+    done, total = scatter_products(factors, sources, small, 7, 6, D // size, D, 1)
     done = done.astype(jnp.float32)
 
     def quarter(pair, k):
@@ -1253,7 +1246,6 @@
         cross_query,
         cross_keyval,
         cross_out,
-        temporal_expand,
     ]
 
     def rounds_of(rows):
@@ -1269,11 +1261,9 @@
         return [
             block_round(0, 1),
             expand_round(2),
-            rows_round(9, rows),
+            rows_round(8, rows),
             block_round(3, 4),
             columns_round((5, 0, third), (6, 0, third), (6, third, third), (7, 0, third)),
-            expand_round(8),
-            rows_round(10, rows),
         ]
 
     (
@@ -1285,17 +1275,20 @@
         full_cq,
         full_ckv,
         full_cout,
-        full_texp,
         full_sshr,
-        full_tshr,
         all_vectors,
     ) = gather_all(
-        [spatial_shrink, temporal_shrink],
+        [spatial_shrink],
         wide,
         jnp.concatenate([spatial_vectors, temporal_vectors], axis=0),
         rounds_of,
         0,
     )
+    full_sqkv, expand_shard, shrink_shard = lax.optimization_barrier(
+        (full_sqkv, temporal_expand, temporal_shrink)
+    )
+    full_texp = lax.all_gather(expand_shard, "sp", axis=0, tiled=True)
+    full_tshr = lax.all_gather(shrink_shard, "sp", axis=0, tiled=True)
     n_spatial = spatial_vectors.shape[0]
     spatial = (full_sqkv, full_sout, full_sexp, full_sshr, all_vectors[:n_spatial])
     temporal = (
@@ -1311,7 +1304,7 @@
     dropped = (drop_mask > 0).astype(jnp.float32)
     text_local = jnp.where(drop_mask[:, :, None, None] > 0, null_caption[None, None], captions)
     text_rows = text_local.reshape(groups, CLIPS * CAP, -1)
-    caption_sum = lax.psum(project(text_rows, caption_weight), "sp")
+    caption_sum = lax.psum(project(text_rows, caption_weight).astype(jnp.float32), "sp")
     caption_sum, first = lax.optimization_barrier((caption_sum, spatial[0]))
     spatial = (first, *spatial[1:])
     frame_mod = frame_modulation(segment_ids, timesteps).reshape(groups, frames, 6, D)
@@ -1348,7 +1341,7 @@
         jnp.concatenate([spatial_terms[4], temporal_terms[6]], axis=0),
     )
     vector_total = lax.dynamic_slice_in_dim(vector_total, first_row, shard_rows, 1)
-    keyval_grad, video_grad = lax.optimization_barrier((keyval_grad, video_grad))
+    keyval_grad, vector_total = lax.optimization_barrier((keyval_grad, vector_total))
     context_grad = input_grad(keyval_grad, temporal[5]).astype(jnp.bfloat16)
     local_context = lax.dynamic_slice_in_dim(context, first_row, shard_rows, 2)
     keyval_weight_grad = weight_grad(local_context, keyval_grad)

time: 1400 us -> 1280 us (0.914)
  local copies, waits for them, and re-layouts: 296 us -> 194 us
  Pallas kernels: 758 us -> 699 us
  blocking collectives: 0 us -> 31.4 us
  waiting for transfers between devices: 52.9 us -> 77.6 us
    pallas_call x1, Pallas kernels: 386 us -> 303 us  [gather_weights(): pl.pallas_call(functools.partial(gather_kernel, rounds, len(shards), len(...]
    all_to_all x1, waiting for transfers between devices: 0.01 us -> 40.2 us  [pair_attention(): lax.all_to_all(to_pairs(shaped), 'sp', split_axis=0, concat_axis=2, tiled...]
    all_to_all x0 -> x1, blocking collectives: none -> 31.4 us  [pair_attention_back(): lax.all_to_all(to_pairs(grad_shaped), 'sp', split_axis=0, concat_axis=2,...]
    unnamed x398 -> x350, local copies, waits for them, and re-layouts: 72.8 us -> 44.7 us
    transpose x13 -> x0, local copies, waits for them, and re-layouts: 25.4 us -> none  [the longest x8 13.4 us: core_rows(): jnp.swapaxes(grouped, 0, 1).reshape(2, size // 2 * rows, flat.shape[0])]
    pallas_call x1, Pallas kernels: 372 us -> 396 us  [scatter_products(): pl.pallas_call(functools.partial(scatter_kernel, pairs, full_pairs, sourc...]
    all_to_all x1, waiting for transfers between devices: 27.8 us -> 8.89 us  [pair_backward(): lax.all_to_all(gradients, 'sp', split_axis=2, concat_axis=0, tiled=True)]
    reshape x7 -> x0, local copies, waits for them, and re-layouts: 17.3 us -> none  [the longest x5 8.78 us: core_rows(): flat = inputs.reshape(-1, inputs.shape[-1])]
  transfers between devices with their start and end apart: 9 -> 10, of which waited for: 4 -> 4; matrix products, arithmetic and copies ran while one was open for 17% -> 20% of each run, Pallas kernels for 28% -> 55%
where the time goes in v4:
time: 1280 us; the launch traced here: 1270 us
  Pallas kernels  699 us (55%)
  local copies, waits for them, and re-layouts  194 us (15%)
  matrix products  180 us (14%)
  waiting for transfers between devices  77.6 us (6%)
  other arithmetic  41.6 us (3%)
  starting transfers between devices  33.7 us (3%)
  blocking collectives  31.4 us (2%)
  between operations  16.2 us (1%)
    pallas_call x1, Pallas kernels, scatter_products(): pl.pallas_call(functools.partial(scatter_kernel, pairs, full_pairs, sourc...  396 us
    pallas_call x1, Pallas kernels, gather_weights(): pl.pallas_call(functools.partial(gather_kernel, rounds, len(shards), len(...  303 us
    dot_general x12, matrix products, project(): return jnp.dot(inputs, weight, preferred_element_type=jnp.float32)  67.6 us
    dot_general x12, matrix products, input_grad(): lax.dot_general(gradients, weight, (((gradients.ndim - 1,), (1,)), ((), (...  67.4 us
    unnamed x350, local copies, waits for them, and re-layouts  44.7 us
    all_to_all x1, waiting for transfers between devices, pair_attention(): lax.all_to_all(to_pairs(shaped), 'sp', split_axis=0, concat_axis=2, tiled...  40.2 us
    all_to_all x1, blocking collectives, pair_attention_back(): lax.all_to_all(to_pairs(grad_shaped), 'sp', split_axis=0, concat_axis=2,...  31.4 us
  transfers between devices with their start and end apart: 10, of which 4 were waited for; matrix products, arithmetic and copies ran while one was open for 20% of the time, Pallas kernels for 55%

profile of v4, /device:TPU:0, one launch (start us, length us, event | category | flops | bytes accessed | tf_op | source)
XLA Modules:
  0.0 1273.1 jit_solution(10538631422463742745)
XLA Ops:
  20.2 302.8 %shard_map.332 = (bf16[2,2,2,2,72,3456]{5,4,3,2,1,0:T(8,128)(2,1)}, bf16[2,2,2,2,72,1152]{5,4,3,2,1,0:T(8,128)(2,1)S(1)}, bf16[2,2,2,2,72,4608]{5,4,3,2,1,0:T(8,...) custom-call(bf16[72,3456]{1,0:T(8,128)(2,1)S(1)} %copy-done.11, ...), custom_call_target="tpu_custom_call" | custom-call | bytes 53157888 | tf_op jit(solution)/shard_map/pallas_call | solution.py:251
  345.2 7.1 fusion.21
  352.3 8.5 reshape.586
  364.6 4.9 all-to-all-start
  402.9 40.2 %all-to-all-done = bf16[16,32,8,216]{3,2,1,0:T(8,128)(2,1)} async-done(((bf16[16,32,8,216]{3,2,1,0:T(8,128)(2,1)}), bf16[16,32,8,216]{3,2,1,0:T(8,128)(2,1)}, u32[]{:S(2)}, u32[]{:S(2)}) %all-to-all-start) | async-done | bytes 1769504 | tf_op jit(solution)/shard_map/all_to_all | solution.py:905
  446.3 4.9 fusion.154
  457.5 18.6 %all-to-all-start.1 = ((bf16[1,32,128,72]{3,1,0,2:T(8,128)(2,1)}), bf16[1,32,128,72]{3,1,0,2:T(8,128)(2,1)}, u32[]{:S(2)}, u32[]{:S(2)}) async-start(bf16[1,32,128,72]{3,1,0,2:T(8,128)(2,1)} %copy.167), calls=%async_computation.1 | async-start | bytes 2097152 | tf_op jit(solution)/shard_map/all_to_all | solution.py:871
  478.9 6.8 fusion.41
  489.8 21.6 %all-to-all-done.1 = bf16[1,32,128,72]{3,1,0,2:T(8,128)(2,1)} async-done(((bf16[1,32,128,72]{3,1,0,2:T(8,128)(2,1)}), bf16[1,32,128,72]{3,1,0,2:T(8,128)(2,1)}, u32[]{:S(2)}, u32[]{:S(2)}) %all-to-all-start.1) | async-done | bytes 589856 | tf_op jit(solution)/shard_map/all_to_all | solution.py:871
  522.5 10.9 multiply_convert_fusion.1
  533.5 4.4 fusion.147
  544.0 7.9 reshape.597
  593.6 10.9 multiply_convert_fusion
  604.5 9.6 convert_reduce_fusion
  614.1 8.9 multiply_reduce_fusion.3
  623.1 9.1 fusion.82
  639.7 4.9 fusion.42
  652.3 4.5 convert_reduce_fusion.10
  673.6 5.5 convert_element_type.289
  679.1 6.6 multiply_reduce_fusion.10
  688.4 9.0 convert_reduce_fusion.1
  697.5 8.2 multiply_reduce_fusion.9
  712.7 31.4 %all_to_all.63 = bf16[16,32,8,72]{3,2,1,0:T(8,128)(2,1)S(1)} all-to-all(bf16[16,32,8,72]{3,2,1,0:T(8,128)(2,1)S(1)} %bitcast.475), channel_id=1, replica_groups=mesh['seq'=2,'sp'=16] {'sp'}, dimensions={0} | all-to-all | bytes 1179648 | tf_op jit(solution)/shard_map/all_to_all | solution.py:916
  751.7 5.2 all-to-all-start.3
  769.4 4.7 convert_element_type.297.refs_5_
  791.2 8.9 all-to-all-done.3
  804.1 4.9 reshape_reshape.20.refs_13_
  809.0 4.7 reshape.613
  814.3 6.6 fusion.80
  824.4 395.8 %shard_map.333 = (bf16[7,4,8,72,1152]{4,3,2,1,0:T(8,128)(2,1)}, bf16[7,2,8,72,1152]{4,3,2,1,0:T(8,128)(2,1)}, bf16[7,2,4,72,1152]{4,3,2,1,0:T(8,128)(2,1)}, bf16...) custom-call(bf16[256,4608]{1,0:T(8,128)(2,1)} %bitcast.534, ...), custom_call_target="tpu_custom_call" | custom-call | flops 17666408448 | bytes 552075264 | tf_op jit(solution)/shard_map/pallas_call | solution.py:704
  1221.1 7.4 convert_reduce_fusion.5
  1257.8 6.3 collective-permute-done.1
  (575 shorter events, 265.3 us)
Async XLA Ops:
  7.2 337.9 %all-reduce.6.cloned.1.call-start = ((), (), s32[]{:S(2)}) async-start(), calls=%async_computation.4 | async-start | bytes 4423680 | tf_op jit(solution)/shard_map/psum | solution.py:1307
  12.1 581.4 %all-gather.3.cloned.1.call-start = ((), (), s32[]{:S(2)}) async-start(), calls=%async_computation.5 | async-start | bytes 11280384 | tf_op jit(solution)/shard_map/all_gather | solution.py:1290
  329.9 188.2 %copy-start.1 = (bf16[2,2,2,2,72,1152]{5,4,3,2,1,0:T(8,128)(2,1)}, bf16[2,2,2,2,72,1152]{5,4,3,2,1,0:T(8,128)(2,1)S(1)}, u32[]{:S(2)}) copy-start(bf16[2,2,2,2,72,1152]{5,4,3,2,1,0:T(8,128)(2,1)S(1)} %get-tuple-element.64) | copy-start | bytes 7962628
  329.9 274.6 %all-gather.5.cloned.1.call-start = ((), (), s32[]{:S(2)}) async-start(), calls=%async_computation.6 | async-start | bytes 11280384 | tf_op jit(solution)/shard_map/all_gather | solution.py:1291
  364.6 78.5 %all-to-all-start = ((bf16[16,32,8,216]{3,2,1,0:T(8,128)(2,1)}), bf16[16,32,8,216]{3,2,1,0:T(8,128)(2,1)}, u32[]{:S(2)}, u32[]{:S(2)}) async-start(bf16[16,32,8,216]{3,2,1,0:T(8,128)(2,1)} %bitcast.467), calls=%async_computation | async-start | bytes 4194304 | tf_op jit(solution)/shard_map/all_to_all | solution.py:905
  387.7 12.2 copy-start.143
  387.7 13.6 %copy-start.37 = (bf16[2,16,8,1152]{3,2,1,0:T(8,128)(2,1)S(1)}, bf16[2,16,8,1152]{3,2,1,0:T(8,128)(2,1)}, u32[]{:S(2)}) copy-start(bf16[2,16,8,1152]{3,2,1,0:T(8,128)(2,1)} %param.45) | copy-start | bytes 1769476
  388.7 12.6 copy-start.87
  396.7 125.1 %copy-start.48 = (f32[2,16,1,1152]{3,1,2,0:T(8,128)}, f32[2,16,1,1152]{3,1,2,0:T(8,128)S(1)}, u32[]{:S(2)}) copy-start(f32[2,16,1,1152]{3,1,2,0:T(8,128)S(1)} %copy.323) | copy-start | bytes 442372
  457.5 53.9 %all-to-all-start.1 = ((bf16[1,32,128,72]{3,1,0,2:T(8,128)(2,1)}), bf16[1,32,128,72]{3,1,0,2:T(8,128)(2,1)}, u32[]{:S(2)}, u32[]{:S(2)}) async-start(bf16[1,32,128,72]{3,1,0,2:T(8,128)(2,1)} %copy.167), calls=%async_computation.1 | async-start | bytes 2097152 | tf_op jit(solution)/shard_map/all_to_all | solution.py:871
  521.5 11.9 copy-start.21
  521.8 11.6 slice-start
  522.2 11.2 copy-start.89
  522.5 10.9 copy-start.95
  522.5 10.9 copy-start.153
  522.5 10.9 slice-start.1
  522.5 10.9 slice-start.2
  604.4 9.6 copy-start.30
  604.5 9.6 copy-start.123
  623.1 10.9 copy-start.8
  688.4 9.1 copy-start.93
  688.4 9.1 copy-start.22
  688.4 9.1 copy-start.49
  688.4 9.1 copy-start.99
  710.6 33.6 %copy-start.141 = (f32[32,128]{1,0:T(8,128)S(1)}, f32[32,128]{1,0:T(8,128)}, u32[]{:S(2)}) copy-start(f32[32,128]{1,0:T(8,128)} %get-tuple-element.183) | copy-start | bytes 49156
  712.4 31.8 %copy-start.33 = (bf16[1,32,128,216]{3,2,1,0:T(8,128)(2,1)S(1)}, bf16[1,32,128,216]{3,2,1,0:T(8,128)(2,1)}, u32[]{:S(2)}) copy-start(bf16[1,32,128,216]{3,2,1,0:T(8,128)(2,1)} %copy_bitcast_fusion.1) | copy-start | bytes 5308420
  712.4 31.7 %copy-start.56 = (f32[32,128,128]{1,2,0:T(8,128)S(1)}, f32[32,128,128]{1,2,0:T(8,128)}, u32[]{:S(2)}) copy-start(f32[32,128,128]{1,2,0:T(8,128)} %get-tuple-element.184) | copy-start | bytes 6291460
  751.7 48.4 %all-to-all-start.3 = ((bf16[1,32,128,216]{3,1,0,2:T(8,128)(2,1)}), bf16[1,32,128,216]{3,1,0,2:T(8,128)(2,1)}, u32[]{:S(2)}, u32[]{:S(2)}) async-start(bf16[1,32,128,216]{3,1,0,2:T(8,128)(2,1)} %copy.194), calls=%async_computation.3 | async-start | bytes 4194304 | tf_op jit(solution)/shard_map/all_to_all | solution.py:899
  756.8 464.2 %all-reduce.8.cloned.1.call-start = ((), (), s32[]{:S(2)}) async-start(), calls=%async_computation.7 | async-start | bytes 4423680 | tf_op jit(solution)/shard_map/psum | solution.py:1134
  1239.5 14.4 %collective-permute-start = (bf16[122,256]{1,0:T(8,128)(2,1)S(1)}, bf16[122,256]{1,0:T(8,128)(2,1)S(1)}, u32[]{:S(2)}, u32[]{:S(2)}) collective-permute-start(bf16[122,256]{1,0:T(8,128)(2,1)S(1)} %pad_maximum_fusion.8), channel_id=1, source_target_pairs={{0,16},{16,0},{1,17},{17,1},{2,18},{18,2},{3,19},{19,3},{4,20},{20... | collective-permute-start | bytes 187400 | tf_op jit(solution)/shard_map/ppermute | solution.py:98
  1242.0 13.9 %collective-permute-start.2 = (bf16[72,2304]{1,0:T(8,128)(2,1)S(1)}, bf16[72,2304]{1,0:T(8,128)(2,1)}, u32[]{:S(2)}, u32[]{:S(2)}) collective-permute-start(bf16[72,2304]{1,0:T(8,128)(2,1)S(1)} %copy-done.75), channel_id=1, source_target_pairs={{0,16},{16,0},{1,17},{17,1},{2,18},{18,2},{3,19},{19,3},{4,20},{20... | collective-permute-start | bytes 995336 | tf_op jit(solution)/shard_map/ppermute | solution.py:98
  1243.9 20.2 %collective-permute-start.1 = (bf16[256,1152]{1,0:T(8,128)(2,1)S(1)}, bf16[256,1152]{1,0:T(8,128)(2,1)}, u32[]{:S(2)}, u32[]{:S(2)}) collective-permute-start(bf16[256,1152]{1,0:T(8,128)(2,1)S(1)} %convolution_convert_fusion.4), channel_id=1, source_target_pairs={{0,16},{16,0},{1,17},{17,1},{2,18},{18,2},{3,19},{19,3},{4,20},{20... | collective-permute-start | bytes 1769480 | tf_op jit(solution)/shard_map/ppermute | solution.py:98
  (147 other events, 560.5 us)
Sparse Core Ops, SparseCore 0:
  12.2 155.0 all-reduce.5
  330.0 127.9 all-gather.2
  460.3 104.1 all-gather.4
  783.8 110.3 all-reduce.7

commit v5 on v4

--- a/solution.py
+++ b/solution.py
@@ -156,9 +156,17 @@
                 return chunk[1 - own_half]
 
             def step(number, stage):
-                first, second = rounds[number]
+                (first, second), late = rounds[number]
                 lead = stage_places(min(stage, count - 2))
-                if stage < count - 2:
+                four = [piece for chunk in (first, second) for piece in (own(chunk), other(chunk))]
+                if late and stage < count:
+                    partner = [flip(1), across, *[flip(bit) for bit in range(count - 1, 1, -1)]][stage]
+                    moves = [(piece, partner) for piece in (four if stage > 1 else four[::2])]
+                    lead = tuple(
+                        slice(None) if d < stage - 2 or (d == count - 2 and stage) else place[d]
+                        for d in range(count)
+                    )
+                elif stage < count - 2:
                     moves = [(own(first), flip(count - 1 - stage)), (own(second), flip(count - 1 - stage))]
                 elif stage == count - 2:
                     moves = [(own(first), flip(1)), (own(second), across)]
@@ -169,15 +177,11 @@
                         (other(second), flip(1)),
                     ]
                 else:
-                    moves = [
-                        (piece, flip(0))
-                        for chunk in (first, second)
-                        for piece in (own(chunk), other(chunk))
-                    ]
+                    moves = [(piece, flip(0)) for piece in four]
                 copies = []
                 for slot, (piece, partner) in enumerate(moves):
                     places = lead
-                    if stage == count - 1 and partner is across or stage == count:
+                    if not late and stage == count - 1 and partner is across or stage == count:
                         places = stage_places(count - 1)
                     target = part(outs[piece[0]], places, piece)
                     source = target
@@ -205,7 +209,7 @@
                 pltpu.make_async_copy(shards[-1], outs[-1].at[stage_places(0)], small_local)
             ]
             local[0].start()
-            for number, pair in enumerate(rounds):
+            for number, (pair, late) in enumerate(rounds):
                 for slot, chunk in enumerate(pair):
                     piece = own(chunk)
                     copy = pltpu.make_async_copy(
@@ -215,22 +219,25 @@
                     )
                     copy.start()
                     local.append(copy)
-            lags = list(range(count - 1)) + [count - 1, count + 1]
-            for time in range(len(rounds) + lags[-1]):
+            lags = {
+                False: [*range(count), count + 1],
+                True: [*range(count - 1), count, count + 2],
+            }
+            for time in range(len(rounds) + count + 2):
                 if time == 1:
                     for copy in local:
                         copy.wait()
                 if 0 < time < count:
                     small[-1].wait_recv()
                     small.append(small_step(time))
-                for stage, lag in enumerate(lags):
-                    number = time - lag
-                    if not 0 <= number < len(rounds):
-                        continue
-                    if stage:
-                        for copy in copies[number, stage - 1]:
-                            copy.wait_recv()
-                    copies[number, stage] = step(number, stage)
+                for stage in range(count + 1):
+                    for number, (_, late) in enumerate(rounds):
+                        if number != time - lags[late][stage]:
+                            continue
+                        if stage:
+                            for copy in copies[number, stage - 1]:
+                                copy.wait_recv()
+                        copies[number, stage] = step(number, stage)
             small[-1].wait_recv()
             for copy in small:
                 copy.wait_send()
@@ -272,9 +279,9 @@
     return full + [small.reshape(small.shape[0], -1)]
 
 
-def columns_round(*quarters):
+def columns_round(*quarters, late=False):
     pieces = [(weight, None, (first, width)) for weight, first, width in quarters]
-    return ((pieces[0], pieces[2]), (pieces[1], pieces[3]))
+    return ((pieces[0], pieces[2]), (pieces[1], pieces[3])), late
 
 
 def rows_round(weight, rows):
@@ -282,7 +289,7 @@
     return (
         ((weight, (0, 0, cut), None), (weight, (1, 0, cut), None)),
         ((weight, (0, cut, rows - cut), None), (weight, (1, cut, rows - cut), None)),
-    )
+    ), False
 
 
 def gather_all(tall, wide, small, rounds_of, collective_id):
@@ -372,7 +379,7 @@
     ).astype(jnp.float32)
 
 
-def scatter_kernel(pairs, full_pairs, sources, n_in, *refs):
+def scatter_kernel(pairs, full_pairs, shrink_pairs, late_pairs, sources, n_in, *refs):
     factors, small = refs[:n_in], refs[n_in]
     refs = refs[n_in + 1 :]
     came, out, small_out = refs[:5], refs[5], refs[6]
@@ -402,6 +409,9 @@
         )
     pl.semaphore_wait(barrier, len(partners))
 
+    def among(pair, chosen):
+        return sum([1 // (1 + (pair - p) * (pair - p)) for p in chosen], 0 * pair)
+
     def remote(source, target, send, recv, partner):
         return pltpu.make_async_remote_copy(
             src_ref=source,
@@ -425,12 +435,22 @@
             flip(0),
         )
 
-    def stage_partner(stage, chunk):
-        if stage == 1:
-            return across if chunk == 0 else flip(1)
-        if stage == 2:
-            return flip(1) if chunk == 0 else across
-        return flip(2) if stage == 3 else flip(3) if stage == 4 else across
+    def is_late(pair):
+        return among(pair, late_pairs)
+
+    def is_second(pair, chunk):
+        return 0 * pair + 1 if chunk == 1 else among(pair, (pairs - 1,))
+
+    def stage_partner(stage, chunk, pair):
+        second = is_second(pair, chunk)
+        if stage < 3:
+            usual = (across, flip(1)) if stage == 1 else (flip(1), across)
+            usual = tuple(a + second * (b - a) for a, b in zip(*usual))
+        else:
+            usual = flip(2) if stage == 3 else flip(3) if stage == 4 else across
+        swapped = (flip(2), flip(3), across, flip(1), across)[stage - 1]
+        late = is_late(pair)
+        return tuple(a + late * (b - a) for a, b in zip(usual, swapped))
 
     def stage_copy(stage, pair, chunk):
         source = sends[stage - 1].at[pair % 2, chunk]
@@ -440,7 +460,7 @@
             target,
             send_sem.at[stage - 1, pair % 2, chunk],
             recv_sem.at[stage - 1, pair, chunk],
-            stage_partner(stage, chunk),
+            stage_partner(stage, chunk, pair),
         )
 
     def out_copy(pair, chunk):
@@ -480,8 +500,8 @@
                 for side in (0, 1):
                     core_copy(pair - 1, chunk, side).wait_send()
 
-        last = pair // 6
-        shrink = (2 - pair % 3) // 2 * (1 - last)
+        last = pair // full_pairs
+        shrink = among(pair, shrink_pairs)
 
         def one(j, carry):
             slot = j % 2
@@ -546,33 +566,46 @@
                 for side in (1, 0):
                     number = 2 * chunk + side
                     load(came[0].at[pair, number], side, 8).wait()
-                    if chunk == 0:
+                    late = is_late(pair)
+
+                    def both():
                         target = sends[0] if side == 1 else keeps[0]
 
-                        def both(block, carry):
+                        def one(block, carry):
                             target[slot, chunk, block] = add(
                                 core_own[number, block], loaded[side, block]
                             )
                             return carry
 
-                        lax.fori_loop(0, 8, both, 0)
-                    else:
-
-                        def split(z, carry):
-                            for target, block in (
-                                (sends[0], 2 * z + 1 - x),
-                                (keeps[0], 2 * z + x),
+                        lax.fori_loop(0, 8, one, 0)
+                        if side == 1:
+                            stage_copy(1, pair, chunk).start()
+
+                    def split():
+                        def one(i, carry):
+                            usual = 2 * i
+                            other = 4 * (i // 2) + i % 2
+                            low = bit_of(2)
+                            for target, a, b in (
+                                (sends[0], usual + 1 - x, other + 2 * (1 - low)),
+                                (keeps[0], usual + x, other + 2 * low),
                             ):
-                                target[slot, chunk, 4 * side + z] = add(
+                                block = a + late * (b - a)
+                                target[slot, chunk, 4 * side + i] = add(
                                     core_own[number, block], loaded[side, block]
                                 )
                             return carry
 
-                        lax.fori_loop(0, 4, split, 0)
-                    if chunk == 0 and side == 1:
-                        stage_copy(1, pair, chunk).start()
-                if chunk == 1:
-                    stage_copy(1, pair, chunk).start()
+                        lax.fori_loop(0, 4, one, 0)
+                        if side == 0:
+                            stage_copy(1, pair, chunk).start()
+
+                    if chunk == 0:
+                        apart = late + is_second(pair, chunk)
+                        pl.when(apart == 0)(both)
+                        pl.when(apart == 1)(split)
+                    else:
+                        split()
 
     def add_stage(stage, pair):
         slot = pair % 2
@@ -598,16 +631,23 @@
                 old, new = keeps[stage - 1], keeps[stage] if stage < 4 else None
 
                 def one(i, carry):
-                    if stage == 1 and chunk == 0:
-                        x = bit_of(1)
-                        gone, kept = 2 * i + 1 - x, 2 * i + x
-                    elif stage == 1:
-                        gone, kept = 4 + i, i
+                    late = is_late(pair)
+                    x, low, high = bit_of(1), bit_of(2), bit_of(3)
+                    if stage == 1:
+                        second = is_second(pair, chunk)
+                        a = (
+                            2 * i + 1 - x + second * (3 + x - i),
+                            2 * i + x + second * (-x - i),
+                        )
+                        start = 4 * (i // 2) + i % 2
+                        b = (start + 2 * (1 - high), start + 2 * high)
                     elif stage == 2:
-                        low = bit_of(2)
-                        gone, kept = 2 * i + 1 - low, 2 * i + low
+                        a = (2 * i + 1 - low, 2 * i + low)
+                        b = (2 + i, i)
                     else:
-                        gone, kept = 1 - bit_of(3), bit_of(3)
+                        a = (1 - high, high)
+                        b = (1 - x, x)
+                    gone, kept = [p + late * (q - p) for p, q in zip(a, b)]
                     sends[stage][slot, chunk, i] = add(
                         old[slot, chunk, gone], loaded[chunk, gone]
                     )
@@ -678,7 +718,9 @@
             stage_copy(5, pair, chunk).wait_recv()
 
 
-def scatter_products(factors, sources, small, pairs, full_pairs, rows, width, collective_id):
+def scatter_products(
+    factors, sources, small, pairs, full_pairs, shrink_pairs, rows, width, collective_id
+):
     tokens = factors[0].shape[0]
     depth = 16 * rows
     low = jnp.bfloat16
@@ -702,7 +744,9 @@
     dma = pltpu.SemaphoreType.DMA
     whole = pl.BlockSpec(memory_space=pltpu.VMEM)
     *_, out, total = pl.pallas_call(
-        functools.partial(scatter_kernel, pairs, full_pairs, sources, len(factors)),
+        functools.partial(
+            scatter_kernel, pairs, full_pairs, shrink_pairs, (), sources, len(factors)
+        ),
         out_shape=hbm + [jax.ShapeDtypeStruct(small.shape, small.dtype)],
         in_specs=[any_space] * len(factors) + [whole],
         out_specs=[any_space] * len(hbm) + [whole],
@@ -745,6 +789,9 @@
     return out, total
 
 
+BESIDE = ((1, "shrink"), )
+
+
 def token_rows(gradients):
     return gradients.reshape(-1, gradients.shape[-1])
 
@@ -766,11 +813,30 @@
         factors.extend(token_rows(member) for member in pair)
         return len(factors) - 2, len(factors) - 1
 
-    for expand, shrink, qkv, out in (terms[1], terms[0]):
-        left, right = add_factors(shrink)
-        sources += [((left, j * D), (right, 0)) for j in range(4)]
-        left, right = add_factors(expand)
-        sources += [((left, 0), (right, j * D)) for j in range(4)]
+    names = ("expand", "shrink", "qkv", "out")
+    results = [dict(), dict()]
+    shrink_pairs, homes = [], []
+
+    def beside(block, name):
+        left, right = [token_rows(member) for member in terms[block][names.index(name)]]
+        product = lax.dot_general(
+            left, right, (((0,), (0,)), ((), ())), preferred_element_type=jnp.float32
+        ).astype(jnp.bfloat16)
+        return lax.psum_scatter(product, "sp", scatter_dimension=0, tiled=True)
+
+    early = [beside(block, name) for block, name in BESIDE]
+    for block in (1, 0):
+        expand, shrink, qkv, out = terms[block]
+        if (block, "shrink") not in BESIDE:
+            shrink_pairs.append(len(homes))
+            homes.append((block, "shrink"))
+            left, right = add_factors(shrink)
+            sources += [((left, j * D), (right, 0)) for j in range(4)]
+        if (block, "expand") not in BESIDE:
+            homes.append((block, "expand"))
+            left, right = add_factors(expand)
+            sources += [((left, 0), (right, j * D)) for j in range(4)]
+        homes.append((block, "qkv"))
         left, right = add_factors(qkv)
         sources += [((left, 0), (right, j * D)) for j in range(3)]
         left, right = add_factors(out)
@@ -778,19 +844,28 @@
     for pair in terms[2]:
         left, right = add_factors(pair)
         sources.append(((left, 0), (right, 0)))
-    done, total = scatter_products(factors, sources, small, 7, 6, D // size, D, 1)
+    pairs = len(homes) + 1
+    if early:
+        small, first = lax.optimization_barrier((small, early[0]))
+        early[0] = first
+    done, total = scatter_products(
+        factors, sources, small, pairs, pairs - 1, tuple(shrink_pairs), D // size, D, 1
+    )
     done = done.astype(jnp.float32)
 
     def quarter(pair, k):
         return done[pair, k // 2, k % 2]
 
-    results = []
-    for first in (0, 3):
-        shrink = jnp.concatenate([quarter(first, k) for k in range(4)], axis=0)
-        expand = jnp.concatenate([quarter(first + 1, k) for k in range(4)], axis=1)
-        qkv = jnp.concatenate([quarter(first + 2, k) for k in range(3)], axis=1)
-        results.append([expand, shrink, qkv, quarter(first + 2, 3)])
-    return results[1], results[0], [quarter(6, 0), quarter(6, 1)], total
+    for pair, (block, name) in enumerate(homes):
+        parts = [quarter(pair, k) for k in range(4)]
+        if name == "qkv":
+            results[block]["out"] = parts.pop()
+        results[block][name] = jnp.concatenate(parts, axis=0 if name == "shrink" else 1)
+    for (block, name), part in zip(BESIDE, early):
+        results[block][name] = sum_seq(part)
+    last = [quarter(pairs - 1, k) for k in range(2)]
+    ordered = [[found[name] for name in names] for found in results]
+    return ordered[0], ordered[1], last, total
 
 
 def halve(members, bit_value, bit, links):
@@ -1249,21 +1324,28 @@
     ]
 
     def rounds_of(rows):
-        def block_round(qkv, out):
+        cut = 512
+
+        def block_round(qkv, out, start, width):
             return columns_round(
-                (qkv, 0, third), (qkv, third, third), (qkv, 2 * third, third), (out, 0, third)
+                (qkv, start, width),
+                (qkv, third + start, width),
+                (qkv, 2 * third + start, width),
+                (out, start, width),
             )
 
-        def expand_round(weight):
+        def expand_round(weight, late=False):
             quarter = FF // 4
-            return columns_round(*[(weight, k * quarter, quarter) for k in range(4)])
+            return columns_round(*[(weight, k * quarter, quarter) for k in range(4)], late=late)
 
         return [
-            block_round(0, 1),
+            block_round(0, 1, 0, cut),
+            block_round(0, 1, cut, third - cut),
             expand_round(2),
             rows_round(8, rows),
-            block_round(3, 4),
             columns_round((5, 0, third), (6, 0, third), (6, third, third), (7, 0, third)),
+            block_round(3, 4, 0, cut),
+            block_round(3, 4, cut, third - cut),
         ]
 
     (

time: 1280 us -> 1240 us (0.969)
  Pallas kernels: 699 us -> 627 us
  waiting for transfers between devices: 77.6 us -> 102 us
    pallas_call x1, Pallas kernels: 396 us -> 343 us  [scatter_products(): pl.pallas_call(functools.partial(scatter_kernel, pairs, full_pairs, shrin...]
    pallas_call x1, Pallas kernels: 303 us -> 284 us  [gather_weights(): pl.pallas_call(functools.partial(gather_kernel, rounds, len(shards), len(...]
    unnamed x350 -> x358, local copies, waits for them, and re-layouts: 44.7 us -> 47.3 us
  transfers between devices with their start and end apart: 10 -> 12, of which waited for: 4 -> 6; matrix products, arithmetic and copies ran while one was open for 20% -> 27% of each run, Pallas kernels for 55% -> 51%
where the time goes in v5:
time: 1240 us; the launch traced here: 1230 us
  Pallas kernels  627 us (51%)
  local copies, waits for them, and re-layouts  197 us (16%)
  matrix products  180 us (15%)
  waiting for transfers between devices  102 us (8%)
  other arithmetic  44 us (4%)
  starting transfers between devices  33 us (3%)
  blocking collectives  31.4 us (3%)
  between operations  16.2 us (1%)
    pallas_call x1, Pallas kernels, scatter_products(): pl.pallas_call(functools.partial(scatter_kernel, pairs, full_pairs, shrin...  343 us
    pallas_call x1, Pallas kernels, gather_weights(): pl.pallas_call(functools.partial(gather_kernel, rounds, len(shards), len(...  284 us
    dot_general x12, matrix products, input_grad(): lax.dot_general(gradients, weight, (((gradients.ndim - 1,), (1,)), ((), (...  65.2 us
    dot_general x12, matrix products, project(): return jnp.dot(inputs, weight, preferred_element_type=jnp.float32)  61.4 us
    unnamed x358, local copies, waits for them, and re-layouts  47.3 us
    all_to_all x1, waiting for transfers between devices, pair_attention(): lax.all_to_all(to_pairs(shaped), 'sp', split_axis=0, concat_axis=2, tiled...  40.5 us
    all_to_all x1, blocking collectives, pair_attention_back(): lax.all_to_all(to_pairs(grad_shaped), 'sp', split_axis=0, concat_axis=2,...  31.4 us
  transfers between devices with their start and end apart: 12, of which 6 were waited for; matrix products, arithmetic and copies ran while one was open for 27% of the time, Pallas kernels for 51%

profile of v5, /device:TPU:0, one launch (start us, length us, event | category | flops | bytes accessed | tf_op | source)
XLA Modules:
  0.0 1230.5 jit_solution(101751677898470435)
XLA Ops:
  20.3 284.4 %shard_map.332 = (bf16[2,2,2,2,72,3456]{5,4,3,2,1,0:T(8,128)(2,1)}, bf16[2,2,2,2,72,1152]{5,4,3,2,1,0:T(8,128)(2,1)S(1)}, bf16[2,2,2,2,72,4608]{5,4,3,2,1,0:T(8,...) custom-call(bf16[72,3456]{1,0:T(8,128)(2,1)S(1)} %copy-done.14, ...), custom_call_target="tpu_custom_call" | custom-call | bytes 53157888 | tf_op jit(solution)/shard_map/pallas_call | solution.py:258
  328.2 7.2 fusion.22
  335.4 8.4 reshape.582
  385.6 40.5 %all-to-all-done = bf16[16,32,8,216]{3,2,1,0:T(8,128)(2,1)} async-done(((bf16[16,32,8,216]{3,2,1,0:T(8,128)(2,1)}), bf16[16,32,8,216]{3,2,1,0:T(8,128)(2,1)}, u32[]{:S(2)}, u32[]{:S(2)}) %all-to-all-start) | async-done | bytes 1769504 | tf_op jit(solution)/shard_map/all_to_all | solution.py:980
  429.5 4.9 fusion.156
  440.8 18.1 %all-to-all-start.1 = ((bf16[1,32,128,72]{3,1,0,2:T(8,128)(2,1)}), bf16[1,32,128,72]{3,1,0,2:T(8,128)(2,1)}, u32[]{:S(2)}, u32[]{:S(2)}) async-start(bf16[1,32,128,72]{3,1,0,2:T(8,128)(2,1)} %copy.171), calls=%async_computation.1 | async-start | bytes 2097152 | tf_op jit(solution)/shard_map/all_to_all | solution.py:946
  461.7 6.8 fusion.42
  472.7 21.4 %all-to-all-done.1 = bf16[1,32,128,72]{3,1,0,2:T(8,128)(2,1)} async-done(((bf16[1,32,128,72]{3,1,0,2:T(8,128)(2,1)}), bf16[1,32,128,72]{3,1,0,2:T(8,128)(2,1)}, u32[]{:S(2)}, u32[]{:S(2)}) %all-to-all-start.1) | async-done | bytes 589856 | tf_op jit(solution)/shard_map/all_to_all | solution.py:946
  505.2 10.8 multiply_convert_fusion.1
  526.6 7.9 reshape.593
  571.5 6.2 fusion.16
  579.9 7.0 fusion.3
  586.9 9.2 convert_reduce_fusion
  596.2 8.9 multiply_reduce_fusion.3
  605.2 9.2 fusion.83
  620.1 5.6 fusion.43
  637.1 4.7 convert_reduce_fusion.10
  658.4 5.6 convert_element_type.298
  664.0 6.6 multiply_reduce_fusion.10
  673.3 8.6 convert_reduce_fusion.1
  682.0 8.3 multiply_reduce_fusion.9
  697.4 31.4 %all_to_all.63 = bf16[16,32,8,72]{3,2,1,0:T(8,128)(2,1)S(1)} all-to-all(bf16[16,32,8,72]{3,2,1,0:T(8,128)(2,1)S(1)} %bitcast.467), channel_id=1, replica_groups=mesh['seq'=2,'sp'=16] {'sp'}, dimensions={0} | all-to-all | bytes 1179648 | tf_op jit(solution)/shard_map/all_to_all | solution.py:991
  736.2 5.2 all-to-all-start.3
  753.1 4.7 convert_element_type.306.refs_3_
  777.3 20.6 %all-to-all-done.3 = bf16[1,32,128,216]{3,1,0,2:T(8,128)(2,1)} async-done(((bf16[1,32,128,216]{3,1,0,2:T(8,128)(2,1)}), bf16[1,32,128,216]{3,1,0,2:T(8,128)(2,1)}, u32[]{:S(2)}, u32[]{:S(2)}) %all-to-all-start.3) | async-done | bytes 1769504 | tf_op jit(solution)/shard_map/all_to_all | solution.py:974
  801.9 4.9 reshape_reshape.20.refs_11_
  806.8 4.8 reshape.609
  811.9 6.6 fusion.81
  823.9 342.6 %shard_map.333 = (bf16[6,4,8,72,1152]{4,3,2,1,0:T(8,128)(2,1)}, bf16[6,2,8,72,1152]{4,3,2,1,0:T(8,128)(2,1)}, bf16[6,2,4,72,1152]{4,3,2,1,0:T(8,128)(2,1)}, bf16...) custom-call(bf16[256,1152]{1,0:T(8,128)(2,1)} %bitcast.499, ...), custom_call_target="tpu_custom_call" | custom-call | flops 14948499456 | bytes 467140608 | tf_op jit(solution)/shard_map/pallas_call | solution.py:746
  1167.4 7.4 convert_reduce_fusion.5
  1202.7 5.3 collective-permute-done.3
  1209.9 9.1 collective-permute-done.1
  (588 shorter events, 281.4 us)
Async XLA Ops:
  7.2 321.0 %all-reduce.6.cloned.1.call-start = ((), (), s32[]{:S(2)}) async-start(), calls=%async_computation.5 | async-start | bytes 4423680 | tf_op jit(solution)/shard_map/psum | solution.py:1389
  12.2 299.4 %copy-start.162 = (s32[2,2]{1,0:T(2,128)S(1)}, s32[2,2]{1,0:T(2,128)}, u32[]{:S(2)}) copy-start(s32[2,2]{1,0:T(2,128)} %param.27) | copy-start | bytes 52
  12.2 300.3 %copy-start.145 = (s32[2,16]{1,0:T(2,128)S(1)}, s32[2,16]{1,0:T(2,128)}, u32[]{:S(2)}) copy-start(s32[2,16]{1,0:T(2,128)} %param.26) | copy-start | bytes 388
  12.2 559.2 %all-gather.3.cloned.1.call-start = ((), (), s32[]{:S(2)}) async-start(), calls=%async_computation.6 | async-start | bytes 11280384 | tf_op jit(solution)/shard_map/all_gather | solution.py:1372
  311.6 189.2 %copy-start.1 = (bf16[2,2,2,2,72,1152]{5,4,3,2,1,0:T(8,128)(2,1)}, bf16[2,2,2,2,72,1152]{5,4,3,2,1,0:T(8,128)(2,1)S(1)}, u32[]{:S(2)}) copy-start(bf16[2,2,2,2,72,1152]{5,4,3,2,1,0:T(8,128)(2,1)S(1)} %get-tuple-element.66) | copy-start | bytes 7962628
  347.8 78.3 %all-to-all-start = ((bf16[16,32,8,216]{3,2,1,0:T(8,128)(2,1)}), bf16[16,32,8,216]{3,2,1,0:T(8,128)(2,1)}, u32[]{:S(2)}, u32[]{:S(2)}) async-start(bf16[16,32,8,216]{3,2,1,0:T(8,128)(2,1)} %bitcast.459), calls=%async_computation | async-start | bytes 4194304 | tf_op jit(solution)/shard_map/all_to_all | solution.py:980
  352.5 234.4 %all-gather.5.cloned.1.call-start = ((), (), s32[]{:S(2)}) async-start(), calls=%async_computation.7 | async-start | bytes 11280384 | tf_op jit(solution)/shard_map/all_gather | solution.py:1373
  371.5 12.8 %copy-start.146 = (s32[2,16]{1,0:T(2,128)S(1)}, s32[2,16]{1,0:T(2,128)}, u32[]{:S(2)}) copy-start(s32[2,16]{1,0:T(2,128)} %param.26) | copy-start | bytes 388
  379.4 187.6 %copy-start.51 = (f32[2,16,1,1152]{3,1,2,0:T(8,128)}, f32[2,16,1,1152]{3,1,2,0:T(8,128)S(1)}, u32[]{:S(2)}) copy-start(f32[2,16,1,1152]{3,1,2,0:T(8,128)S(1)} %copy.326) | copy-start | bytes 442372
  381.0 123.5 %copy-start.49 = (f32[2,16,1,1152]{3,1,2,0:T(8,128)}, f32[2,16,1,1152]{3,1,2,0:T(8,128)S(1)}, u32[]{:S(2)}) copy-start(f32[2,16,1,1152]{3,1,2,0:T(8,128)S(1)} %copy.328) | copy-start | bytes 442372
  440.8 53.4 %all-to-all-start.1 = ((bf16[1,32,128,72]{3,1,0,2:T(8,128)(2,1)}), bf16[1,32,128,72]{3,1,0,2:T(8,128)(2,1)}, u32[]{:S(2)}, u32[]{:S(2)}) async-start(bf16[1,32,128,72]{3,1,0,2:T(8,128)(2,1)} %copy.171), calls=%async_computation.1 | async-start | bytes 2097152 | tf_op jit(solution)/shard_map/all_to_all | solution.py:946
  458.8 365.1 %reduce-scatter.2.cloned.1.call-start = ((), (), s32[]{:S(2)}) async-start(), calls=%async_computation.9 | async-start | bytes 11280384 | tf_op jit(solution)/shard_map/reduce_scatter | solution.py:825
  504.2 11.9 copy-start.24
  504.6 11.6 slice-start
  504.9 11.2 copy-start.83
  505.2 10.9 copy-start.90
  505.2 10.9 copy-start.157
  505.2 10.9 slice-start.1
  505.2 10.9 slice-start.2
  586.9 9.3 copy-start.78
  586.9 9.3 copy-start.106
  586.9 9.3 copy-start.121
  605.2 11.0 copy-start.11
  695.2 33.6 %copy-start.144 = (f32[32,128]{1,0:T(8,128)S(1)}, f32[32,128]{1,0:T(8,128)}, u32[]{:S(2)}) copy-start(f32[32,128]{1,0:T(8,128)} %get-tuple-element.182) | copy-start | bytes 49156
  697.0 31.7 %copy-start.37 = (bf16[1,32,128,216]{3,2,1,0:T(8,128)(2,1)S(1)}, bf16[1,32,128,216]{3,2,1,0:T(8,128)(2,1)}, u32[]{:S(2)}) copy-start(bf16[1,32,128,216]{3,2,1,0:T(8,128)(2,1)} %copy_bitcast_fusion.1) | copy-start | bytes 5308420
  697.1 31.7 %copy-start.60 = (f32[32,128,128]{1,2,0:T(8,128)S(1)}, f32[32,128,128]{1,2,0:T(8,128)}, u32[]{:S(2)}) copy-start(f32[32,128,128]{1,2,0:T(8,128)} %get-tuple-element.183) | copy-start | bytes 6291460
  736.2 61.6 %all-to-all-start.3 = ((bf16[1,32,128,216]{3,1,0,2:T(8,128)(2,1)}), bf16[1,32,128,216]{3,1,0,2:T(8,128)(2,1)}, u32[]{:S(2)}, u32[]{:S(2)}) async-start(bf16[1,32,128,216]{3,1,0,2:T(8,128)(2,1)} %copy.198), calls=%async_computation.3 | async-start | bytes 4194304 | tf_op jit(solution)/shard_map/all_to_all | solution.py:974
  741.4 426.0 %all-reduce.8.cloned.1.call-start = ((), (), s32[]{:S(2)}) async-start(), calls=%async_computation.8 | async-start | bytes 4423680 | tf_op jit(solution)/shard_map/psum | solution.py:1209
  1181.3 40.0 %collective-permute-start.2 = (bf16[288,1152]{1,0:T(8,128)(2,1)}, bf16[288,1152]{1,0:T(8,128)(2,1)}, u32[]{:S(2)}, u32[]{:S(2)}) collective-permute-start(bf16[288,1152]{1,0:T(8,128)(2,1)} %reduce-scatter.2.cloned.1.call-done), channel_id=1, source_target_pairs={{0,16},{16,0},{1,17},{17,1},{2,18},{18,2},{3,19},{19,3},{4,20},{20... | collective-permute-start | bytes 1990664 | tf_op jit(solution)/shard_map/ppermute | solution.py:98
  1184.3 16.5 %collective-permute-start = (bf16[122,256]{1,0:T(8,128)(2,1)S(1)}, bf16[122,256]{1,0:T(8,128)(2,1)S(1)}, u32[]{:S(2)}, u32[]{:S(2)}) collective-permute-start(bf16[122,256]{1,0:T(8,128)(2,1)S(1)} %pad_maximum_fusion.7), channel_id=1, source_target_pairs={{0,16},{16,0},{1,17},{17,1},{2,18},{18,2},{3,19},{19,3},{4,20},{20... | collective-permute-start | bytes 187400 | tf_op jit(solution)/shard_map/ppermute | solution.py:98
  1185.6 22.3 %collective-permute-start.3 = (bf16[72,2304]{1,0:T(8,128)(2,1)}, bf16[72,2304]{1,0:T(8,128)(2,1)}, u32[]{:S(2)}, u32[]{:S(2)}) collective-permute-start(bf16[72,2304]{1,0:T(8,128)(2,1)} %fusion.46), channel_id=1, source_target_pairs={{0,16},{16,0},{1,17},{17,1},{2,18},{18,2},{3,19},{19,3},{4,20},{20... | collective-permute-start | bytes 995336 | tf_op jit(solution)/shard_map/ppermute | solution.py:98
  1188.2 30.9 %collective-permute-start.1 = (bf16[256,1152]{1,0:T(8,128)(2,1)S(1)}, bf16[256,1152]{1,0:T(8,128)(2,1)}, u32[]{:S(2)}, u32[]{:S(2)}) collective-permute-start(bf16[256,1152]{1,0:T(8,128)(2,1)S(1)} %convolution_convert_fusion.4), channel_id=1, source_target_pairs={{0,16},{16,0},{1,17},{17,1},{2,18},{18,2},{3,19},{19,3},{4,20},{20... | collective-permute-start | bytes 1769480 | tf_op jit(solution)/shard_map/ppermute | solution.py:98
  (153 other events, 549.6 us)
Sparse Core Ops, SparseCore 0:
  12.3 141.4 all-reduce.5
  311.8 128.4 all-gather.2
  442.6 104.6 all-gather.4
  625.9 148.9 reduce-scatter.1
  778.3 111.3 all-reduce.7

commit v6 on v5

--- a/solution.py
+++ b/solution.py
@@ -914,16 +914,50 @@
     return (branch_grad, gate_grad)
 
 
+def split_kernel(width, source, target):
+    for head in range(HEADS):
+        target[:, head] = source[:, :, head * width : (head + 1) * width]
+
+
+def merge_kernel(width, source, target):
+    for head in range(HEADS):
+        target[:, :, head * width : (head + 1) * width] = source[:, head]
+
+
+def move_heads(kernel, values, width, shape):
+    step = 8
+
+    def block(dims):
+        return pl.BlockSpec((step, *dims[1:]), lambda i: (i, *[0] * (len(dims) - 1)))
+
+    return pl.pallas_call(
+        functools.partial(kernel, width),
+        grid=(shape[0] // step,),
+        in_specs=[block(values.shape)],
+        out_specs=block(shape),
+        out_shape=jax.ShapeDtypeStruct(shape, values.dtype),
+        compiler_params=pltpu.CompilerParams(vmem_limit_bytes=32 << 20),
+        cost_estimate=pl.CostEstimate(
+            flops=0, bytes_accessed=4 * values.size, transcendentals=0
+        ),
+    )(values)
+
+
 def to_pairs(values):
-    groups, frames, patches, head_count, columns = values.shape
-    reordered = jnp.transpose(values, (0, 1, 3, 2, 4))
-    return reordered.reshape(lax.axis_size("sp"), -1, patches, columns)
+    groups, frames, patches, columns = values.shape
+    width = columns // HEADS
+    flat = values.reshape(groups * frames, patches, columns)
+    shape = (groups * frames, HEADS, patches, width)
+    return move_heads(split_kernel, flat, width, shape).reshape(
+        lax.axis_size("sp"), -1, patches, width
+    )
 
 
 def from_pairs(values, groups, frames):
-    devices, pair_count, patches, columns = values.shape
-    reordered = values.reshape(groups, frames, -1, patches, columns)
-    return jnp.transpose(reordered, (0, 1, 3, 2, 4))
+    devices, pair_count, patches, width = values.shape
+    pairs = values.reshape(groups * frames, HEADS, patches, width)
+    shape = (groups * frames, patches, HEADS * width)
+    return move_heads(merge_kernel, pairs, width, shape)
 
 
 def pair_scores(triple):
@@ -976,19 +1010,17 @@
 
 def pair_attention(triple):
     groups, frames, patches = triple.shape[:3]
-    shaped = triple.reshape(groups, frames, patches, HEADS, 3 * HEAD_DIM)
-    pairs = lax.all_to_all(to_pairs(shaped), "sp", split_axis=0, concat_axis=2, tiled=True)
+    pairs = lax.all_to_all(to_pairs(triple), "sp", split_axis=0, concat_axis=2, tiled=True)
     exchanged = attend_pairs(pairs)
     return from_pairs(exchanged, groups, frames).reshape(groups, frames, patches, D), pairs
 
 
 def pair_attention_back(pairs, mixture_grad):
     groups, frames, patches = mixture_grad.shape[:3]
-    grad_shaped = mixture_grad.reshape(groups, frames, patches, HEADS, HEAD_DIM)
     returned = pair_backward(
         (
             pairs,
-            lax.all_to_all(to_pairs(grad_shaped), "sp", split_axis=0, concat_axis=2, tiled=True),
+            lax.all_to_all(to_pairs(mixture_grad), "sp", split_axis=0, concat_axis=2, tiled=True),
         )
     )
     return from_pairs(returned, groups, frames).reshape(groups, frames, patches, 3 * D)

time: 1240 us -> 1230 us (level)
  local copies, waits for them, and re-layouts: 197 us -> 156 us
    reshape x6 -> x0, local copies, waits for them, and re-layouts: 22.7 us -> none  [the longest x2 12.4 us: pair_attention(): shaped = triple.reshape(groups, frames, patches, HEADS, 3 * HEAD_DIM)]
    unnamed x358 -> x344, local copies, waits for them, and re-layouts: 47.3 us -> 44.2 us
  transfers between devices with their start and end apart: 12 -> 12, of which waited for: 6 -> 6; matrix products, arithmetic and copies ran while one was open for 27% -> 24% of each run, Pallas kernels for 51% -> 52%
where the time goes in v6:
time: 1230 us; the launch traced here: 1220 us
  Pallas kernels  632 us (51%)
  matrix products  182 us (15%)
  local copies, waits for them, and re-layouts  156 us (13%)
  waiting for transfers between devices  113 us (9%)
  other arithmetic  46 us (4%)
  starting transfers between devices  39.7 us (3%)
  blocking collectives  31.9 us (3%)
  between operations  16.5 us (1%)
    pallas_call x1, Pallas kernels, scatter_products(): pl.pallas_call(functools.partial(scatter_kernel, pairs, full_pairs, shrin...  342 us
    pallas_call x1, Pallas kernels, gather_weights(): pl.pallas_call(functools.partial(gather_kernel, rounds, len(shards), len(...  284 us
    dot_general x12, matrix products, input_grad(): lax.dot_general(gradients, weight, (((gradients.ndim - 1,), (1,)), ((), (...  68.3 us
    dot_general x12, matrix products, project(): return jnp.dot(inputs, weight, preferred_element_type=jnp.float32)  59.4 us
    unnamed x344, local copies, waits for them, and re-layouts  44.2 us
    all_to_all x1, waiting for transfers between devices, pair_attention(): lax.all_to_all(to_pairs(triple), 'sp', split_axis=0, concat_axis=2, tiled...  36 us
    all_to_all x1, waiting for transfers between devices, pair_backward(): lax.all_to_all(gradients, 'sp', split_axis=2, concat_axis=0, tiled=True)  32.8 us
    all_to_all x1, blocking collectives, pair_attention_back(): lax.all_to_all(to_pairs(mixture_grad), 'sp', split_axis=0, concat_axis=2,...  31.9 us
  transfers between devices with their start and end apart: 12, of which 6 were waited for; matrix products, arithmetic and copies ran while one was open for 24% of the time, Pallas kernels for 52%

profile of v6, /device:TPU:0, one launch (start us, length us, event | category | flops | bytes accessed | tf_op | source)
XLA Modules:
  0.0 1216.4 jit_solution(7073590152992493105)
XLA Ops:
  19.7 284.3 %shard_map.332 = (bf16[2,2,2,2,72,3456]{5,4,3,2,1,0:T(8,128)(2,1)}, bf16[2,2,2,2,72,1152]{5,4,3,2,1,0:T(8,128)(2,1)S(1)}, bf16[2,2,2,2,72,4608]{5,4,3,2,1,0:T(8,...) custom-call(bf16[72,3456]{1,0:T(8,128)(2,1)S(1)} %copy-done.16, ...), custom_call_target="tpu_custom_call" | custom-call | bytes 53157888 | tf_op jit(solution)/shard_map/pallas_call | solution.py:258
  327.6 5.9 fusion.22
  336.0 4.7 all-to-all-start
  373.9 36.0 %all-to-all-done = bf16[16,32,8,216]{3,2,1,0:T(8,128)(2,1)} async-done(((bf16[16,32,8,216]{3,2,1,0:T(8,128)(2,1)}), bf16[16,32,8,216]{3,2,1,0:T(8,128)(2,1)}, u32[]{:S(2)}, u32[]{:S(2)}) %all-to-all-start) | async-done | bytes 1769504 | tf_op jit(solution)/shard_map/all_to_all | solution.py:1013
  413.1 4.9 fusion.156
  424.3 25.1 %all-to-all-start.1 = ((bf16[1,32,128,72]{3,1,0,2:T(8,128)(2,1)}), bf16[1,32,128,72]{3,1,0,2:T(8,128)(2,1)}, u32[]{:S(2)}, u32[]{:S(2)}) async-start(bf16[1,32,128,72]{3,1,0,2:T(8,128)(2,1)} %copy.162), calls=%async_computation.1 | async-start | bytes 2097152 | tf_op jit(solution)/shard_map/all_to_all | solution.py:980
  452.3 6.8 fusion.42
  463.2 25.0 %all-to-all-done.1 = bf16[1,32,128,72]{3,1,0,2:T(8,128)(2,1)} async-done(((bf16[1,32,128,72]{3,1,0,2:T(8,128)(2,1)}), bf16[1,32,128,72]{3,1,0,2:T(8,128)(2,1)}, u32[]{:S(2)}, u32[]{:S(2)}) %all-to-all-start.1) | async-done | bytes 589856 | tf_op jit(solution)/shard_map/all_to_all | solution.py:980
  493.9 11.0 multiply_convert_fusion.1
  505.1 4.4 fusion.149
  514.1 8.6 reshape.591
  560.5 6.2 fusion.16
  568.9 7.0 fusion.3
  576.0 9.5 convert_reduce_fusion
  585.6 9.9 multiply_reduce_fusion.3
  595.6 9.6 fusion.83
  612.1 5.7 fusion.43
  617.9 4.4 fusion.45
  651.8 5.7 convert_element_type.298
  657.6 6.6 multiply_reduce_fusion.10
  666.9 8.6 convert_reduce_fusion.1
  675.6 8.3 multiply_reduce_fusion.9
  689.4 31.9 %all_to_all.63 = bf16[16,32,8,72]{3,2,1,0:T(8,128)(2,1)S(1)} all-to-all(bf16[16,32,8,72]{3,2,1,0:T(8,128)(2,1)S(1)} %bitcast.434), channel_id=1, replica_groups=mesh['seq'=2,'sp'=16] {'sp'}, dimensions={0} | all-to-all | bytes 1179648 | tf_op jit(solution)/shard_map/all_to_all | solution.py:1023
  728.8 5.1 all-to-all-start.3
  743.7 4.7 convert_element_type.306.refs_3_
  757.9 32.8 %all-to-all-done.3 = bf16[1,32,128,216]{3,1,0,2:T(8,128)(2,1)} async-done(((bf16[1,32,128,216]{3,1,0,2:T(8,128)(2,1)}), bf16[1,32,128,216]{3,1,0,2:T(8,128)(2,1)}, u32[]{:S(2)}, u32[]{:S(2)}) %all-to-all-start.3) | async-done | bytes 1769504 | tf_op jit(solution)/shard_map/all_to_all | solution.py:1008
  795.2 7.2 fusion.81
  809.9 342.3 %shard_map.337 = (bf16[6,4,8,72,1152]{4,3,2,1,0:T(8,128)(2,1)}, bf16[6,2,8,72,1152]{4,3,2,1,0:T(8,128)(2,1)}, bf16[6,2,4,72,1152]{4,3,2,1,0:T(8,128)(2,1)}, bf16...) custom-call(bf16[256,1152]{1,0:T(8,128)(2,1)} %bitcast.489, ...), custom_call_target="tpu_custom_call" | custom-call | flops 14948499456 | bytes 467140608 | tf_op jit(solution)/shard_map/pallas_call | solution.py:746
  1153.1 7.4 convert_reduce_fusion.5
  1182.1 4.4 collective-permute-done
  1188.5 5.3 collective-permute-done.3
  1195.7 9.0 collective-permute-done.1
  (568 shorter events, 251.5 us)
Async XLA Ops:
  7.2 320.4 %all-reduce.6.cloned.1.call-start = ((), (), s32[]{:S(2)}) async-start(), calls=%async_computation.5 | async-start | bytes 4423680 | tf_op jit(solution)/shard_map/psum | solution.py:1421
  11.6 299.4 %copy-start.155 = (s32[2,2]{1,0:T(2,128)S(1)}, s32[2,2]{1,0:T(2,128)}, u32[]{:S(2)}) copy-start(s32[2,2]{1,0:T(2,128)} %param.27) | copy-start | bytes 52
  11.6 300.2 %copy-start.137 = (s32[2,16]{1,0:T(2,128)S(1)}, s32[2,16]{1,0:T(2,128)}, u32[]{:S(2)}) copy-start(s32[2,16]{1,0:T(2,128)} %param.26) | copy-start | bytes 388
  11.6 548.8 %all-gather.3.cloned.1.call-start = ((), (), s32[]{:S(2)}) async-start(), calls=%async_computation.6 | async-start | bytes 11280384 | tf_op jit(solution)/shard_map/all_gather | solution.py:1404
  311.0 180.1 %copy-start.2 = (bf16[2,2,2,2,72,1152]{5,4,3,2,1,0:T(8,128)(2,1)}, bf16[2,2,2,2,72,1152]{5,4,3,2,1,0:T(8,128)(2,1)S(1)}, u32[]{:S(2)}) copy-start(bf16[2,2,2,2,72,1152]{5,4,3,2,1,0:T(8,128)(2,1)S(1)} %get-tuple-element.66) | copy-start | bytes 7962628
  336.0 73.9 %all-to-all-start = ((bf16[16,32,8,216]{3,2,1,0:T(8,128)(2,1)}), bf16[16,32,8,216]{3,2,1,0:T(8,128)(2,1)}, u32[]{:S(2)}, u32[]{:S(2)}) async-start(bf16[16,32,8,216]{3,2,1,0:T(8,128)(2,1)} %bitcast.11), calls=%async_computation | async-start | bytes 4194304 | tf_op jit(solution)/shard_map/all_to_all | solution.py:1013
  340.8 235.2 %all-gather.5.cloned.1.call-start = ((), (), s32[]{:S(2)}) async-start(), calls=%async_computation.7 | async-start | bytes 11280384 | tf_op jit(solution)/shard_map/all_gather | solution.py:1405
  359.7 12.8 %copy-start.138 = (s32[2,16]{1,0:T(2,128)S(1)}, s32[2,16]{1,0:T(2,128)}, u32[]{:S(2)}) copy-start(s32[2,16]{1,0:T(2,128)} %param.26) | copy-start | bytes 388
  367.7 188.4 %copy-start.56 = (f32[2,16,1,1152]{3,1,2,0:T(8,128)}, f32[2,16,1,1152]{3,1,2,0:T(8,128)S(1)}, u32[]{:S(2)}) copy-start(f32[2,16,1,1152]{3,1,2,0:T(8,128)S(1)} %copy.312) | copy-start | bytes 442372
  369.3 124.1 %copy-start.54 = (f32[2,16,1,1152]{3,1,2,0:T(8,128)}, f32[2,16,1,1152]{3,1,2,0:T(8,128)S(1)}, u32[]{:S(2)}) copy-start(f32[2,16,1,1152]{3,1,2,0:T(8,128)S(1)} %copy.314) | copy-start | bytes 442372
  424.3 63.9 %all-to-all-start.1 = ((bf16[1,32,128,72]{3,1,0,2:T(8,128)(2,1)}), bf16[1,32,128,72]{3,1,0,2:T(8,128)(2,1)}, u32[]{:S(2)}, u32[]{:S(2)}) async-start(bf16[1,32,128,72]{3,1,0,2:T(8,128)(2,1)} %copy.162), calls=%async_computation.1 | async-start | bytes 2097152 | tf_op jit(solution)/shard_map/all_to_all | solution.py:980
  449.4 360.5 %reduce-scatter.2.cloned.1.call-start = ((), (), s32[]{:S(2)}) async-start(), calls=%async_computation.9 | async-start | bytes 11280384 | tf_op jit(solution)/shard_map/reduce_scatter | solution.py:825
  493.1 11.9 copy-start.26
  493.1 11.8 copy-start.102
  493.4 11.5 copy-start.116
  493.4 11.5 copy-start.110
  493.5 11.5 slice-start
  493.8 11.2 copy-start.92
  493.9 11.1 copy-start.99
  493.9 11.1 copy-start.149
  493.9 11.1 slice-start.1
  493.9 11.1 slice-start.2
  595.6 11.7 copy-start.12
  687.5 33.8 %copy-start.66 = (f32[32,128,128]{1,2,0:T(8,128)S(1)}, f32[32,128,128]{1,2,0:T(8,128)}, u32[]{:S(2)}) copy-start(f32[32,128,128]{1,2,0:T(8,128)} %get-tuple-element.183) | copy-start | bytes 6291460
  688.6 32.8 %copy-start.40 = (bf16[1,32,128,216]{3,2,1,0:T(8,128)(2,1)S(1)}, bf16[1,32,128,216]{3,2,1,0:T(8,128)(2,1)}, u32[]{:S(2)}) copy-start(bf16[1,32,128,216]{3,2,1,0:T(8,128)(2,1)} %copy_bitcast_fusion.1) | copy-start | bytes 5308420
  688.6 32.8 %copy-start.136 = (f32[32,128]{1,0:T(8,128)S(1)}, f32[32,128]{1,0:T(8,128)}, u32[]{:S(2)}) copy-start(f32[32,128]{1,0:T(8,128)} %get-tuple-element.182) | copy-start | bytes 49156
  728.8 61.9 %all-to-all-start.3 = ((bf16[1,32,128,216]{3,1,0,2:T(8,128)(2,1)}), bf16[1,32,128,216]{3,1,0,2:T(8,128)(2,1)}, u32[]{:S(2)}, u32[]{:S(2)}) async-start(bf16[1,32,128,216]{3,1,0,2:T(8,128)(2,1)} %copy.187), calls=%async_computation.3 | async-start | bytes 4194304 | tf_op jit(solution)/shard_map/all_to_all | solution.py:1008
  733.9 419.2 %all-reduce.8.cloned.1.call-start = ((), (), s32[]{:S(2)}) async-start(), calls=%async_computation.8 | async-start | bytes 4423680 | tf_op jit(solution)/shard_map/psum | solution.py:1241
  1167.1 39.8 %collective-permute-start.2 = (bf16[288,1152]{1,0:T(8,128)(2,1)}, bf16[288,1152]{1,0:T(8,128)(2,1)}, u32[]{:S(2)}, u32[]{:S(2)}) collective-permute-start(bf16[288,1152]{1,0:T(8,128)(2,1)} %reduce-scatter.2.cloned.1.call-done), channel_id=1, source_target_pairs={{0,16},{16,0},{1,17},{17,1},{2,18},{18,2},{3,19},{19,3},{4,20},{20... | collective-permute-start | bytes 1990664 | tf_op jit(solution)/shard_map/ppermute | solution.py:98
  1170.3 16.3 %collective-permute-start = (bf16[122,256]{1,0:T(8,128)(2,1)S(1)}, bf16[122,256]{1,0:T(8,128)(2,1)S(1)}, u32[]{:S(2)}, u32[]{:S(2)}) collective-permute-start(bf16[122,256]{1,0:T(8,128)(2,1)S(1)} %pad_maximum_fusion.7), channel_id=1, source_target_pairs={{0,16},{16,0},{1,17},{17,1},{2,18},{18,2},{3,19},{19,3},{4,20},{20... | collective-permute-start | bytes 187400 | tf_op jit(solution)/shard_map/ppermute | solution.py:98
  1171.5 22.3 %collective-permute-start.3 = (bf16[72,2304]{1,0:T(8,128)(2,1)}, bf16[72,2304]{1,0:T(8,128)(2,1)}, u32[]{:S(2)}, u32[]{:S(2)}) collective-permute-start(bf16[72,2304]{1,0:T(8,128)(2,1)} %fusion.46), channel_id=1, source_target_pairs={{0,16},{16,0},{1,17},{17,1},{2,18},{18,2},{3,19},{19,3},{4,20},{20... | collective-permute-start | bytes 995336 | tf_op jit(solution)/shard_map/ppermute | solution.py:98
  1174.2 30.5 %collective-permute-start.1 = (bf16[256,1152]{1,0:T(8,128)(2,1)S(1)}, bf16[256,1152]{1,0:T(8,128)(2,1)}, u32[]{:S(2)}, u32[]{:S(2)}) collective-permute-start(bf16[256,1152]{1,0:T(8,128)(2,1)S(1)} %convolution_convert_fusion.4), channel_id=1, source_target_pairs={{0,16},{16,0},{1,17},{17,1},{2,18},{18,2},{3,19},{19,3},{4,20},{20... | collective-permute-start | bytes 1769480 | tf_op jit(solution)/shard_map/ppermute | solution.py:98
  (146 other events, 613.0 us)
Sparse Core Ops, SparseCore 0:
  11.7 141.2 all-reduce.5
  311.1 123.0 all-gather.2
  436.5 107.2 all-gather.4
  618.0 148.9 reduce-scatter.1
  770.4 110.6 all-reduce.7

commit v7 on v6

--- a/solution.py
+++ b/solution.py
@@ -529,15 +529,25 @@
                 return carry
 
             lax.fori_loop(0, 16, store, 0)
-            return carry
-
-        lax.fori_loop(0, 4 - 2 * last, one, 0)
-        for chunk in (0, 1):
-
-            @pl.when(has(pair, chunk))
+
+            @pl.when((j == 1) & (shrink == 0))
             def _():
                 for side in (0, 1):
-                    core_copy(pair, chunk, side).start()
+                    core_copy(pair, 0, side).start()
+
+            return carry
+
+        lax.fori_loop(0, 4 - 2 * last, one, 0)
+
+        @pl.when(shrink == 1)
+        def _():
+            for side in (0, 1):
+                core_copy(pair, 0, side).start()
+
+        @pl.when(has(pair, 1))
+        def _():
+            for side in (0, 1):
+                core_copy(pair, 1, side).start()
 
     def add(a, b):
         return (a.astype(jnp.float32) + b.astype(jnp.float32)).astype(jnp.bfloat16)
@@ -1371,13 +1381,15 @@
             return columns_round(*[(weight, k * quarter, quarter) for k in range(4)], late=late)
 
         return [
-            block_round(0, 1, 0, cut),
+            block_round(0, 1, 0, cut // 2),
+            block_round(0, 1, cut // 2, cut // 2),
             block_round(0, 1, cut, third - cut),
             expand_round(2),
             rows_round(8, rows),
             columns_round((5, 0, third), (6, 0, third), (6, third, third), (7, 0, third)),
-            block_round(3, 4, 0, cut),
-            block_round(3, 4, cut, third - cut),
+            block_round(3, 4, 0, third - cut),
+            block_round(3, 4, third - cut, cut // 2),
+            block_round(3, 4, third - cut // 2, cut // 2),
         ]
 
     (

time: 1230 us -> 1230 us (level)
  no operation moved by 1% of the time
where the time goes in v7:
time: 1230 us; the launch traced here: 1210 us
  Pallas kernels  626 us (51%)
  matrix products  182 us (15%)
  local copies, waits for them, and re-layouts  156 us (13%)
  waiting for transfers between devices  116 us (9%)
  other arithmetic  46 us (4%)
  starting transfers between devices  38.5 us (3%)
  blocking collectives  32.7 us (3%)
  between operations  16.5 us (1%)
    pallas_call x1, Pallas kernels, scatter_products(): pl.pallas_call(functools.partial(scatter_kernel, pairs, full_pairs, shrin...  339 us
    pallas_call x1, Pallas kernels, gather_weights(): pl.pallas_call(functools.partial(gather_kernel, rounds, len(shards), len(...  282 us
    dot_general x12, matrix products, input_grad(): lax.dot_general(gradients, weight, (((gradients.ndim - 1,), (1,)), ((), (...  68.2 us
    dot_general x12, matrix products, project(): return jnp.dot(inputs, weight, preferred_element_type=jnp.float32)  60.2 us
    unnamed x344, local copies, waits for them, and re-layouts  44.2 us
    all_to_all x1, waiting for transfers between devices, pair_attention(): lax.all_to_all(to_pairs(triple), 'sp', split_axis=0, concat_axis=2, tiled...  37.1 us
    all_to_all x1, waiting for transfers between devices, pair_backward(): lax.all_to_all(gradients, 'sp', split_axis=2, concat_axis=0, tiled=True)  32.9 us
    all_to_all x1, blocking collectives, pair_attention_back(): lax.all_to_all(to_pairs(mixture_grad), 'sp', split_axis=0, concat_axis=2,...  32.7 us
  transfers between devices with their start and end apart: 12, of which 6 were waited for; matrix products, arithmetic and copies ran while one was open for 24% of the time, Pallas kernels for 52%

profile of v7, /device:TPU:0, one launch (start us, length us, event | category | flops | bytes accessed | tf_op | source)
XLA Modules:
  0.0 1213.5 jit_solution(12936382847826320945)
XLA Ops:
  19.7 281.8 %shard_map.332 = (bf16[2,2,2,2,72,3456]{5,4,3,2,1,0:T(8,128)(2,1)}, bf16[2,2,2,2,72,1152]{5,4,3,2,1,0:T(8,128)(2,1)S(1)}, bf16[2,2,2,2,72,4608]{5,4,3,2,1,0:T(8,...) custom-call(bf16[72,3456]{1,0:T(8,128)(2,1)S(1)} %copy-done.16, ...), custom_call_target="tpu_custom_call" | custom-call | bytes 53157888 | tf_op jit(solution)/shard_map/pallas_call | solution.py:258
  325.2 5.9 fusion.22
  333.6 4.8 all-to-all-start
  371.5 37.1 %all-to-all-done = bf16[16,32,8,216]{3,2,1,0:T(8,128)(2,1)} async-done(((bf16[16,32,8,216]{3,2,1,0:T(8,128)(2,1)}), bf16[16,32,8,216]{3,2,1,0:T(8,128)(2,1)}, u32[]{:S(2)}, u32[]{:S(2)}) %all-to-all-start) | async-done | bytes 1769504 | tf_op jit(solution)/shard_map/all_to_all | solution.py:1023
  411.8 5.0 fusion.156
  423.1 24.1 %all-to-all-start.1 = ((bf16[1,32,128,72]{3,1,0,2:T(8,128)(2,1)}), bf16[1,32,128,72]{3,1,0,2:T(8,128)(2,1)}, u32[]{:S(2)}, u32[]{:S(2)}) async-start(bf16[1,32,128,72]{3,1,0,2:T(8,128)(2,1)} %copy.162), calls=%async_computation.1 | async-start | bytes 2097152 | tf_op jit(solution)/shard_map/all_to_all | solution.py:990
  450.1 6.8 fusion.42
  461.0 26.1 %all-to-all-done.1 = bf16[1,32,128,72]{3,1,0,2:T(8,128)(2,1)} async-done(((bf16[1,32,128,72]{3,1,0,2:T(8,128)(2,1)}), bf16[1,32,128,72]{3,1,0,2:T(8,128)(2,1)}, u32[]{:S(2)}, u32[]{:S(2)}) %all-to-all-start.1) | async-done | bytes 589856 | tf_op jit(solution)/shard_map/all_to_all | solution.py:990
  492.8 11.9 multiply_convert_fusion.1
  504.8 4.4 fusion.149
  513.8 8.6 reshape.591
  560.1 6.2 fusion.16
  568.5 7.0 fusion.3
  575.6 9.5 convert_reduce_fusion
  585.2 9.9 multiply_reduce_fusion.3
  595.2 9.6 fusion.83
  611.8 5.7 fusion.43
  617.5 4.4 fusion.45
  651.5 5.8 convert_element_type.298
  657.3 6.6 multiply_reduce_fusion.10
  666.6 8.6 convert_reduce_fusion.1
  675.3 8.3 multiply_reduce_fusion.9
  689.1 32.7 %all_to_all.63 = bf16[16,32,8,72]{3,2,1,0:T(8,128)(2,1)S(1)} all-to-all(bf16[16,32,8,72]{3,2,1,0:T(8,128)(2,1)S(1)} %bitcast.434), channel_id=1, replica_groups=mesh['seq'=2,'sp'=16] {'sp'}, dimensions={0} | all-to-all | bytes 1179648 | tf_op jit(solution)/shard_map/all_to_all | solution.py:1033
  729.2 5.2 all-to-all-start.3
  744.1 4.7 convert_element_type.306.refs_3_
  758.3 32.9 %all-to-all-done.3 = bf16[1,32,128,216]{3,1,0,2:T(8,128)(2,1)} async-done(((bf16[1,32,128,216]{3,1,0,2:T(8,128)(2,1)}), bf16[1,32,128,216]{3,1,0,2:T(8,128)(2,1)}, u32[]{:S(2)}, u32[]{:S(2)}) %all-to-all-start.3) | async-done | bytes 1769504 | tf_op jit(solution)/shard_map/all_to_all | solution.py:1018
  795.7 7.2 fusion.81
  810.4 338.9 %shard_map.337 = (bf16[6,4,8,72,1152]{4,3,2,1,0:T(8,128)(2,1)}, bf16[6,2,8,72,1152]{4,3,2,1,0:T(8,128)(2,1)}, bf16[6,2,4,72,1152]{4,3,2,1,0:T(8,128)(2,1)}, bf16...) custom-call(bf16[256,1152]{1,0:T(8,128)(2,1)} %bitcast.489, ...), custom_call_target="tpu_custom_call" | custom-call | flops 14948499456 | bytes 467140608 | tf_op jit(solution)/shard_map/pallas_call | solution.py:756
  1150.2 7.4 convert_reduce_fusion.5
  1179.3 4.4 collective-permute-done
  1185.7 5.3 collective-permute-done.3
  1192.9 9.0 collective-permute-done.1
  (568 shorter events, 251.4 us)
Async XLA Ops:
  7.2 318.0 %all-reduce.6.cloned.1.call-start = ((), (), s32[]{:S(2)}) async-start(), calls=%async_computation.5 | async-start | bytes 4423680 | tf_op jit(solution)/shard_map/psum | solution.py:1433
  11.6 297.0 %copy-start.155 = (s32[2,2]{1,0:T(2,128)S(1)}, s32[2,2]{1,0:T(2,128)}, u32[]{:S(2)}) copy-start(s32[2,2]{1,0:T(2,128)} %param.27) | copy-start | bytes 52
  11.6 297.8 %copy-start.137 = (s32[2,16]{1,0:T(2,128)S(1)}, s32[2,16]{1,0:T(2,128)}, u32[]{:S(2)}) copy-start(s32[2,16]{1,0:T(2,128)} %param.26) | copy-start | bytes 388
  11.6 548.4 %all-gather.3.cloned.1.call-start = ((), (), s32[]{:S(2)}) async-start(), calls=%async_computation.6 | async-start | bytes 11280384 | tf_op jit(solution)/shard_map/all_gather | solution.py:1416
  308.5 181.4 %copy-start.2 = (bf16[2,2,2,2,72,1152]{5,4,3,2,1,0:T(8,128)(2,1)}, bf16[2,2,2,2,72,1152]{5,4,3,2,1,0:T(8,128)(2,1)S(1)}, u32[]{:S(2)}) copy-start(bf16[2,2,2,2,72,1152]{5,4,3,2,1,0:T(8,128)(2,1)S(1)} %get-tuple-element.66) | copy-start | bytes 7962628
  333.6 75.0 %all-to-all-start = ((bf16[16,32,8,216]{3,2,1,0:T(8,128)(2,1)}), bf16[16,32,8,216]{3,2,1,0:T(8,128)(2,1)}, u32[]{:S(2)}, u32[]{:S(2)}) async-start(bf16[16,32,8,216]{3,2,1,0:T(8,128)(2,1)} %bitcast.11), calls=%async_computation | async-start | bytes 4194304 | tf_op jit(solution)/shard_map/all_to_all | solution.py:1023
  338.4 237.2 %all-gather.5.cloned.1.call-start = ((), (), s32[]{:S(2)}) async-start(), calls=%async_computation.7 | async-start | bytes 11280384 | tf_op jit(solution)/shard_map/all_gather | solution.py:1417
  357.3 12.8 %copy-start.138 = (s32[2,16]{1,0:T(2,128)S(1)}, s32[2,16]{1,0:T(2,128)}, u32[]{:S(2)}) copy-start(s32[2,16]{1,0:T(2,128)} %param.26) | copy-start | bytes 388
  365.3 190.4 %copy-start.56 = (f32[2,16,1,1152]{3,1,2,0:T(8,128)}, f32[2,16,1,1152]{3,1,2,0:T(8,128)S(1)}, u32[]{:S(2)}) copy-start(f32[2,16,1,1152]{3,1,2,0:T(8,128)S(1)} %copy.312) | copy-start | bytes 442372
  366.9 125.4 %copy-start.54 = (f32[2,16,1,1152]{3,1,2,0:T(8,128)}, f32[2,16,1,1152]{3,1,2,0:T(8,128)S(1)}, u32[]{:S(2)}) copy-start(f32[2,16,1,1152]{3,1,2,0:T(8,128)S(1)} %copy.314) | copy-start | bytes 442372
  423.1 64.1 %all-to-all-start.1 = ((bf16[1,32,128,72]{3,1,0,2:T(8,128)(2,1)}), bf16[1,32,128,72]{3,1,0,2:T(8,128)(2,1)}, u32[]{:S(2)}, u32[]{:S(2)}) async-start(bf16[1,32,128,72]{3,1,0,2:T(8,128)(2,1)} %copy.162), calls=%async_computation.1 | async-start | bytes 2097152 | tf_op jit(solution)/shard_map/all_to_all | solution.py:990
  447.2 363.2 %reduce-scatter.2.cloned.1.call-start = ((), (), s32[]{:S(2)}) async-start(), calls=%async_computation.9 | async-start | bytes 11280384 | tf_op jit(solution)/shard_map/reduce_scatter | solution.py:835
  492.0 12.7 %copy-start.26 = (f32[2,16,8,1152]{3,2,1,0:T(8,128)}, f32[2,16,8,1152]{3,2,1,0:T(8,128)S(1)}, u32[]{:S(2)}) copy-start(f32[2,16,8,1152]{3,2,1,0:T(8,128)S(1)} %get-tuple-element.122) | copy-start | bytes 3538948
  492.0 12.6 %copy-start.102 = (f32[2,16,8]{2,1,0:T(8,128)}, f32[2,16,8]{2,1,0:T(8,128)S(1)}, u32[]{:S(2)}) copy-start(f32[2,16,8]{2,1,0:T(8,128)S(1)} %broadcast_multiply_fusion.2) | copy-start | bytes 3076
  492.3 12.3 %copy-start.116 = (f32[2,16,8]{2,1,0:T(8,128)}, f32[2,16,8]{2,1,0:T(8,128)S(1)}, u32[]{:S(2)}) copy-start(f32[2,16,8]{2,1,0:T(8,128)S(1)} %multiply_reduce_fusion.14) | copy-start | bytes 3076
  492.3 12.3 %copy-start.110 = (f32[2,16,8]{2,1,0:T(8,128)}, f32[2,16,8]{2,1,0:T(8,128)S(1)}, u32[]{:S(2)}) copy-start(f32[2,16,8]{2,1,0:T(8,128)S(1)} %fusion.132) | copy-start | bytes 3076
  492.4 12.3 %slice-start = ((s8[10616832]{0:T(1024)(128)(4,1)}), s8[4194304]{0:T(1024)(128)(4,1)S(1)}, s32[]{:S(2)}) async-start(s8[10616832]{0:T(1024)(128)(4,1)} %bitcast.506), calls=%async_computation.10 | async-start | bytes 8388608
  492.7 12.0 copy-start.92
  492.7 12.0 copy-start.99
  492.8 12.0 copy-start.149
  492.8 12.0 slice-start.1
  492.8 12.0 slice-start.2
  595.2 11.7 copy-start.12
  687.2 34.6 %copy-start.66 = (f32[32,128,128]{1,2,0:T(8,128)S(1)}, f32[32,128,128]{1,2,0:T(8,128)}, u32[]{:S(2)}) copy-start(f32[32,128,128]{1,2,0:T(8,128)} %get-tuple-element.183) | copy-start | bytes 6291460
  688.2 33.5 %copy-start.40 = (bf16[1,32,128,216]{3,2,1,0:T(8,128)(2,1)S(1)}, bf16[1,32,128,216]{3,2,1,0:T(8,128)(2,1)}, u32[]{:S(2)}) copy-start(bf16[1,32,128,216]{3,2,1,0:T(8,128)(2,1)} %copy_bitcast_fusion.1) | copy-start | bytes 5308420
  688.3 33.5 %copy-start.136 = (f32[32,128]{1,0:T(8,128)S(1)}, f32[32,128]{1,0:T(8,128)}, u32[]{:S(2)}) copy-start(f32[32,128]{1,0:T(8,128)} %get-tuple-element.182) | copy-start | bytes 49156
  729.2 62.0 %all-to-all-start.3 = ((bf16[1,32,128,216]{3,1,0,2:T(8,128)(2,1)}), bf16[1,32,128,216]{3,1,0,2:T(8,128)(2,1)}, u32[]{:S(2)}, u32[]{:S(2)}) async-start(bf16[1,32,128,216]{3,1,0,2:T(8,128)(2,1)} %copy.187), calls=%async_computation.3 | async-start | bytes 4194304 | tf_op jit(solution)/shard_map/all_to_all | solution.py:1018
  734.4 415.9 %all-reduce.8.cloned.1.call-start = ((), (), s32[]{:S(2)}) async-start(), calls=%async_computation.8 | async-start | bytes 4423680 | tf_op jit(solution)/shard_map/psum | solution.py:1251
  1164.2 39.8 %collective-permute-start.2 = (bf16[288,1152]{1,0:T(8,128)(2,1)}, bf16[288,1152]{1,0:T(8,128)(2,1)}, u32[]{:S(2)}, u32[]{:S(2)}) collective-permute-start(bf16[288,1152]{1,0:T(8,128)(2,1)} %reduce-scatter.2.cloned.1.call-done), channel_id=1, source_target_pairs={{0,16},{16,0},{1,17},{17,1},{2,18},{18,2},{3,19},{19,3},{4,20},{20... | collective-permute-start | bytes 1990664 | tf_op jit(solution)/shard_map/ppermute | solution.py:98
  1167.6 16.1 %collective-permute-start = (bf16[122,256]{1,0:T(8,128)(2,1)S(1)}, bf16[122,256]{1,0:T(8,128)(2,1)S(1)}, u32[]{:S(2)}, u32[]{:S(2)}) collective-permute-start(bf16[122,256]{1,0:T(8,128)(2,1)S(1)} %pad_maximum_fusion.7), channel_id=1, source_target_pairs={{0,16},{16,0},{1,17},{17,1},{2,18},{18,2},{3,19},{19,3},{4,20},{20... | collective-permute-start | bytes 187400 | tf_op jit(solution)/shard_map/ppermute | solution.py:98
  1168.6 22.3 %collective-permute-start.3 = (bf16[72,2304]{1,0:T(8,128)(2,1)}, bf16[72,2304]{1,0:T(8,128)(2,1)}, u32[]{:S(2)}, u32[]{:S(2)}) collective-permute-start(bf16[72,2304]{1,0:T(8,128)(2,1)} %fusion.46), channel_id=1, source_target_pairs={{0,16},{16,0},{1,17},{17,1},{2,18},{18,2},{3,19},{19,3},{4,20},{20... | collective-permute-start | bytes 995336 | tf_op jit(solution)/shard_map/ppermute | solution.py:98
  1171.5 30.4 %collective-permute-start.1 = (bf16[256,1152]{1,0:T(8,128)(2,1)S(1)}, bf16[256,1152]{1,0:T(8,128)(2,1)}, u32[]{:S(2)}, u32[]{:S(2)}) collective-permute-start(bf16[256,1152]{1,0:T(8,128)(2,1)S(1)} %convolution_convert_fusion.4), channel_id=1, source_target_pairs={{0,16},{16,0},{1,17},{17,1},{2,18},{18,2},{3,19},{19,3},{4,20},{20... | collective-permute-start | bytes 1769480 | tf_op jit(solution)/shard_map/ppermute | solution.py:98
  (146 other events, 612.4 us)
Sparse Core Ops, SparseCore 0:
  11.7 143.6 all-reduce.5
  308.7 123.0 all-gather.2
  434.1 110.2 all-gather.4
  617.6 149.8 reduce-scatter.1
  771.0 110.2 all-reduce.7
